TPU v7x, 128 devices: a whole 4x4x4 slice. The times are simulated.
128 devices in a mesh: shard: 128 (over z, x, y, core).
Axes of the slice: x: 4, y: 4, z: 4, core: 2. Of those that a mesh axis runs over, the one named last changes fastest.
Arguments:
- embeddings: bfloat16 [2048, 128, 1280], P('shard'), may hold values from -6 to 6
- lengths: int32 [2048], P('shard'), may hold values from 16 to 128
- requests: int32 [128, 128], P('shard'), may hold values from -1 to 15, as said below
- query_local: int32 [128, 128], P('shard'), may hold values from 0 to 15
Outputs:
- local_best: float32 [2048, 128], P('shard')
- cross_best: float32 [2048, 128], P('shard')
Inputs may be any that keep to these rules, and one draw needn't show every extreme that they name: requests[d, o] is -1 where cluster d lists no partner in cluster o, else a protein index within cluster o; requests[d, d] is -1; the number of listed partners differs from cluster to cluster.
All inputs are finite; a program needn't handle non-finite values.
Results may differ from a plain program's by a relative error of at most 0.0003.
Values may be sent and summed in bfloat16 or wider, within the bound.
No kernel may reach another device: no remote copies, remote signals or barrier semaphores. Data moves between devices by JAX's collectives and lax.ppermute only.
A program may use at most 256 MiB of HBM per device.

v0:
```python
import functools

import jax
import jax.numpy as jnp
from jax import lax
from jax.experimental import pallas as pl
from jax.experimental.pallas import tpu as pltpu
from jax.sharding import PartitionSpec as P

lowest = -1e30
N = 128
GR = 8
C1 = 2
K = 64
DEPTH = 16
GROUP = 4
URGENT = 64
TRIES = 6

R_F1ROW, R_F1COL, R_F1COLM, R_F2ROW, R_F2COL, R_SEND, R_SENDM, R_GIN, R_LIN, R_OWN, R_LEFT, R_GOUT = range(12)


def swap_rows(x, s):
    return jnp.where((s & 1) == 0, pltpu.roll(x, N - 1, 0), pltpu.roll(x, 1, 0))


def swap_cols(x, r):
    return jnp.where((r & 1) == 0, pltpu.roll(x, N - 1, 1), pltpu.roll(x, 1, 1))


def skew(x, by, axis, sign):
    for b in range(7):
        shift = (1 << b) if sign > 0 else N - (1 << b)
        x = jnp.where(((by >> b) & 1) == 1, pltpu.roll(x, shift, axis), x)
    return x


def before(x, s):
    total = x
    for b in range(7):
        total = total + jnp.where(s >= (1 << b), pltpu.roll(total, 1 << b, 0), 0)
    return total - x


def route_kernel(c2, me_ref, plan_ref, tab_ref, tmp_ref, first_ref):
    s = lax.broadcasted_iota(jnp.int32, (N, N), 0)
    r = lax.broadcasted_iota(jnp.int32, (N, N), 1)
    req = plan_ref[:, :N]
    q = plan_ref[:, N : 2 * N]
    lens = plan_ref[:, 2 * N :]
    lens_t = lens.T
    live = (req >= 0).astype(jnp.int32)
    req = jnp.maximum(req, 0)
    la = jnp.zeros((N, N), jnp.int32)
    lb = jnp.zeros((N, N), jnp.int32)
    for p in range(16):
        la = jnp.where(q == p, lens[:, p : p + 1], la)
        lb = jnp.where(req == p, lens_t[p : p + 1, :], lb)
    la = la * live
    lb = lb * live
    lb_t = lb.T
    ga = (la + 15) >> 4
    gb = (lb + 15) >> 4
    ga_t = ga.T
    gb_t = gb.T
    anti = live - live.T
    base = 1000 * (gb + gb_t - ga - ga_t) + jnp.where(((s + r) & 1) == 0, 250, -250)
    score = base
    bias_col = jnp.zeros((N, 1), jnp.int32)
    bias_row = jnp.zeros((1, N), jnp.int32)
    for eta in (10, 6, 4):
        gets = score < 0
        net = jnp.where(gets, gb_t, ga) - jnp.where(gets, gb, ga_t)
        bias_row = bias_row + eta * jnp.sum(net, axis=0, keepdims=True)
        bias_col = bias_col - eta * jnp.sum(net, axis=1, keepdims=True)
        score = base + anti * (bias_col - bias_row)
    lister_gets = score < 0
    lin = jnp.where(lister_gets, lb_t, la)
    psend = jnp.where(lister_gets, req.T, q)
    pown = jnp.where(lister_gets, q.T, req)
    m_tot = (lin + 15) >> 4

    diag = s == r
    free1 = jnp.where(diag, 0, C1)
    n = jnp.minimum(m_tot, free1)
    rem = m_tot - n
    w1 = free1 - n
    for k in range(C1):
        w1 = w1 | jnp.where(k < n, ((r << 3) | k) << (2 + 11 * k), 0)
    free2 = jnp.where(diag, 0, c2)
    g_from = m_tot - rem
    n = jnp.minimum(rem, free2)
    rem = rem - n
    w2 = free2 - n
    for k in range(c2):
        w2 = w2 | jnp.where(k < n, ((g_from + k) << 2) << (2 + 14 * k), 0)
    rem_c = swap_cols(rem, r)
    g_from = swap_cols(m_tot, r) - rem_c
    used = C1 - (w1 & 3)
    n = jnp.where(diag, 0, jnp.minimum(rem_c, w1 & 3))
    n = jnp.maximum(jnp.minimum(n, K - before(n, s)), 0)
    w1 = w1 - n
    for k in range(C1):
        code = (1 << 10) | ((r ^ 1) << 3) | (g_from + k - used)
        w1 = w1 | jnp.where((k >= used) & (k < used + n), code << (2 + 11 * k), 0)
    rem = swap_cols(rem_c - n, r)
    rem_s = swap_rows(rem, s)
    g_from = swap_rows(m_tot, s) - rem_s
    used = c2 - (w2 & 3)
    n = jnp.where(diag, 0, jnp.minimum(rem_s, w2 & 3))
    w2 = w2 - n
    for k in range(c2):
        code = 1 | ((g_from + k - used) << 2)
        w2 = w2 | jnp.where((k >= used) & (k < used + n), code << (2 + 14 * k), 0)
    rem = swap_rows(rem_s - n, s)

    w1 = skew(w1, s, 1, -1)
    w2 = skew(w2, r, 0, -1)

    def step(least, urgent, w1, w2, rem):
        f1 = w1 & 3
        f2 = w2 & 3
        ok = (jnp.minimum(jnp.minimum(f1, f2), rem) > 0) & (rem + urgent >= least)
        g = m_tot - rem
        code1 = (r << 3) | g
        code2 = 2 | (g << 2) | ((C1 - f1) << 5) | (s << 6)
        new1 = (w1 - 1) | (code1 << jnp.where(f1 == C1, 2, 13))
        new2 = (w2 - 1) | (code2 << jnp.where(f2 == c2, 2, 16))
        w1 = jnp.where(ok, new1, w1)
        w2 = jnp.where(ok, new2, w2)
        rem = jnp.where(ok, rem - 1, rem)
        return pltpu.roll(w1, N - 1, 1), pltpu.roll(w2, N - 1, 0), rem

    first_ref[0] = w1
    first_ref[1] = w2
    first_ref[2] = rem

    def attempt(c):
        tries, _, _, _, _, urgent = c
        w1, w2, rem = first_ref[0], first_ref[1], first_ref[2]
        turns = jnp.int32(0)
        left = jnp.int32(0)
        for least in (URGENT, 4, 2, 1):

            def open_count(rem):
                return jnp.sum(((rem > 0) & (rem + urgent >= least)).astype(jnp.int32))

            def body(c):
                i, _, w1, w2, rem = c
                for _ in range(8):
                    w1, w2, rem = step(least, urgent, w1, w2, rem)
                return i + 1, open_count(rem), w1, w2, rem

            i, left, w1, w2, rem = lax.while_loop(
                lambda c: (c[0] < N // 8) & (c[1] > 0),
                body,
                (jnp.int32(0), open_count(rem), w1, w2, rem),
            )
            turns = turns + 8 * i
        return tries + 1, left, turns, w1, w2, jnp.where(rem > 0, URGENT, urgent)

    _, left, turns, w1, w2, _ = lax.while_loop(
        lambda c: (c[0] < TRIES) & (c[1] > 0),
        attempt,
        (jnp.int32(0), jnp.int32(1), jnp.int32(0), w1, w2, jnp.zeros((N, N), jnp.int32)),
    )
    turns = turns & (N - 1)
    w1 = skew(pltpu.roll(w1, turns, 1), s, 1, 1)
    w2 = skew(pltpu.roll(w2, turns, 0), r, 0, 1)

    me = me_ref[0]
    mate = me ^ 1

    def put(x, *rows):
        tmp_ref[...] = x
        for row, at in rows:
            tab_ref[row : row + 1, :] = tmp_ref[pl.ds(at, 1), :]

    put(w1, (R_F1ROW, me))
    put(w1.T, (R_F1COL, me), (R_F1COLM, mate))
    put(w2, (R_F2ROW, me))
    put(w2.T, (R_F2COL, me))
    put(psend, (R_SEND, me), (R_SENDM, mate))
    put(m_tot.T, (R_GIN, me))
    put(lin.T, (R_LIN, me))
    put(pown.T, (R_OWN, me))
    tab_ref[R_LEFT : R_LEFT + 1, :] = jnp.full((1, N), left, jnp.int32)
    put(m_tot, (R_GOUT, me))
    tab_ref[R_GOUT + 1 :, :] = jnp.zeros((16 - R_GOUT - 1, N), jnp.int32)


def route(c2, me, plan):
    return pl.pallas_call(
        functools.partial(route_kernel, c2),
        out_shape=jax.ShapeDtypeStruct((16, N), jnp.int32),
        in_specs=[pl.BlockSpec(memory_space=pltpu.SMEM), pl.BlockSpec(memory_space=pltpu.VMEM)],
        out_specs=pl.BlockSpec(memory_space=pltpu.VMEM),
        scratch_shapes=[pltpu.VMEM((N, N), jnp.int32), pltpu.VMEM((3, N, N), jnp.int32)],
        compiler_params=pltpu.CompilerParams(vmem_limit_bytes=32 << 20),
        name=f"route{c2}",
    )(me, plan)


def pack1_kernel(tab_ref, own_ref, out_ref, buf, sem):
    parts = sem.shape[0]
    each = N // parts

    def piece(ref, part):
        return ref.at[pl.ds(part * each * C1, each * C1)]

    for part in range(parts):

        def body(j, _):
            w = tab_ref[R_F1ROW, j]
            for k in range(C1):
                code = w >> (2 + 11 * k)
                buf[j * C1 + k] = own_ref[tab_ref[R_SEND, (code >> 3) & (N - 1)] * GR + (code & 7)]
            return 0

        lax.fori_loop(part * each, (part + 1) * each, body, 0, unroll=4)
        pltpu.make_async_copy(piece(buf, part), piece(out_ref, part), sem.at[part]).start()
    for part in range(parts):
        pltpu.make_async_copy(piece(buf, part), piece(out_ref, part), sem.at[part]).wait()


def pack1(tab, own):
    parts = 8
    shape = (N * C1,) + own.shape[1:]
    return pl.pallas_call(
        pack1_kernel,
        out_shape=jax.ShapeDtypeStruct(shape, own.dtype),
        in_specs=[pl.BlockSpec(memory_space=pltpu.SMEM), pl.BlockSpec(memory_space=pltpu.VMEM)],
        out_specs=pl.BlockSpec(memory_space=pltpu.HBM),
        scratch_shapes=[pltpu.VMEM(shape, own.dtype), pltpu.SemaphoreType.DMA((parts,))],
        compiler_params=pltpu.CompilerParams(vmem_limit_bytes=40 << 20),
        name="pack1",
    )(tab, own)


def pack2_kernel(c2, tab_ref, own_ref, mate_ref, got_ref, out_ref, buf, in_sem, out_sem):
    parts = in_sem.shape[0]
    each = N // parts

    def fetch(part):
        def body(j, _):
            to = part * each + j
            w = tab_ref[R_F2ROW, to]
            for k in range(c2):
                code = w >> (2 + 14 * k)
                kind = code & 3
                g = (code >> 2) & 7
                slot = ((code >> 6) & (N - 1)) * C1 + ((code >> 5) & 1)
                dst = buf.at[to * c2 + k]

                @pl.when(kind == 0)
                def _():
                    src = own_ref.at[tab_ref[R_SEND, to] * GR + g]
                    pltpu.make_async_copy(src, dst, in_sem.at[part]).start()

                @pl.when(kind == 1)
                def _():
                    src = mate_ref.at[tab_ref[R_SENDM, to] * GR + g]
                    pltpu.make_async_copy(src, dst, in_sem.at[part]).start()

                @pl.when(kind >= 2)
                def _():
                    pltpu.make_async_copy(got_ref.at[slot], dst, in_sem.at[part]).start()

            return 0

        lax.fori_loop(0, each, body, 0, unroll=4)

    def piece(ref, part):
        return ref.at[pl.ds(part * each * c2, each * c2)]

    for part in range(parts):
        fetch(part)
    for part in range(parts):
        pltpu.make_async_copy(piece(buf, part), piece(buf, part), in_sem.at[part]).wait()
        pltpu.make_async_copy(piece(buf, part), piece(out_ref, part), out_sem.at[part]).start()
    for part in range(parts):
        pltpu.make_async_copy(piece(buf, part), piece(out_ref, part), out_sem.at[part]).wait()


def pack2(c2, tab, own, mate, got):
    parts = 4
    shape = (N * c2,) + own.shape[1:]
    return pl.pallas_call(
        functools.partial(pack2_kernel, c2),
        out_shape=jax.ShapeDtypeStruct(shape, own.dtype),
        in_specs=[pl.BlockSpec(memory_space=pltpu.SMEM)] + [pl.BlockSpec(memory_space=pltpu.HBM)] * 3,
        out_specs=pl.BlockSpec(memory_space=pltpu.HBM),
        scratch_shapes=[
            pltpu.VMEM(shape, own.dtype),
            pltpu.SemaphoreType.DMA((parts,)),
            pltpu.SemaphoreType.DMA((parts,)),
        ],
        compiler_params=pltpu.CompilerParams(vmem_limit_bytes=40 << 20),
        name="pack2",
    )(tab, own, mate, got)


def hand_kernel(tab_ref, got_ref, out_ref, sem):
    def body(s, count):
        w = tab_ref[R_F1COL, s]
        for k in range(C1):
            mine = (w >> (2 + 11 * k + 10)) & 1

            @pl.when(mine == 1)
            def _():
                pltpu.make_async_copy(got_ref.at[s * C1 + k], out_ref.at[count], sem).start()

            count = count + mine
        return count

    count = lax.fori_loop(0, N, body, jnp.int32(0))

    def fill(j, _):
        pltpu.make_async_copy(got_ref.at[0], out_ref.at[j], sem).start()
        return 0

    lax.fori_loop(count, K, fill, 0)
    pltpu.make_async_copy(out_ref, out_ref, sem).wait()


def hand(tab, got):
    return pl.pallas_call(
        hand_kernel,
        out_shape=jax.ShapeDtypeStruct((K,) + got.shape[1:], got.dtype),
        in_specs=[pl.BlockSpec(memory_space=pltpu.SMEM), pl.BlockSpec(memory_space=pltpu.HBM)],
        out_specs=pl.BlockSpec(memory_space=pltpu.VMEM),
        scratch_shapes=[pltpu.SemaphoreType.DMA],
        compiler_params=pltpu.CompilerParams(vmem_limit_bytes=40 << 20),
        name="hand",
    )(tab, got)


def pack_whole_kernel(tab_ref, own_ref, out_ref):
    out_ref[...] = own_ref[...]


def pack_whole(tab, own):
    block = (GR,) + own.shape[1:]
    return pl.pallas_call(
        pack_whole_kernel,
        grid_spec=pltpu.PrefetchScalarGridSpec(
            num_scalar_prefetch=1,
            grid=(N,),
            in_specs=[pl.BlockSpec(block, lambda i, tab: (tab[R_SEND, i], 0, 0))],
            out_specs=pl.BlockSpec(block, lambda i, tab: (i, 0, 0)),
        ),
        out_shape=jax.ShapeDtypeStruct((N * GR,) + own.shape[1:], own.dtype),
        name="pack_whole",
    )(tab, own)


def place_kernel(c2, me_ref, tab_ref, loc_ref):
    me = me_ref[0]

    def body(s, c):
        count, handed = c
        if c2 == 0:
            for g in range(GR):
                loc_ref[s * GR + g] = s * GR + g
        else:
            w = tab_ref[R_F1COL, s]
            filled = C1 - (w & 3)
            for k in range(C1):
                code = w >> (2 + 11 * k)

                @pl.when((k < filled) & (((code >> 3) & 0xFF) == me) & (s != me))
                def _():
                    loc_ref[s * GR + (code & 7)] = s * C1 + k

            w = tab_ref[R_F1COLM, s]
            for k in range(C1):
                code = w >> (2 + 11 * k)
                handed_here = (code >> 10) & 1

                @pl.when(handed_here == 1)
                def _():
                    loc_ref[s * GR + (code & 7)] = (C1 + c2) * N + handed

                handed = handed + handed_here

            w = tab_ref[R_F2COL, s]
            filled = c2 - (w & 3)
            for k in range(c2):
                code = w >> (2 + 14 * k)
                kind = code & 3
                origin = jnp.where(kind >= 2, (code >> 6) & (N - 1), s ^ (kind & 1))

                @pl.when((k < filled) & (s != me))
                def _():
                    loc_ref[origin * GR + ((code >> 2) & 7)] = C1 * N + s * c2 + k

        is_live = tab_ref[R_GIN, s] > 0

        is_late = is_live & (tab_ref[R_GIN, s] > C1)
        early, late = count

        @pl.when(is_live)
        def _():
            loc_ref[N * GR + jnp.where(is_late, N - 1 - late, early)] = s

        late = late + is_late.astype(jnp.int32)
        return (early + (is_live.astype(jnp.int32) - is_late.astype(jnp.int32)), late), handed

    zero = jnp.int32(0)
    (early, late), _ = lax.fori_loop(0, N, body, ((zero, zero), zero))
    loc_ref[N * GR + N] = early
    loc_ref[N * GR + N + 1] = late


def place(c2, me, tab):
    return pl.pallas_call(
        functools.partial(place_kernel, c2),
        out_shape=jax.ShapeDtypeStruct((N * GR + N + 128,), jnp.int32),
        in_specs=[pl.BlockSpec(memory_space=pltpu.SMEM)] * 2,
        out_specs=pl.BlockSpec(memory_space=pltpu.SMEM),
        name="place",
    )(me, tab)


def match_kernel(late, ends, tab_ref, loc_ref, lens_ref, own_ref, best0_ref, ret0_ref, *refs):
    gots, (best_ref, ret_ref, buf, sem) = refs[: len(ends)], refs[len(ends) :]
    scale = 1.0 / jnp.sqrt(jnp.float32(own_ref.shape[2]))
    best_ref[...] = best0_ref[...]
    ret_ref[...] = ret0_ref[...]
    count = loc_ref[N * GR + N + int(late)]

    def sender(i):
        return loc_ref[N * GR + (N - 1 - i if late else i)]

    def fetch(i):
        @pl.when(i < count)
        def _():
            s = sender(i)
            slot = i & (DEPTH - 1)
            granules = tab_ref[R_GIN, s]
            for g in range(GR if late else min(GR, C1)):

                @pl.when(g < granules)
                def _():
                    at = loc_ref[s * GR + g]
                    start = 0
                    for got_ref, end in zip(gots, ends):

                        @pl.when((at >= start) & (at < end))
                        def _(got_ref=got_ref, start=start):
                            pltpu.make_async_copy(
                                got_ref.at[at - start], buf.at[slot, g], sem.at[slot, g]
                            ).start()

                        start = end

    def arrive(i):
        @pl.when(i < count)
        def _():
            s = sender(i)
            slot = i & (DEPTH - 1)
            granules = tab_ref[R_GIN, s]
            for g in range(GR if late else min(GR, C1)):

                @pl.when(g < granules)
                def _():
                    pltpu.make_async_copy(gots[0].at[0], buf.at[slot, g], sem.at[slot, g]).wait()

    for i in range(DEPTH - GROUP):
        fetch(i)
    row = lax.broadcasted_iota(jnp.int32, (N, N), 0)
    col = lax.broadcasted_iota(jnp.int32, (N, N), 1)

    def score_of(i):
        s = sender(i)
        p = tab_ref[R_OWN, s]
        incoming = buf[i & (DEPTH - 1)].reshape(N, own_ref.shape[2])
        score = lax.dot_general(
            own_ref[p], incoming, (((1,), (1,)), ((), ())), preferred_element_type=jnp.float32
        )
        return s, p, score * scale

    def best_of(s, p, score):
        len_in = tab_ref[R_LIN, s]
        len_own = lens_ref[p]
        real_in = col < len_in
        real_own = row < len_own
        over_in = jnp.sum(jnp.where(real_in, score, 0.0), 1, keepdims=True) / len_in.astype(jnp.float32)
        own_count = len_own.astype(jnp.float32)
        over_own = jnp.sum(jnp.where(real_own, score, 0.0), 0, keepdims=True) / own_count
        grand = jnp.sum(jnp.where(real_own[:, :1], over_in, 0.0), 0, keepdims=True) / own_count
        own_best = (
            jnp.max(jnp.where(real_in, score - over_own, lowest), 1, keepdims=True) - over_in + grand
        )
        in_best = (
            jnp.max(jnp.where(real_own, score - over_in, lowest), 0, keepdims=True) - over_own + grand
        )
        return own_best, in_best

    def body(j, _):
        first = j * GROUP
        for u in range(GROUP):
            fetch(first + u + DEPTH - GROUP)
        for u in range(GROUP):
            arrive(first + u)
        scores = [score_of(jnp.minimum(first + u, count - 1)) for u in range(GROUP)]
        found = [best_of(*x) for x in scores]
        best = best_ref[...]
        for (s, p, _), (own_best, in_best) in zip(scores, found):
            best = jnp.where(col == p, jnp.maximum(best, own_best), best)
            ret_ref[pl.ds(s, 1), :] = in_best
        best_ref[...] = best
        return 0

    lax.fori_loop(0, (count + GROUP - 1) // GROUP, body, 0)


def match(late, tab, loc, lens, own, best, ret, *gots):
    ends = []
    for got in gots:
        ends.append((ends[-1] if ends else 0) + got.shape[0])
    return pl.pallas_call(
        functools.partial(match_kernel, late, tuple(ends)),
        out_shape=[jax.ShapeDtypeStruct((N, N), jnp.float32)] * 2,
        in_specs=[pl.BlockSpec(memory_space=pltpu.SMEM)] * 3
        + [pl.BlockSpec(memory_space=pltpu.VMEM)] * 3
        + [pl.BlockSpec(memory_space=pltpu.HBM)] * len(gots),
        out_specs=[pl.BlockSpec(memory_space=pltpu.VMEM)] * 2,
        scratch_shapes=[
            pltpu.VMEM((DEPTH, GR, 16, own.shape[2]), own.dtype),
            pltpu.SemaphoreType.DMA((DEPTH, GR)),
        ],
        compiler_params=pltpu.CompilerParams(vmem_limit_bytes=40 << 20),
        name="match_late" if late else "match_early",
    )(tab, loc, lens, own, best, ret, *gots)


def centred(score_matrix, row_validity_mask, col_mask):
    row_count = jnp.sum(row_validity_mask, -1)
    col_count = jnp.sum(col_mask, -1)
    row_mean = jnp.sum(score_matrix * col_mask[..., None, :], -1) / col_count[..., None]
    col_mean = jnp.sum(score_matrix * row_validity_mask[..., :, None], -2) / row_count[..., None]
    grand_mean = jnp.sum(row_mean * row_validity_mask, -1) / row_count
    return (
        score_matrix - row_mean[..., :, None] - col_mean[..., None, :] + grand_mean[..., None, None]
    )


def within_cluster(embeddings, masks):
    proteins_here, slots, width = embeddings.shape
    inverse_square_root = 1.0 / jnp.sqrt(jnp.float32(width))
    block_size = 8
    block_count = proteins_here // block_size

    def one_block(block_start):
        block_rows = lax.dynamic_slice_in_dim(embeddings, block_start, block_size, 0)
        block_mask = lax.dynamic_slice_in_dim(masks, block_start, block_size, 0)
        score_matrix = (
            jnp.einsum("bie,qje->bqij", block_rows, embeddings, preferred_element_type=jnp.float32)
            * inverse_square_root
        )
        cent = centred(score_matrix, block_mask[:, None, :], masks[None, :, :])
        row_max = jnp.max(jnp.where(masks[None, :, None, :] > 0, cent, lowest), -1)
        self_pair = (block_start + jnp.arange(block_size))[:, None] == jnp.arange(proteins_here)[
            None, :
        ]
        row_max = jnp.where(self_pair[:, :, None], lowest, row_max)
        best_match = jnp.max(row_max, 1)
        return jnp.where(block_mask > 0, best_match, 0.0)

    start_offsets = jnp.arange(block_count) * block_size
    return lax.map(one_block, start_offsets).reshape(proteins_here, slots)


def exchange(x):
    return lax.all_to_all(x, "shard", split_axis=0, concat_axis=0, tiled=True)


def other_core(x):
    return lax.ppermute(x, "shard", [(d, d ^ 1) for d in range(N)])


def per_device(embeddings, lengths, requests, query_local):
    proteins_here, slots, width = embeddings.shape
    masks = (jnp.arange(slots)[None, :] < lengths[:, None]).astype(jnp.float32)
    me = lax.axis_index("shard").astype(jnp.int32)[None]
    plan = jnp.concatenate([requests, query_local, lengths[None, :]], 1)
    plan = jnp.pad(plan, ((0, 0), (0, 3 * N - plan.shape[1])))
    plan = exchange(jnp.broadcast_to(plan, (N, 3 * N)))
    own = embeddings.reshape(proteins_here * GR, 16, width)

    nothing = jnp.full((N, N), lowest, jnp.float32)

    def finish(tab, best, ret, local_best):
        returned = exchange(ret)
        mine = (tab[R_SEND][None, :] == jnp.arange(proteins_here)[:, None]) & (tab[R_GOUT] > 0)[None, :]
        from_ret = jnp.max(jnp.where(mine[:, :, None], returned[None, :, :], lowest), 1)
        best = jnp.maximum(from_ret, best[:, :proteins_here].T)
        cross_best = jnp.where((masks > 0) & (best > -1e29), best, 0.0)
        return local_best, cross_best

    def packed(c2, tab):
        loc = place(c2, me, tab)
        got1 = exchange(pack1(tab, own))
        local_best = within_cluster(embeddings, masks)
        rows, local_best = lax.optimization_barrier((own, local_best))
        mate = other_core(rows)
        got1, local_best, mate = lax.optimization_barrier((got1, local_best, mate))
        send2 = pack2(c2, tab, own, mate, got1)
        send2, got1 = lax.optimization_barrier((send2, got1))
        got2 = exchange(send2)
        handed = other_core(hand(tab, got1))
        best, ret = match(False, tab, loc, lengths, embeddings, nothing, nothing, got1)
        best, ret, got2 = lax.optimization_barrier((best, ret, got2))
        best, ret = match(True, tab, loc, lengths, embeddings, best, ret, got1, got2, handed)
        return finish(tab, best, ret, local_best)

    def whole(tab):
        loc = place(0, me, tab)
        got = exchange(pack_whole(tab, own))
        local_best = within_cluster(embeddings, masks)
        best, ret = match(False, tab, loc, lengths, embeddings, nothing, nothing, got)
        best, ret = match(True, tab, loc, lengths, embeddings, best, ret, got)
        return finish(tab, best, ret, local_best)

    def second(_):
        tab = route(2, me, plan)
        return lax.cond(tab[R_LEFT, 0] == 0, functools.partial(packed, 2), whole, tab)

    tab = route(1, me, plan)
    return lax.cond(tab[R_LEFT, 0] == 0, functools.partial(packed, 1), second, tab)


def solution(mesh):
    placed = (P("shard", None, None), P("shard"), P("shard", None), P("shard", None))
    return jax.shard_map(
        per_device,
        mesh=mesh,
        in_specs=placed,
        out_specs=(P("shard", None), P("shard", None)),
        check_vma=False,
    )
```

profile of v0, /device:TPU:1, one launch (start us, length us, event | category | flops | bytes accessed | tf_op | source)
XLA Modules:
  0.0 303.8 jit_solution(6463469246121008858)
XLA Ops:
  2.1 11.5 %all-to-all-start.8 = ((s32[128,1,384]{2,1,0:T(1,128)}), s32[128,1,384]{2,1,0:T(1,128)S(1)}, u32[]{:S(2)}, u32[]{:S(2)}) async-start(s32[128,1,384]{2,1,0:T(1,128)} %broadcast_in_dim.222), calls=%async_computation.8 | async-start | bytes 393216 | tf_op jit(solution)/shard_map/all_to_all | solution.py:576
  14.3 9.9 %all-to-all-done.8 = s32[128,1,384]{2,1,0:T(1,128)S(1)} async-done(((s32[128,1,384]{2,1,0:T(1,128)}), s32[128,1,384]{2,1,0:T(1,128)S(1)}, u32[]{:S(2)}, u32[]{:S(2)}) %all-to-all-start.8) | async-done | bytes 196640 | tf_op jit(solution)/shard_map/all_to_all | solution.py:576
  24.2 20.7 %route1.1 = s32[16,128]{1,0:T(8,128)S(1)} custom-call(s32[1]{0:T(128)} %bitcast.43.me_ref, s32[128,384]{1,0:T(8,128)S(1)} %bitcast.174), custom_call_target="tpu_custom_call" | custom-call | tf_op jit(solution)/shard_map/route1/pallas_call | solution.py:193
  46.0 257.7 %conditional.2 = (f32[16,128]{1,0:T(8,128)}, f32[16,128]{1,0:T(8,128)}) conditional(s32[]{:T(128)} %bitcast.45, (s32[1]{0:T(128)}, s32[128,384]{1,0:T(8,128)S(1)}, f32[16,128]{0,1:T(8,128)S(1)}, bf16[16,128,1280]{2,1,0:T(8,128)(2,1)}, bf16[128,16,1280]{2,1,0:T(8,128)(2,1)}, /*index=5*/s32[16]{0:T(128)}) %tuple.150, (s32[16,128]{1,0:T(8,128)S(1)}, ...), branch_computations={%region_0.23_spmd, %region_23.34_spmd} | conditional | flops 5390275584 | bytes 209450736 | solution.py:631
  46.9 4.6 %pack1.3 = bf16[256,16,1280]{2,1,0:T(8,128)(2,1)S(1)} custom-call(s32[16,128]{1,0:T(8,128)} %copy-done.14, bf16[128,16,1280]{2,1,0:T(8,128)(2,1)} %bitcast.171), custom_call_target="tpu_custom_call" | custom-call | tf_op jit(solution)/shard_map/cond/branch_1_fun/pack1/pallas_call | solution.py:229
  51.5 3.8 %copy-done.1 = bf16[256,16,1280]{2,1,0:T(8,128)(2,1)} copy-done((bf16[256,16,1280]{2,1,0:T(8,128)(2,1)}, bf16[256,16,1280]{2,1,0:T(8,128)(2,1)S(1)}, u32[]{:S(2)}) %copy-start.1) | copy-done | bytes 10485784 | tf_op jit(solution)/shard_map/cond
  55.3 5.2 %all-to-all-start = ((bf16[256,16,1280]{2,1,0:T(8,128)(2,1)}), bf16[256,16,1280]{2,1,0:T(8,128)(2,1)}, u32[]{:S(2)}, u32[]{:S(2)}) async-start(bf16[256,16,1280]{2,1,0:T(8,128)(2,1)} %copy-done.1), calls=%async_computation | async-start | bytes 20971520 | tf_op jit(solution)/shard_map/cond/branch_1_fun/all_to_all | solution.py:576
  60.7 33.3 %while.32 = (s32[]{:T(128)}, f32[2,8,128]{2,1,0:T(8,128)S(1)}, s32[2]{0:T(128)S(1)}, f32[16,128]{1,0:T(8,128)S(1)}, bf16[16,128,1280]{2,1,0:T(8,128)(2,1)}, /*in...) while((s32[]{:T(128)}, f32[2,8,128]{2,1,0:T(8,128)S(1)}, s32[2]{0:T(128)S(1)}, ...), condition=%wide.region_32.32_spmd, body=%wide.region_25.31_spmd.sunk | while | flops 5389736960 | bytes 25377404 | solution.py:572
  63.3 10.0 %multiply_reduce_fusion.15 = (f32[8,16,128]{2,1,0:T(8,128)S(1)}, f32[8,128,16]{1,2,0:T(8,128)S(1)}, f32[8,128,16,128]{1,3,2,0:T(8,128)S(1)}) fusion(f32[8,128]{1,0:T(8,128)S(1)} %broadcast_multiply_fusion.12, f32[16,128]{1,0:T(8,128)S(1)} %broadcast_multiply_fusion.13, bf16[16,128,1280]{2,1,0:T(8,128)(2,1)} %get-tuple-element.572, s32[]{:T(128)S(6)} %select_n.110), kind=kOutput, calls=%fused_computation.69.clone.1 | convolution fusion | flops 5377064960 | bytes 16396292 | tf_op jit(solution)/shard_map/cond/branch_1_fun/while/body/eval_jaxpr/bie,qje->bqij/dot_general | solution.py:559
  73.5 3.4 %fusion.41 = f32[8,16,128]{2,1,0:T(8,128)S(1)} fusion(f32[8,128,16,128]{1,3,2,0:T(8,128)S(1)} %get-tuple-element.515, f32[8,16]{1,0:T(8,128)S(1)} %broadcast_divide_fusion.9, f32[8,16,128]{2,1,0:T(8,128)S(1)} %get-tuple-element.520, f32[8,16,128]{2,1,0:T(8,128)S(1)} %get-tuple-element.521, pred[16,128]{1,0:T(8,128)(4,1)S(1)} %broadcast_compare_fusion.6), kind=kLoop, calls=%fused_computation.68.clone.1 | loop fusion | flops 12566528 | bytes 8587776 | tf_op jit(solution)/shard_map/cond/branch_1_fun/while/body/eval_jaxpr/reduce_max | solution.py:563
  80.3 9.3 %multiply_reduce_fusion.15 = (f32[8,16,128]{2,1,0:T(8,128)S(1)}, f32[8,128,16]{1,2,0:T(8,128)S(1)}, f32[8,128,16,128]{1,3,2,0:T(8,128)S(1)}) fusion(f32[8,128]{1,0:T(8,128)S(1)} %broadcast_multiply_fusion.12, f32[16,128]{1,0:T(8,128)S(1)} %broadcast_multiply_fusion.13, bf16[16,128,1280]{2,1,0:T(8,128)(2,1)} %get-tuple-element.572, s32[]{:T(128)S(6)} %select_n.110), kind=kOutput, calls=%fused_computation.69.clone.1 | convolution fusion | flops 5377064960 | bytes 16396292 | tf_op jit(solution)/shard_map/cond/branch_1_fun/while/body/eval_jaxpr/bie,qje->bqij/dot_general | solution.py:559
  89.8 3.4 %fusion.41 = f32[8,16,128]{2,1,0:T(8,128)S(1)} fusion(f32[8,128,16,128]{1,3,2,0:T(8,128)S(1)} %get-tuple-element.515, f32[8,16]{1,0:T(8,128)S(1)} %broadcast_divide_fusion.9, f32[8,16,128]{2,1,0:T(8,128)S(1)} %get-tuple-element.520, f32[8,16,128]{2,1,0:T(8,128)S(1)} %get-tuple-element.521, pred[16,128]{1,0:T(8,128)(4,1)S(1)} %broadcast_compare_fusion.6), kind=kLoop, calls=%fused_computation.68.clone.1 | loop fusion | flops 12566528 | bytes 8587776 | tf_op jit(solution)/shard_map/cond/branch_1_fun/while/body/eval_jaxpr/reduce_max | solution.py:563
  95.4 8.5 %collective-permute-done.mate_ref = bf16[128,16,1280]{2,1,0:T(8,128)(2,1)S(1)} collective-permute-done((bf16[128,16,1280]{2,1,0:T(8,128)(2,1)}, bf16[128,16,1280]{2,1,0:T(8,128)(2,1)S(1)}, u32[]{:S(2)}, u32[]{:S(2)}) %collective-permute-start) | collective-permute-done | bytes 5242912 | tf_op jit(solution)/shard_map/cond/branch_1_fun/ppermute | solution.py:580
  106.2 78.8 %all-to-all-done.got_ref.refs_0_ = bf16[256,16,1280]{2,1,0:T(8,128)(2,1)} async-done(((bf16[256,16,1280]{2,1,0:T(8,128)(2,1)}), bf16[256,16,1280]{2,1,0:T(8,128)(2,1)}, u32[]{:S(2)}, u32[]{:S(2)}) %all-to-all-start) | async-done | bytes 10485792 | tf_op jit(solution)/shard_map/cond/branch_1_fun/all_to_all | solution.py:576
  185.0 2.5 copy-done.6
  187.4 5.1 %pack2.3 = bf16[128,16,1280]{2,1,0:T(8,128)(2,1)S(1)} custom-call(s32[16,128]{1,0:T(8,128)S(1)} %copy-done.15, bf16[128,16,1280]{2,1,0:T(8,128)(2,1)} %bitcast.173, bf16[128,16,1280]{2,1,0:T(8,128)(2,1)S(1)} %copy-done.6, bf16[256,16,1280]{2,1,0:T(8,128)(2,1)} %all-to-all-done.got_ref.refs_0_), custom_call_target="tpu_custom_call" | custom-call | tf_op jit(solution)/shard_map/cond/branch_1_fun/pack2/pallas_call | solution.py:288
  194.8 9.0 %all-to-all-start.1 = ((bf16[128,16,1280]{2,1,0:T(8,128)(2,1)}), bf16[128,16,1280]{2,1,0:T(8,128)(2,1)}, u32[]{:S(2)}, u32[]{:S(2)}) async-start(bf16[128,16,1280]{2,1,0:T(8,128)(2,1)} %copy-done.2), calls=%async_computation.1 | async-start | bytes 10485760 | tf_op jit(solution)/shard_map/cond/branch_1_fun/all_to_all | solution.py:576
  203.8 8.2 %hand.3 = bf16[64,16,1280]{2,1,0:T(8,128)(2,1)} custom-call(s32[16,128]{1,0:T(8,128)S(1)} %copy-done.15, bf16[256,16,1280]{2,1,0:T(8,128)(2,1)} %all-to-all-done.got_ref.refs_0_), custom_call_target="tpu_custom_call" | custom-call | tf_op jit(solution)/shard_map/cond/branch_1_fun/hand/pallas_call | solution.py:327
  212.3 5.7 %place.5.loc_ref = s32[1280]{0:T(1024)} custom-call(s32[1]{0:T(128)} %get-tuple-element.247.me_ref, s32[16,128]{1,0:T(8,128)S(1)} %copy-done.15), custom_call_target="tpu_custom_call" | custom-call | tf_op jit(solution)/shard_map/cond/branch_1_fun/place/pallas_call | solution.py:416
  218.8 9.0 %match_early.5 = (f32[128,128]{1,0:T(8,128)S(1)}, f32[128,128]{1,0:T(8,128)S(1)}) custom-call(s32[16,128]{1,0:T(8,128)S(1)} %copy-done.15, s32[1280]{0:T(1024)S(1)} %copy-done.9, s32[16]{0:T(128)S(1)} %copy-done.18, bf16[16,128,1280]{2,1,0:T(8,128)(2,1)} %get-tuple-element.651, f32[128,128]{1,0:T(8,128)S(1)} %broadcast_in_dim.213.best0_ref.ret0_ref, ...), custom_call_target="tpu_custom_call" | custom-call | tf_op jit(solution)/shard_map/cond/branch_1_fun/match_early/pallas_call | solution.py:522
  227.8 40.1 %all-to-all-done.1.refs_1_ = bf16[128,16,1280]{2,1,0:T(8,128)(2,1)} async-done(((bf16[128,16,1280]{2,1,0:T(8,128)(2,1)}), bf16[128,16,1280]{2,1,0:T(8,128)(2,1)}, u32[]{:S(2)}, u32[]{:S(2)}) %all-to-all-start.1) | async-done | bytes 5242912 | tf_op jit(solution)/shard_map/cond/branch_1_fun/all_to_all | solution.py:576
  267.9 15.6 %match_late.5 = (f32[128,128]{1,0:T(8,128)S(1)}, f32[128,128]{1,0:T(8,128)}) custom-call(s32[16,128]{1,0:T(8,128)S(1)} %copy-done.15, s32[1280]{0:T(1024)S(1)} %copy-done.10, s32[16]{0:T(128)S(1)} %copy-done.18, bf16[16,128,1280]{2,1,0:T(8,128)(2,1)} %get-tuple-element.651, f32[128,128]{1,0:T(8,128)S(1)} %get-tuple-element.255.best0_ref, ...), custom_call_target="tpu_custom_call" | custom-call | tf_op jit(solution)/shard_map/cond/branch_1_fun/match_late/pallas_call | solution.py:522
  283.5 9.5 %all-to-all-start.2 = ((f32[128,1,128]{2,1,0:T(1,128)}), f32[128,1,128]{2,1,0:T(1,128)S(1)}, u32[]{:S(2)}, u32[]{:S(2)}) async-start(f32[128,1,128]{2,1,0:T(1,128)} %bitcast.40), calls=%async_computation.2 | async-start | bytes 131072 | tf_op jit(solution)/shard_map/cond/branch_1_fun/all_to_all | solution.py:576
  293.0 9.6 %all-to-all-done.2 = f32[128,1,128]{2,1,0:T(1,128)S(1)} async-done(((f32[128,1,128]{2,1,0:T(1,128)}), f32[128,1,128]{2,1,0:T(1,128)S(1)}, u32[]{:S(2)}, u32[]{:S(2)}) %all-to-all-start.2) | async-done | bytes 65568 | tf_op jit(solution)/shard_map/cond/branch_1_fun/all_to_all | solution.py:576
  (61 shorter events, 15.1 us)
Async XLA Ops:
  2.1 22.0 %all-to-all-start.8 = ((s32[128,1,384]{2,1,0:T(1,128)}), s32[128,1,384]{2,1,0:T(1,128)S(1)}, u32[]{:S(2)}, u32[]{:S(2)}) async-start(s32[128,1,384]{2,1,0:T(1,128)} %broadcast_in_dim.222), calls=%async_computation.8 | async-start | bytes 393216 | tf_op jit(solution)/shard_map/all_to_all | solution.py:576
  46.3 0.6 copy-start.14
  51.5 3.8 %copy-start.1 = (bf16[256,16,1280]{2,1,0:T(8,128)(2,1)}, bf16[256,16,1280]{2,1,0:T(8,128)(2,1)S(1)}, u32[]{:S(2)}) copy-start(bf16[256,16,1280]{2,1,0:T(8,128)(2,1)S(1)} %pack1.3) | copy-start | bytes 31457284 | tf_op jit(solution)/shard_map/cond
  55.3 129.6 %all-to-all-start = ((bf16[256,16,1280]{2,1,0:T(8,128)(2,1)}), bf16[256,16,1280]{2,1,0:T(8,128)(2,1)}, u32[]{:S(2)}, u32[]{:S(2)}) async-start(bf16[256,16,1280]{2,1,0:T(8,128)(2,1)} %copy-done.1), calls=%async_computation | async-start | bytes 20971520 | tf_op jit(solution)/shard_map/cond/branch_1_fun/all_to_all | solution.py:576
  60.6 124.3 %copy-start.15 = (s32[16,128]{1,0:T(8,128)S(1)}, s32[16,128]{1,0:T(8,128)}, u32[]{:S(2)}) copy-start(s32[16,128]{1,0:T(8,128)} %copy-done.14) | copy-start | bytes 24580 | tf_op jit(solution)/shard_map/cond
  94.0 133.8 %copy-start.22 = (f32[2,8,128]{2,1,0:T(8,128)}, f32[2,8,128]{2,1,0:T(8,128)S(1)}, u32[]{:S(2)}) copy-start(f32[2,8,128]{2,1,0:T(8,128)S(1)} %get-tuple-element.243) | copy-start | bytes 24580 | tf_op jit(solution)/shard_map/cond
  94.0 9.8 %collective-permute-start = (bf16[128,16,1280]{2,1,0:T(8,128)(2,1)}, bf16[128,16,1280]{2,1,0:T(8,128)(2,1)S(1)}, u32[]{:S(2)}, u32[]{:S(2)}) collective-permute-start(bf16[128,16,1280]{2,1,0:T(8,128)(2,1)} %bitcast.172), channel_id=1, source_target_pairs={{0,1},{1,0},{2,3},{3,2},{4,5},{5,4},{6,7},{7,6},{8,9},{9,8},{10,11... | collective-permute-start | bytes 15728648 | tf_op jit(solution)/shard_map/cond/branch_1_fun/ppermute | solution.py:580
  103.9 2.3 copy-start.5
  185.0 2.5 copy-start.6
  192.5 2.2 copy-start.2
  194.8 73.2 %all-to-all-start.1 = ((bf16[128,16,1280]{2,1,0:T(8,128)(2,1)}), bf16[128,16,1280]{2,1,0:T(8,128)(2,1)}, u32[]{:S(2)}, u32[]{:S(2)}) async-start(bf16[128,16,1280]{2,1,0:T(8,128)(2,1)} %copy-done.2), calls=%async_computation.1 | async-start | bytes 10485760 | tf_op jit(solution)/shard_map/cond/branch_1_fun/all_to_all | solution.py:576
  203.8 14.3 %copy-start.18 = (s32[16]{0:T(128)S(1)}, s32[16]{0:T(128)}, u32[]{:S(2)}) copy-start(s32[16]{0:T(128)} %get-tuple-element.248.lens_ref) | copy-start | bytes 196 | tf_op jit(solution)/shard_map/cond
  212.0 55.9 %collective-permute-start.1 = (bf16[64,16,1280]{2,1,0:T(8,128)(2,1)}, bf16[64,16,1280]{2,1,0:T(8,128)(2,1)S(1)}, u32[]{:S(2)}, u32[]{:S(2)}) collective-permute-start(bf16[64,16,1280]{2,1,0:T(8,128)(2,1)} %hand.3), channel_id=1, source_target_pairs={{0,1},{1,0},{2,3},{3,2},{4,5},{5,4},{6,7},{7,6},{8,9},{9,8},{10,11... | collective-permute-start | bytes 7864328 | tf_op jit(solution)/shard_map/cond/branch_1_fun/ppermute | solution.py:580
  218.1 49.9 %copy-start.10 = (s32[1280]{0:T(1024)S(1)}, s32[1280]{0:T(1024)}, u32[]{:S(2)}) copy-start(s32[1280]{0:T(1024)} %place.5.loc_ref) | copy-start | bytes 15364 | tf_op jit(solution)/shard_map/cond
  218.1 0.7 copy-start.9
  283.5 19.1 %all-to-all-start.2 = ((f32[128,1,128]{2,1,0:T(1,128)}), f32[128,1,128]{2,1,0:T(1,128)S(1)}, u32[]{:S(2)}, u32[]{:S(2)}) async-start(f32[128,1,128]{2,1,0:T(1,128)} %bitcast.40), calls=%async_computation.2 | async-start | bytes 131072 | tf_op jit(solution)/shard_map/cond/branch_1_fun/all_to_all | solution.py:576
where the time goes:
time: 302 us; the launch traced here: 304 us
  waiting for transfers between devices  147 us (49%)
  Pallas kernels  68.8 us (23%)
  starting transfers between devices  36.9 us (12%)
  matrix products  19.3 us (6%)
  local copies, waits for them, and re-layouts  15.6 us (5%)
  other arithmetic  10.8 us (4%)
  loops' own time  4.27 us (1%)
    all_to_all x4, waiting for transfers between devices, exchange(): return lax.all_to_all(x, 'shard', split_axis=0, concat_axis=0, tiled=True)  138 us
    all_to_all x4, starting transfers between devices, exchange(): return lax.all_to_all(x, 'shard', split_axis=0, concat_axis=0, tiled=True)  35.2 us
    pallas_call x2, Pallas kernels, match(): pl.pallas_call(functools.partial(match_kernel, late, tuple(ends)), out_sh...  24.5 us
    pallas_call x1, Pallas kernels, route(): pl.pallas_call(functools.partial(route_kernel, c2), out_shape=jax.ShapeDt...  20.7 us
    dot_general x2, matrix products, one_block(): jnp.einsum('bie,qje->bqij', block_rows, embeddings, preferred_element_typ...  19.3 us
    cond x20, local copies, waits for them, and re-layouts  12.2 us
    ppermute x2, waiting for transfers between devices, other_core(): return lax.ppermute(x, 'shard', [(d, d ^ 1) for d in range(N)])  8.5 us
    pallas_call x1, Pallas kernels, hand(): pl.pallas_call(hand_kernel, out_shape=jax.ShapeDtypeStruct((K,) + got.sha...  8.17 us
  transfers between devices with their start and end apart: 6, of which 5 were waited for; matrix products, arithmetic and copies ran while one was open for 10% of the time, Pallas kernels for 8%

commit v1 on v0

--- a/solution.py
+++ b/solution.py
@@ -14,7 +14,6 @@
 K = 64
 DEPTH = 16
 GROUP = 4
-URGENT = 64
 TRIES = 6
 
 R_F1ROW, R_F1COL, R_F1COLM, R_F2ROW, R_F2COL, R_SEND, R_SENDM, R_GIN, R_LIN, R_OWN, R_LEFT, R_GOUT = range(12)
@@ -86,7 +85,7 @@
     rem = m_tot - n
     w1 = free1 - n
     for k in range(C1):
-        w1 = w1 | jnp.where(k < n, ((r << 3) | k) << (2 + 11 * k), 0)
+        w1 = w1 | jnp.where(k < n, ((r << 3) | k) << (2 + 12 * k), 0)
     free2 = jnp.where(diag, 0, c2)
     g_from = m_tot - rem
     n = jnp.minimum(rem, free2)
@@ -94,6 +93,22 @@
     w2 = free2 - n
     for k in range(c2):
         w2 = w2 | jnp.where(k < n, ((g_from + k) << 2) << (2 + 14 * k), 0)
+    m_swap = swap_rows(m_tot, s)
+    rem_s = swap_rows(rem, s)
+    used = C1 - (w1 & 3)
+    n = jnp.where(diag, 0, jnp.minimum(rem_s, w1 & 3))
+    w1 = w1 - n
+    for k in range(C1):
+        code = (1 << 11) | (r << 3) | (m_swap - rem_s + k - used)
+        w1 = w1 | jnp.where((k >= used) & (k < used + n), code << (2 + 12 * k), 0)
+    rem_s = rem_s - n
+    used = c2 - (w2 & 3)
+    n = jnp.where(diag, 0, jnp.minimum(rem_s, w2 & 3))
+    w2 = w2 - n
+    for k in range(c2):
+        code = 1 | ((m_swap - rem_s + k - used) << 2)
+        w2 = w2 | jnp.where((k >= used) & (k < used + n), code << (2 + 14 * k), 0)
+    rem = swap_rows(rem_s - n, s)
     rem_c = swap_cols(rem, r)
     g_from = swap_cols(m_tot, r) - rem_c
     used = C1 - (w1 & 3)
@@ -102,62 +117,56 @@
     w1 = w1 - n
     for k in range(C1):
         code = (1 << 10) | ((r ^ 1) << 3) | (g_from + k - used)
-        w1 = w1 | jnp.where((k >= used) & (k < used + n), code << (2 + 11 * k), 0)
+        w1 = w1 | jnp.where((k >= used) & (k < used + n), code << (2 + 12 * k), 0)
     rem = swap_cols(rem_c - n, r)
-    rem_s = swap_rows(rem, s)
-    g_from = swap_rows(m_tot, s) - rem_s
-    used = c2 - (w2 & 3)
-    n = jnp.where(diag, 0, jnp.minimum(rem_s, w2 & 3))
-    w2 = w2 - n
-    for k in range(c2):
-        code = 1 | ((g_from + k - used) << 2)
-        w2 = w2 | jnp.where((k >= used) & (k < used + n), code << (2 + 14 * k), 0)
-    rem = swap_rows(rem_s - n, s)
 
     w1 = skew(w1, s, 1, -1)
     w2 = skew(w2, r, 0, -1)
 
-    def step(least, urgent, w1, w2, rem):
+    last = m_tot - 1
+    kept2 = ((s << 6) | 2) << 2
+
+    def step(limit, w1, w2, g):
         f1 = w1 & 3
         f2 = w2 & 3
-        ok = (jnp.minimum(jnp.minimum(f1, f2), rem) > 0) & (rem + urgent >= least)
-        g = m_tot - rem
-        code1 = (r << 3) | g
-        code2 = 2 | (g << 2) | ((C1 - f1) << 5) | (s << 6)
-        new1 = (w1 - 1) | (code1 << jnp.where(f1 == C1, 2, 13))
-        new2 = (w2 - 1) | (code2 << jnp.where(f2 == c2, 2, 16))
-        w1 = jnp.where(ok, new1, w1)
-        w2 = jnp.where(ok, new2, w2)
-        rem = jnp.where(ok, rem - 1, rem)
-        return pltpu.roll(w1, N - 1, 1), pltpu.roll(w2, N - 1, 0), rem
+        ok = (jnp.minimum(f1, f2) > 0) & (g <= limit)
+        first = f1 == C1
+        at = g << 2
+        code1 = (r << 5) | at
+        w1_new = w1 + jnp.where(first, code1, code1 << 12) - 1
+        code2 = kept2 + (at << 2) + jnp.where(first, 0, 1 << 7)
+        if c2 > 1:
+            code2 = jnp.where(f2 == c2, code2, code2 << 14)
+        w2_new = w2 + code2 - 1
+        w1 = jnp.where(ok, w1_new, w1)
+        w2 = jnp.where(ok, w2_new, w2)
+        g = jnp.where(ok, g + 1, g)
+        return pltpu.roll(w1, N - 1, 1), pltpu.roll(w2, N - 1, 0), g
 
     first_ref[0] = w1
     first_ref[1] = w2
-    first_ref[2] = rem
+    first_ref[2] = m_tot - rem
+
+    def sweep(limit, turns, w1, w2, g):
+        def body(c):
+            i, _, w1, w2, g = c
+            for _ in range(8):
+                w1, w2, g = step(limit, w1, w2, g)
+            return i + 1, jnp.max(limit - g), w1, w2, g
+
+        i, most, w1, w2, g = lax.while_loop(
+            lambda c: (c[0] < N // 8) & (c[1] >= 0),
+            body,
+            (jnp.int32(0), jnp.max(limit - g), w1, w2, g),
+        )
+        return most, turns + 8 * i, w1, w2, g
 
     def attempt(c):
         tries, _, _, _, _, urgent = c
-        w1, w2, rem = first_ref[0], first_ref[1], first_ref[2]
-        turns = jnp.int32(0)
-        left = jnp.int32(0)
-        for least in (URGENT, 4, 2, 1):
-
-            def open_count(rem):
-                return jnp.sum(((rem > 0) & (rem + urgent >= least)).astype(jnp.int32))
-
-            def body(c):
-                i, _, w1, w2, rem = c
-                for _ in range(8):
-                    w1, w2, rem = step(least, urgent, w1, w2, rem)
-                return i + 1, open_count(rem), w1, w2, rem
-
-            i, left, w1, w2, rem = lax.while_loop(
-                lambda c: (c[0] < N // 8) & (c[1] > 0),
-                body,
-                (jnp.int32(0), open_count(rem), w1, w2, rem),
-            )
-            turns = turns + 8 * i
-        return tries + 1, left, turns, w1, w2, jnp.where(rem > 0, URGENT, urgent)
+        limit = jnp.where(urgent > 0, last, -1)
+        _, turns, w1, w2, g = sweep(limit, 0, first_ref[0], first_ref[1], first_ref[2])
+        most, turns, w1, w2, g = sweep(last, turns, w1, w2, g)
+        return tries + 1, most + 1, turns, w1, w2, jnp.where(g <= last, 1, urgent)
 
     _, left, turns, w1, w2, _ = lax.while_loop(
         lambda c: (c[0] < TRIES) & (c[1] > 0),
@@ -201,7 +210,7 @@
     )(me, plan)
 
 
-def pack1_kernel(tab_ref, own_ref, out_ref, buf, sem):
+def pack1_kernel(tab_ref, own_ref, mate_ref, out_ref, buf, sem):
     parts = sem.shape[0]
     each = N // parts
 
@@ -213,8 +222,18 @@
         def body(j, _):
             w = tab_ref[R_F1ROW, j]
             for k in range(C1):
-                code = w >> (2 + 11 * k)
-                buf[j * C1 + k] = own_ref[tab_ref[R_SEND, (code >> 3) & (N - 1)] * GR + (code & 7)]
+                code = w >> (2 + 12 * k)
+                to = (code >> 3) & (N - 1)
+                from_mate = (code >> 11) & 1
+
+                @pl.when(from_mate == 0)
+                def _():
+                    buf[j * C1 + k] = own_ref[tab_ref[R_SEND, to] * GR + (code & 7)]
+
+                @pl.when(from_mate == 1)
+                def _():
+                    buf[j * C1 + k] = mate_ref[tab_ref[R_SENDM, to] * GR + (code & 7)]
+
             return 0
 
         lax.fori_loop(part * each, (part + 1) * each, body, 0, unroll=4)
@@ -223,18 +242,18 @@
         pltpu.make_async_copy(piece(buf, part), piece(out_ref, part), sem.at[part]).wait()
 
 
-def pack1(tab, own):
+def pack1(tab, own, mate):
     parts = 8
     shape = (N * C1,) + own.shape[1:]
     return pl.pallas_call(
         pack1_kernel,
-        out_shape=jax.ShapeDtypeStruct(shape, own.dtype),
-        in_specs=[pl.BlockSpec(memory_space=pltpu.SMEM), pl.BlockSpec(memory_space=pltpu.VMEM)],
+        out_shape=pltpu.HBM(shape, own.dtype),
+        in_specs=[pl.BlockSpec(memory_space=pltpu.SMEM)] + [pl.BlockSpec(memory_space=pltpu.VMEM)] * 2,
         out_specs=pl.BlockSpec(memory_space=pltpu.HBM),
         scratch_shapes=[pltpu.VMEM(shape, own.dtype), pltpu.SemaphoreType.DMA((parts,))],
         compiler_params=pltpu.CompilerParams(vmem_limit_bytes=40 << 20),
         name="pack1",
-    )(tab, own)
+    )(tab, own, mate)
 
 
 def pack2_kernel(c2, tab_ref, own_ref, mate_ref, got_ref, out_ref, buf, in_sem, out_sem):
@@ -287,7 +306,7 @@
     shape = (N * c2,) + own.shape[1:]
     return pl.pallas_call(
         functools.partial(pack2_kernel, c2),
-        out_shape=jax.ShapeDtypeStruct(shape, own.dtype),
+        out_shape=pltpu.HBM(shape, own.dtype),
         in_specs=[pl.BlockSpec(memory_space=pltpu.SMEM)] + [pl.BlockSpec(memory_space=pltpu.HBM)] * 3,
         out_specs=pl.BlockSpec(memory_space=pltpu.HBM),
         scratch_shapes=[
@@ -297,14 +316,14 @@
         ],
         compiler_params=pltpu.CompilerParams(vmem_limit_bytes=40 << 20),
         name="pack2",
-    )(tab, own, mate, got)
+    )(tab, *(pltpu.with_memory_space_constraint(x, pltpu.HBM) for x in (own, mate, got)))
 
 
 def hand_kernel(tab_ref, got_ref, out_ref, sem):
     def body(s, count):
         w = tab_ref[R_F1COL, s]
         for k in range(C1):
-            mine = (w >> (2 + 11 * k + 10)) & 1
+            mine = (w >> (2 + 12 * k + 10)) & 1
 
             @pl.when(mine == 1)
             def _():
@@ -366,15 +385,15 @@
             w = tab_ref[R_F1COL, s]
             filled = C1 - (w & 3)
             for k in range(C1):
-                code = w >> (2 + 11 * k)
+                code = w >> (2 + 12 * k)
 
                 @pl.when((k < filled) & (((code >> 3) & 0xFF) == me) & (s != me))
                 def _():
-                    loc_ref[s * GR + (code & 7)] = s * C1 + k
+                    loc_ref[(s ^ ((code >> 11) & 1)) * GR + (code & 7)] = s * C1 + k
 
             w = tab_ref[R_F1COLM, s]
             for k in range(C1):
-                code = w >> (2 + 11 * k)
+                code = w >> (2 + 12 * k)
                 handed_here = (code >> 10) & 1
 
                 @pl.when(handed_here == 1)
@@ -422,9 +441,10 @@
     )(me, tab)
 
 
-def match_kernel(late, ends, tab_ref, loc_ref, lens_ref, own_ref, best0_ref, ret0_ref, *refs):
+def match_kernel(late, ends, tab_ref, loc_ref, lens_ref, own_t_ref, best0_ref, ret0_ref, *refs):
     gots, (best_ref, ret_ref, buf, sem) = refs[: len(ends)], refs[len(ends) :]
-    scale = 1.0 / jnp.sqrt(jnp.float32(own_ref.shape[2]))
+    width = own_t_ref.shape[1]
+    scale = 1.0 / jnp.sqrt(jnp.float32(width))
     best_ref[...] = best0_ref[...]
     ret_ref[...] = ret0_ref[...]
     count = loc_ref[N * GR + N + int(late)]
@@ -474,26 +494,23 @@
     def score_of(i):
         s = sender(i)
         p = tab_ref[R_OWN, s]
-        incoming = buf[i & (DEPTH - 1)].reshape(N, own_ref.shape[2])
-        score = lax.dot_general(
-            own_ref[p], incoming, (((1,), (1,)), ((), ())), preferred_element_type=jnp.float32
-        )
-        return s, p, score * scale
+        incoming = buf[i & (DEPTH - 1)].reshape(N, width)
+        return s, p, jnp.dot(incoming, own_t_ref[p], preferred_element_type=jnp.float32) * scale
 
     def best_of(s, p, score):
         len_in = tab_ref[R_LIN, s]
         len_own = lens_ref[p]
-        real_in = col < len_in
-        real_own = row < len_own
-        over_in = jnp.sum(jnp.where(real_in, score, 0.0), 1, keepdims=True) / len_in.astype(jnp.float32)
-        own_count = len_own.astype(jnp.float32)
-        over_own = jnp.sum(jnp.where(real_own, score, 0.0), 0, keepdims=True) / own_count
-        grand = jnp.sum(jnp.where(real_own[:, :1], over_in, 0.0), 0, keepdims=True) / own_count
+        in_count = len_in.astype(jnp.float32)
+        real_in = row < len_in
+        real_own = col < len_own
+        over_own = jnp.sum(jnp.where(real_own, score, 0.0), 1, keepdims=True) / len_own.astype(jnp.float32)
+        over_in = jnp.sum(jnp.where(real_in, score, 0.0), 0, keepdims=True) / in_count
+        grand = jnp.sum(jnp.where(real_in[:, :1], over_own, 0.0), 0, keepdims=True) / in_count
         own_best = (
-            jnp.max(jnp.where(real_in, score - over_own, lowest), 1, keepdims=True) - over_in + grand
+            jnp.max(jnp.where(real_in, score - over_own, lowest), 0, keepdims=True) - over_in + grand
         )
         in_best = (
-            jnp.max(jnp.where(real_own, score - over_in, lowest), 0, keepdims=True) - over_own + grand
+            jnp.max(jnp.where(real_own, score - over_in, lowest), 1, keepdims=True) - over_own + grand
         )
         return own_best, in_best
 
@@ -505,34 +522,36 @@
             arrive(first + u)
         scores = [score_of(jnp.minimum(first + u, count - 1)) for u in range(GROUP)]
         found = [best_of(*x) for x in scores]
-        best = best_ref[...]
+        ret = ret_ref[...]
         for (s, p, _), (own_best, in_best) in zip(scores, found):
-            best = jnp.where(col == p, jnp.maximum(best, own_best), best)
-            ret_ref[pl.ds(s, 1), :] = in_best
-        best_ref[...] = best
+            best_ref[pl.ds(p, 1), :] = jnp.maximum(best_ref[pl.ds(p, 1), :], own_best)
+            ret = jnp.where(col == s, in_best, ret)
+        ret_ref[...] = ret
         return 0
 
     lax.fori_loop(0, (count + GROUP - 1) // GROUP, body, 0)
-
-
-def match(late, tab, loc, lens, own, best, ret, *gots):
+    if late:
+        ret_ref[...] = ret_ref[...].T
+
+
+def match(late, tab, loc, lens, own_t, best, ret, *gots):
     ends = []
     for got in gots:
         ends.append((ends[-1] if ends else 0) + got.shape[0])
     return pl.pallas_call(
         functools.partial(match_kernel, late, tuple(ends)),
-        out_shape=[jax.ShapeDtypeStruct((N, N), jnp.float32)] * 2,
+        out_shape=[jax.ShapeDtypeStruct(x.shape, x.dtype) for x in (best, ret)],
         in_specs=[pl.BlockSpec(memory_space=pltpu.SMEM)] * 3
         + [pl.BlockSpec(memory_space=pltpu.VMEM)] * 3
         + [pl.BlockSpec(memory_space=pltpu.HBM)] * len(gots),
         out_specs=[pl.BlockSpec(memory_space=pltpu.VMEM)] * 2,
         scratch_shapes=[
-            pltpu.VMEM((DEPTH, GR, 16, own.shape[2]), own.dtype),
+            pltpu.VMEM((DEPTH, GR, 16, own_t.shape[1]), own_t.dtype),
             pltpu.SemaphoreType.DMA((DEPTH, GR)),
         ],
         compiler_params=pltpu.CompilerParams(vmem_limit_bytes=40 << 20),
         name="match_late" if late else "match_early",
-    )(tab, loc, lens, own, best, ret, *gots)
+    )(tab, loc, lens, own_t, best, ret, *gots)
 
 
 def centred(score_matrix, row_validity_mask, col_mask):
@@ -589,38 +608,41 @@
     plan = exchange(jnp.broadcast_to(plan, (N, 3 * N)))
     own = embeddings.reshape(proteins_here * GR, 16, width)
 
-    nothing = jnp.full((N, N), lowest, jnp.float32)
+    mate = other_core(own)
+    none_own = jnp.full((proteins_here, slots), lowest, jnp.float32)
+    none_in = jnp.full((N, slots), lowest, jnp.float32)
 
     def finish(tab, best, ret, local_best):
         returned = exchange(ret)
         mine = (tab[R_SEND][None, :] == jnp.arange(proteins_here)[:, None]) & (tab[R_GOUT] > 0)[None, :]
         from_ret = jnp.max(jnp.where(mine[:, :, None], returned[None, :, :], lowest), 1)
-        best = jnp.maximum(from_ret, best[:, :proteins_here].T)
+        best = jnp.maximum(from_ret, best)
         cross_best = jnp.where((masks > 0) & (best > -1e29), best, 0.0)
         return local_best, cross_best
 
     def packed(c2, tab):
         loc = place(c2, me, tab)
-        got1 = exchange(pack1(tab, own))
+        got1 = exchange(pack1(tab, own, mate))
         local_best = within_cluster(embeddings, masks)
-        rows, local_best = lax.optimization_barrier((own, local_best))
-        mate = other_core(rows)
-        got1, local_best, mate = lax.optimization_barrier((got1, local_best, mate))
+        rows, local_best = lax.optimization_barrier((embeddings, local_best))
+        own_t = jnp.swapaxes(rows, 1, 2)
+        got1, local_best, own_t = lax.optimization_barrier((got1, local_best, own_t))
         send2 = pack2(c2, tab, own, mate, got1)
         send2, got1 = lax.optimization_barrier((send2, got1))
         got2 = exchange(send2)
         handed = other_core(hand(tab, got1))
-        best, ret = match(False, tab, loc, lengths, embeddings, nothing, nothing, got1)
+        best, ret = match(False, tab, loc, lengths, own_t, none_own, none_in, got1)
         best, ret, got2 = lax.optimization_barrier((best, ret, got2))
-        best, ret = match(True, tab, loc, lengths, embeddings, best, ret, got1, got2, handed)
+        best, ret = match(True, tab, loc, lengths, own_t, best, ret, got1, got2, handed)
         return finish(tab, best, ret, local_best)
 
     def whole(tab):
         loc = place(0, me, tab)
         got = exchange(pack_whole(tab, own))
+        own_t = jnp.swapaxes(embeddings, 1, 2)
         local_best = within_cluster(embeddings, masks)
-        best, ret = match(False, tab, loc, lengths, embeddings, nothing, nothing, got)
-        best, ret = match(True, tab, loc, lengths, embeddings, best, ret, got)
+        best, ret = match(False, tab, loc, lengths, own_t, none_own, none_in, got)
+        best, ret = match(True, tab, loc, lengths, own_t, best, ret, got)
         return finish(tab, best, ret, local_best)
 
     def second(_):

time: 302 us -> 291 us (0.964)
  Pallas kernels: 68.8 us -> 55.7 us
  waiting for transfers between devices: 147 us -> 142 us
    pallas_call x2, Pallas kernels: 24.5 us -> 13.8 us  [match(): pl.pallas_call(functools.partial(match_kernel, late, tuple(ends)), out_sh...]
    pallas_call x1, Pallas kernels: 20.7 us -> 10.2 us  [route(): pl.pallas_call(functools.partial(route_kernel, c2), out_shape=jax.ShapeDt...]
    pallas_call x2, Pallas kernels: 9.66 us -> 18.4 us  [the longest x1 10.7 us: pack1(): pl.pallas_call(pack1_kernel, out_shape=pltpu.HBM(shape, own.dtype), in_sp...]
    ppermute x2, waiting for transfers between devices: 8.5 us -> 0.01 us  [other_core(): return lax.ppermute(x, 'shard', [(d, d ^ 1) for d in range(N)])]
    another operation x0 -> x1, local copies, waits for them, and re-layouts: none -> 7.88 us
    cond x21 -> x12, local copies, waits for them, and re-layouts: 12.9 us -> 5.68 us
    all_to_all x4, waiting for transfers between devices: 138 us -> 142 us  [exchange(): return lax.all_to_all(x, 'shard', split_axis=0, concat_axis=0, tiled=True)]
  transfers between devices with their start and end apart: 6 -> 6, of which waited for: 5 -> 4; matrix products, arithmetic and copies ran while one was open for 10% -> 15% of each run, Pallas kernels for 8% -> 10%
where the time goes in v1:
time: 291 us
  waiting for transfers between devices  142 us (49%)
  Pallas kernels  55.7 us (19%)
  starting transfers between devices  38.6 us (13%)
  matrix products  19.2 us (7%)
  local copies, waits for them, and re-layouts  18.1 us (6%)
  other arithmetic  11.7 us (4%)
  loops' own time  4.28 us (1%)
    all_to_all x4, waiting for transfers between devices, exchange(): return lax.all_to_all(x, 'shard', split_axis=0, concat_axis=0, tiled=True)  142 us
    all_to_all x4, starting transfers between devices, exchange(): return lax.all_to_all(x, 'shard', split_axis=0, concat_axis=0, tiled=True)  36.1 us
    dot_general x2, matrix products, one_block(): jnp.einsum('bie,qje->bqij', block_rows, embeddings, preferred_element_typ...  19.2 us
    pallas_call x2, Pallas kernels, match(): pl.pallas_call(functools.partial(match_kernel, late, tuple(ends)), out_sh...  13.8 us
    pallas_call x1, Pallas kernels, pack1(): pl.pallas_call(pack1_kernel, out_shape=pltpu.HBM(shape, own.dtype), in_sp...  10.7 us
    pallas_call x1, Pallas kernels, route(): pl.pallas_call(functools.partial(route_kernel, c2), out_shape=jax.ShapeDt...  10.2 us
    another operation x1, local copies, waits for them, and re-layouts  7.88 us
    pallas_call x1, Pallas kernels, pack2(): pl.pallas_call(functools.partial(pack2_kernel, c2), out_shape=pltpu.HBM(s...  7.74 us
  transfers between devices with their start and end apart: 6, of which 4 were waited for; matrix products, arithmetic and copies ran while one was open for 15% of the time, Pallas kernels for 10%

profile of v1, /device:TPU:1, one launch (start us, length us, event | category | flops | bytes accessed | tf_op | source)
XLA Modules:
  0.0 290.6 jit_solution(9481090981659295898)
XLA Ops:
  3.6 10.2 %all-to-all-start.8 = ((s32[128,1,384]{2,1,0:T(1,128)}), s32[128,1,384]{2,1,0:T(1,128)S(1)}, u32[]{:S(2)}, u32[]{:S(2)}) async-start(s32[128,1,384]{2,1,0:T(1,128)} %broadcast_in_dim.231), calls=%async_computation.8 | async-start | bytes 393216 | tf_op jit(solution)/shard_map/all_to_all | solution.py:595
  14.6 9.8 %all-to-all-done.8 = s32[128,1,384]{2,1,0:T(1,128)S(1)} async-done(((s32[128,1,384]{2,1,0:T(1,128)}), s32[128,1,384]{2,1,0:T(1,128)S(1)}, u32[]{:S(2)}, u32[]{:S(2)}) %all-to-all-start.8) | async-done | bytes 196640 | tf_op jit(solution)/shard_map/all_to_all | solution.py:595
  24.4 10.2 %route1.1 = s32[16,128]{1,0:T(8,128)} custom-call(s32[1]{0:T(128)} %bitcast.43.me_ref, s32[128,384]{1,0:T(8,128)S(1)} %bitcast.164), custom_call_target="tpu_custom_call" | custom-call | tf_op jit(solution)/shard_map/route1/pallas_call | solution.py:202
  36.4 253.6 %conditional.2 = ((f32[16,128]{1,0:T(8,128)}, f32[16,128]{1,0:T(8,128)S(1)})) conditional(s32[]{:T(128)} %bitcast.45, (s32[1]{0:T(128)}, s32[128,384]{1,0:T(8,128)S(1)}, f32[16,128]{1,0:T(8,128)S(1)}, bf16[16,128,1280]{2,1,0:T(8,128)(2,1)}, bf16[128,16,1280]{2,1,0:T(8,128)(2,1)}, /*index=5*/s32[16]{0:T(128)}, ...), branch_computations={%region_0.23_spmd, %region_23.34_spmd} | conditional | flops 5390275584 | bytes 172615264 | solution.py:653
  36.6 10.7 %pack1.3 = bf16[256,16,1280]{2,1,0:T(8,128)(2,1)} custom-call(s32[16,128]{1,0:T(8,128)} %get-tuple-element.247.tab_ref, bf16[128,16,1280]{2,1,0:T(8,128)(2,1)} %bitcast.162, bf16[128,16,1280]{2,1,0:T(8,128)(2,1)} %get-tuple-element.249.mate_ref), custom_call_target="tpu_custom_call" | custom-call | tf_op jit(solution)/shard_map/cond/branch_1_fun/pack1/pallas_call | solution.py:248
  47.3 5.2 %all-to-all-start = ((bf16[256,16,1280]{2,1,0:T(8,128)(2,1)}), bf16[256,16,1280]{2,1,0:T(8,128)(2,1)}, u32[]{:S(2)}, u32[]{:S(2)}) async-start(bf16[256,16,1280]{2,1,0:T(8,128)(2,1)} %pack1.3), calls=%async_computation | async-start | bytes 20971520 | tf_op jit(solution)/shard_map/cond/branch_1_fun/all_to_all | solution.py:595
  52.6 7.9 %copy.30 = bf16[16,128,1280]{1,2,0:T(8,128)(2,1)} copy(bf16[16,128,1280]{2,1,0:T(8,128)(2,1)} %get-tuple-element.596) | data formatting | bytes 10485760 | tf_op jit(solution)/shard_map
  60.6 33.4 %while.32 = (s32[]{:T(128)}, f32[2,8,128]{2,1,0:T(8,128)S(1)}, s32[2]{0:T(128)S(1)}, f32[16,128]{1,0:T(8,128)S(1)}, bf16[16,128,1280]{2,1,0:T(8,128)(2,1)}, /*in...) while((s32[]{:T(128)}, f32[2,8,128]{2,1,0:T(8,128)S(1)}, s32[2]{0:T(128)S(1)}, ...), condition=%wide.region_32.32_spmd, body=%wide.region_25.31_spmd.sunk | while | flops 5389736960 | bytes 25377404 | solution.py:591
  63.2 10.0 %multiply_reduce_fusion.15 = (f32[8,16,128]{2,1,0:T(8,128)S(1)}, f32[8,128,16]{1,2,0:T(8,128)S(1)}, f32[8,128,16,128]{1,3,2,0:T(8,128)S(1)}) fusion(f32[8,128]{1,0:T(8,128)S(1)} %broadcast_multiply_fusion.12, f32[16,128]{1,0:T(8,128)S(1)} %broadcast_multiply_fusion.13, bf16[16,128,1280]{2,1,0:T(8,128)(2,1)} %get-tuple-element.614, s32[]{:T(128)S(6)} %select_n.110), kind=kOutput, calls=%fused_computation.67.clone.1 | convolution fusion | flops 5377064960 | bytes 16396292 | tf_op jit(solution)/shard_map/cond/branch_1_fun/while/body/eval_jaxpr/bie,qje->bqij/dot_general | solution.py:578
  73.4 3.4 %fusion.41 = f32[8,16,128]{2,1,0:T(8,128)S(1)} fusion(f32[8,128,16,128]{1,3,2,0:T(8,128)S(1)} %get-tuple-element.557, f32[8,16]{1,0:T(8,128)S(1)} %broadcast_divide_fusion.9, f32[8,16,128]{2,1,0:T(8,128)S(1)} %get-tuple-element.562, f32[8,16,128]{2,1,0:T(8,128)S(1)} %get-tuple-element.563, pred[16,128]{1,0:T(8,128)(4,1)S(1)} %broadcast_compare_fusion.6), kind=kLoop, calls=%fused_computation.66.clone.1 | loop fusion | flops 12566528 | bytes 8587776 | tf_op jit(solution)/shard_map/cond/branch_1_fun/while/body/eval_jaxpr/reduce_max | solution.py:582
  80.2 9.3 %multiply_reduce_fusion.15 = (f32[8,16,128]{2,1,0:T(8,128)S(1)}, f32[8,128,16]{1,2,0:T(8,128)S(1)}, f32[8,128,16,128]{1,3,2,0:T(8,128)S(1)}) fusion(f32[8,128]{1,0:T(8,128)S(1)} %broadcast_multiply_fusion.12, f32[16,128]{1,0:T(8,128)S(1)} %broadcast_multiply_fusion.13, bf16[16,128,1280]{2,1,0:T(8,128)(2,1)} %get-tuple-element.614, s32[]{:T(128)S(6)} %select_n.110), kind=kOutput, calls=%fused_computation.67.clone.1 | convolution fusion | flops 5377064960 | bytes 16396292 | tf_op jit(solution)/shard_map/cond/branch_1_fun/while/body/eval_jaxpr/bie,qje->bqij/dot_general | solution.py:578
  89.7 3.4 %fusion.41 = f32[8,16,128]{2,1,0:T(8,128)S(1)} fusion(f32[8,128,16,128]{1,3,2,0:T(8,128)S(1)} %get-tuple-element.557, f32[8,16]{1,0:T(8,128)S(1)} %broadcast_divide_fusion.9, f32[8,16,128]{2,1,0:T(8,128)S(1)} %get-tuple-element.562, f32[8,16,128]{2,1,0:T(8,128)S(1)} %get-tuple-element.563, pred[16,128]{1,0:T(8,128)(4,1)S(1)} %broadcast_compare_fusion.6), kind=kLoop, calls=%fused_computation.66.clone.1 | loop fusion | flops 12566528 | bytes 8587776 | tf_op jit(solution)/shard_map/cond/branch_1_fun/while/body/eval_jaxpr/reduce_max | solution.py:582
  94.0 83.0 %all-to-all-done.got_ref.refs_0_ = bf16[256,16,1280]{2,1,0:T(8,128)(2,1)} async-done(((bf16[256,16,1280]{2,1,0:T(8,128)(2,1)}), bf16[256,16,1280]{2,1,0:T(8,128)(2,1)}, u32[]{:S(2)}, u32[]{:S(2)}) %all-to-all-start) | async-done | bytes 10485792 | tf_op jit(solution)/shard_map/cond/branch_1_fun/all_to_all | solution.py:595
  177.0 7.7 %pack2.3 = bf16[128,16,1280]{2,1,0:T(8,128)(2,1)} custom-call(s32[16,128]{1,0:T(8,128)} %get-tuple-element.247.tab_ref, bf16[128,16,1280]{2,1,0:T(8,128)(2,1)} %bitcast.163, bf16[128,16,1280]{2,1,0:T(8,128)(2,1)} %get-tuple-element.249.mate_ref, bf16[256,16,1280]{2,1,0:T(8,128)(2,1)} %all-to-all-done.got_ref.refs_0_), custom_call_target="tpu_custom_call" | custom-call | tf_op jit(solution)/shard_map/cond/branch_1_fun/pack2/pallas_call | solution.py:307
  184.7 9.0 %all-to-all-start.1 = ((bf16[128,16,1280]{2,1,0:T(8,128)(2,1)}), bf16[128,16,1280]{2,1,0:T(8,128)(2,1)}, u32[]{:S(2)}, u32[]{:S(2)}) async-start(bf16[128,16,1280]{2,1,0:T(8,128)(2,1)} %pack2.3), calls=%async_computation.1 | async-start | bytes 10485760 | tf_op jit(solution)/shard_map/cond/branch_1_fun/all_to_all | solution.py:595
  193.7 7.3 %hand.3 = bf16[64,16,1280]{2,1,0:T(8,128)(2,1)S(1)} custom-call(s32[16,128]{1,0:T(8,128)} %get-tuple-element.247.tab_ref, bf16[256,16,1280]{2,1,0:T(8,128)(2,1)} %all-to-all-done.got_ref.refs_0_), custom_call_target="tpu_custom_call" | custom-call | tf_op jit(solution)/shard_map/cond/branch_1_fun/hand/pallas_call | solution.py:346
  202.0 6.0 %place.5.loc_ref = s32[1280]{0:T(1024)} custom-call(s32[1]{0:T(128)} %get-tuple-element.256.me_ref, s32[16,128]{1,0:T(8,128)} %get-tuple-element.247.tab_ref), custom_call_target="tpu_custom_call" | custom-call | tf_op jit(solution)/shard_map/cond/branch_1_fun/place/pallas_call | solution.py:435
  209.4 2.5 copy-done
  212.6 5.8 %match_early.5 = (f32[16,128]{1,0:T(8,128)S(1)}, f32[128,128]{1,0:T(8,128)S(1)}) custom-call(s32[16,128]{1,0:T(8,128)} %get-tuple-element.247.tab_ref, s32[1280]{0:T(1024)S(1)} %copy-done.2, s32[16]{0:T(128)S(1)} %copy-done.10, bf16[16,1280,128]{2,1,0:T(8,128)(2,1)S(1)} %bitcast.152, f32[16,128]{1,0:T(8,128)S(1)} %broadcast_in_dim.221.best0_ref, ...), custom_call_target="tpu_custom_call" | custom-call | tf_op jit(solution)/shard_map/cond/branch_1_fun/match_early/pallas_call | solution.py:541
  218.4 39.3 %all-to-all-done.1.refs_1_ = bf16[128,16,1280]{2,1,0:T(8,128)(2,1)} async-done(((bf16[128,16,1280]{2,1,0:T(8,128)(2,1)}), bf16[128,16,1280]{2,1,0:T(8,128)(2,1)}, u32[]{:S(2)}, u32[]{:S(2)}) %all-to-all-start.1) | async-done | bytes 5242912 | tf_op jit(solution)/shard_map/cond/branch_1_fun/all_to_all | solution.py:595
  257.8 2.5 copy-done.1
  260.3 8.0 %match_late.5 = (f32[16,128]{1,0:T(8,128)S(1)}, f32[128,128]{1,0:T(8,128)}) custom-call(s32[16,128]{1,0:T(8,128)} %get-tuple-element.247.tab_ref, s32[1280]{0:T(1024)S(1)} %copy-done.3, s32[16]{0:T(128)S(1)} %copy-done.10, bf16[16,1280,128]{2,1,0:T(8,128)(2,1)S(1)} %bitcast.153, f32[16,128]{1,0:T(8,128)S(1)} %get-tuple-element.264.best0_ref, ...), custom_call_target="tpu_custom_call" | custom-call | tf_op jit(solution)/shard_map/cond/branch_1_fun/match_late/pallas_call | solution.py:541
  268.3 11.7 %all-to-all-start.2 = ((f32[128,1,128]{2,1,0:T(1,128)}), f32[128,1,128]{2,1,0:T(1,128)S(1)}, u32[]{:S(2)}, u32[]{:S(2)}) async-start(f32[128,1,128]{2,1,0:T(1,128)} %bitcast.41), calls=%async_computation.2 | async-start | bytes 131072 | tf_op jit(solution)/shard_map/cond/branch_1_fun/all_to_all | solution.py:595
  280.0 9.6 %all-to-all-done.2 = f32[128,1,128]{2,1,0:T(1,128)S(1)} async-done(((f32[128,1,128]{2,1,0:T(1,128)}), f32[128,1,128]{2,1,0:T(1,128)S(1)}, u32[]{:S(2)}, u32[]{:S(2)}) %all-to-all-start.2) | async-done | bytes 65568 | tf_op jit(solution)/shard_map/cond/branch_1_fun/all_to_all | solution.py:595
  (54 shorter events, 12.6 us)
Async XLA Ops:
  0.6 35.8 %collective-permute-start.2 = (bf16[128,16,1280]{2,1,0:T(8,128)(2,1)}, bf16[128,16,1280]{2,1,0:T(8,128)(2,1)}, u32[]{:S(2)}, u32[]{:S(2)}) collective-permute-start(bf16[128,16,1280]{2,1,0:T(8,128)(2,1)} %bitcast.158), channel_id=1, source_target_pairs={{0,1},{1,0},{2,3},{3,2},{4,5},{5,4},{6,7},{7,6},{8,9},{9,8},{10,11... | collective-permute-start | bytes 15728648 | tf_op jit(solution)/shard_map/ppermute | solution.py:599
  3.6 20.7 %all-to-all-start.8 = ((s32[128,1,384]{2,1,0:T(1,128)}), s32[128,1,384]{2,1,0:T(1,128)S(1)}, u32[]{:S(2)}, u32[]{:S(2)}) async-start(s32[128,1,384]{2,1,0:T(1,128)} %broadcast_in_dim.231), calls=%async_computation.8 | async-start | bytes 393216 | tf_op jit(solution)/shard_map/all_to_all | solution.py:595
  47.3 129.6 %all-to-all-start = ((bf16[256,16,1280]{2,1,0:T(8,128)(2,1)}), bf16[256,16,1280]{2,1,0:T(8,128)(2,1)}, u32[]{:S(2)}, u32[]{:S(2)}) async-start(bf16[256,16,1280]{2,1,0:T(8,128)(2,1)} %pack1.3), calls=%async_computation | async-start | bytes 20971520 | tf_op jit(solution)/shard_map/cond/branch_1_fun/all_to_all | solution.py:595
  94.0 124.5 %copy-start.15 = (f32[2,8,128]{2,1,0:T(8,128)}, f32[2,8,128]{2,1,0:T(8,128)S(1)}, u32[]{:S(2)}) copy-start(f32[2,8,128]{2,1,0:T(8,128)S(1)} %get-tuple-element.252) | copy-start | bytes 24580 | tf_op jit(solution)/shard_map/cond
  184.7 73.1 %all-to-all-start.1 = ((bf16[128,16,1280]{2,1,0:T(8,128)(2,1)}), bf16[128,16,1280]{2,1,0:T(8,128)(2,1)}, u32[]{:S(2)}, u32[]{:S(2)}) async-start(bf16[128,16,1280]{2,1,0:T(8,128)(2,1)} %pack2.3), calls=%async_computation.1 | async-start | bytes 10485760 | tf_op jit(solution)/shard_map/cond/branch_1_fun/all_to_all | solution.py:595
  193.7 15.7 %copy-start.10 = (s32[16]{0:T(128)S(1)}, s32[16]{0:T(128)}, u32[]{:S(2)}) copy-start(s32[16]{0:T(128)} %get-tuple-element.257.lens_ref) | copy-start | bytes 196 | tf_op jit(solution)/shard_map/cond
  201.0 56.8 %collective-permute-start = (bf16[64,16,1280]{2,1,0:T(8,128)(2,1)S(1)}, bf16[64,16,1280]{2,1,0:T(8,128)(2,1)}, u32[]{:S(2)}, u32[]{:S(2)}) collective-permute-start(bf16[64,16,1280]{2,1,0:T(8,128)(2,1)S(1)} %hand.3), channel_id=1, source_target_pairs={{0,1},{1,0},{2,3},{3,2},{4,5},{5,4},{6,7},{7,6},{8,9},{9,8},{10,11... | collective-permute-start | bytes 7864328 | tf_op jit(solution)/shard_map/cond/branch_1_fun/ppermute | solution.py:599
  208.0 49.8 %copy-start.3 = (s32[1280]{0:T(1024)S(1)}, s32[1280]{0:T(1024)}, u32[]{:S(2)}) copy-start(s32[1280]{0:T(1024)} %place.5.loc_ref) | copy-start | bytes 15364 | tf_op jit(solution)/shard_map/cond
  209.4 2.5 copy-start
  211.9 0.7 copy-start.2
  257.8 2.5 copy-start.1
  268.3 21.3 %all-to-all-start.2 = ((f32[128,1,128]{2,1,0:T(1,128)}), f32[128,1,128]{2,1,0:T(1,128)S(1)}, u32[]{:S(2)}, u32[]{:S(2)}) async-start(f32[128,1,128]{2,1,0:T(1,128)} %bitcast.41), calls=%async_computation.2 | async-start | bytes 131072 | tf_op jit(solution)/shard_map/cond/branch_1_fun/all_to_all | solution.py:595
  290.0 0.6 copy-start.11

commit v2 on v1

--- a/solution.py
+++ b/solution.py
@@ -16,7 +16,7 @@
 GROUP = 4
 TRIES = 6
 
-R_F1ROW, R_F1COL, R_F1COLM, R_F2ROW, R_F2COL, R_SEND, R_SENDM, R_GIN, R_LIN, R_OWN, R_LEFT, R_GOUT = range(12)
+R_F1ROW, R_F1COL, R_F1COLM, R_F2ROW, R_F2COL, R_SEND, R_SENDM, R_GIN, R_LIN, R_OWN, R_GOUT = range(11)
 
 
 def swap_rows(x, s):
@@ -41,7 +41,7 @@
     return total - x
 
 
-def route_kernel(c2, me_ref, plan_ref, tab_ref, tmp_ref, first_ref):
+def route_kernel(c2, me_ref, plan_ref, tab_ref, left_ref, tmp_ref, first_ref):
     s = lax.broadcasted_iota(jnp.int32, (N, N), 0)
     r = lax.broadcasted_iota(jnp.int32, (N, N), 1)
     req = plan_ref[:, :N]
@@ -86,13 +86,6 @@
     w1 = free1 - n
     for k in range(C1):
         w1 = w1 | jnp.where(k < n, ((r << 3) | k) << (2 + 12 * k), 0)
-    free2 = jnp.where(diag, 0, c2)
-    g_from = m_tot - rem
-    n = jnp.minimum(rem, free2)
-    rem = rem - n
-    w2 = free2 - n
-    for k in range(c2):
-        w2 = w2 | jnp.where(k < n, ((g_from + k) << 2) << (2 + 14 * k), 0)
     m_swap = swap_rows(m_tot, s)
     rem_s = swap_rows(rem, s)
     used = C1 - (w1 & 3)
@@ -101,7 +94,15 @@
     for k in range(C1):
         code = (1 << 11) | (r << 3) | (m_swap - rem_s + k - used)
         w1 = w1 | jnp.where((k >= used) & (k < used + n), code << (2 + 12 * k), 0)
-    rem_s = rem_s - n
+    rem = swap_rows(rem_s - n, s)
+    free2 = jnp.where(diag, 0, c2)
+    g_from = m_tot - rem
+    n = jnp.minimum(rem, free2)
+    rem = rem - n
+    w2 = free2 - n
+    for k in range(c2):
+        w2 = w2 | jnp.where(k < n, ((g_from + k) << 2) << (2 + 14 * k), 0)
+    rem_s = swap_rows(rem, s)
     used = c2 - (w2 & 3)
     n = jnp.where(diag, 0, jnp.minimum(rem_s, w2 & 3))
     w2 = w2 - n
@@ -193,7 +194,7 @@
     put(m_tot.T, (R_GIN, me))
     put(lin.T, (R_LIN, me))
     put(pown.T, (R_OWN, me))
-    tab_ref[R_LEFT : R_LEFT + 1, :] = jnp.full((1, N), left, jnp.int32)
+    left_ref[0] = left
     put(m_tot, (R_GOUT, me))
     tab_ref[R_GOUT + 1 :, :] = jnp.zeros((16 - R_GOUT - 1, N), jnp.int32)
 
@@ -201,45 +202,58 @@
 def route(c2, me, plan):
     return pl.pallas_call(
         functools.partial(route_kernel, c2),
-        out_shape=jax.ShapeDtypeStruct((16, N), jnp.int32),
+        out_shape=[jax.ShapeDtypeStruct((16, N), jnp.int32), jax.ShapeDtypeStruct((1,), jnp.int32)],
         in_specs=[pl.BlockSpec(memory_space=pltpu.SMEM), pl.BlockSpec(memory_space=pltpu.VMEM)],
-        out_specs=pl.BlockSpec(memory_space=pltpu.VMEM),
+        out_specs=[pl.BlockSpec(memory_space=pltpu.VMEM), pl.BlockSpec(memory_space=pltpu.SMEM)],
         scratch_shapes=[pltpu.VMEM((N, N), jnp.int32), pltpu.VMEM((3, N, N), jnp.int32)],
         compiler_params=pltpu.CompilerParams(vmem_limit_bytes=32 << 20),
         name=f"route{c2}",
     )(me, plan)
 
 
-def pack1_kernel(tab_ref, own_ref, mate_ref, out_ref, buf, sem):
-    parts = sem.shape[0]
+def pack1_kernel(tab_ref, own_ref, mate_ref, out_ref, buf, in_sem, out_sem):
+    parts = out_sem.shape[0]
     each = N // parts
 
     def piece(ref, part):
         return ref.at[pl.ds(part * each * C1, each * C1)]
 
+    def codes(j):
+        w = tab_ref[R_F1ROW, j]
+        return [(k, w >> (2 + 12 * k)) for k in range(C1)]
+
+    def from_mate(part, j, k, code):
+        at = tab_ref[R_SENDM, (code >> 3) & (N - 1)] * GR + (code & 7)
+        return pltpu.make_async_copy(mate_ref.at[at], buf.at[j * C1 + k], in_sem.at[part])
+
     for part in range(parts):
 
-        def body(j, _):
-            w = tab_ref[R_F1ROW, j]
-            for k in range(C1):
-                code = w >> (2 + 12 * k)
-                to = (code >> 3) & (N - 1)
-                from_mate = (code >> 11) & 1
-
-                @pl.when(from_mate == 0)
+        def start(j, count, part=part):
+            for k, code in codes(j):
+                is_mate = (code >> 11) & 1
+
+                @pl.when(is_mate == 1)
                 def _():
-                    buf[j * C1 + k] = own_ref[tab_ref[R_SEND, to] * GR + (code & 7)]
-
-                @pl.when(from_mate == 1)
+                    from_mate(part, j, k, code).start()
+
+                @pl.when(is_mate == 0)
                 def _():
-                    buf[j * C1 + k] = mate_ref[tab_ref[R_SENDM, to] * GR + (code & 7)]
-
+                    at = tab_ref[R_SEND, (code >> 3) & (N - 1)] * GR + (code & 7)
+                    buf[j * C1 + k] = own_ref[at]
+
+                count = count + is_mate
+            return count
+
+        count = lax.fori_loop(part * each, (part + 1) * each, start, jnp.int32(0), unroll=4)
+
+        def finish(i, _, part=part):
+            pltpu.make_async_copy(mate_ref.at[0], buf.at[0], in_sem.at[part]).wait()
             return 0
 
-        lax.fori_loop(part * each, (part + 1) * each, body, 0, unroll=4)
-        pltpu.make_async_copy(piece(buf, part), piece(out_ref, part), sem.at[part]).start()
+        lax.fori_loop(0, count, finish, 0)
+        pltpu.make_async_copy(piece(buf, part), piece(out_ref, part), out_sem.at[part]).start()
     for part in range(parts):
-        pltpu.make_async_copy(piece(buf, part), piece(out_ref, part), sem.at[part]).wait()
+        pltpu.make_async_copy(piece(buf, part), piece(out_ref, part), out_sem.at[part]).wait()
 
 
 def pack1(tab, own, mate):
@@ -248,12 +262,20 @@
     return pl.pallas_call(
         pack1_kernel,
         out_shape=pltpu.HBM(shape, own.dtype),
-        in_specs=[pl.BlockSpec(memory_space=pltpu.SMEM)] + [pl.BlockSpec(memory_space=pltpu.VMEM)] * 2,
+        in_specs=[
+            pl.BlockSpec(memory_space=pltpu.SMEM),
+            pl.BlockSpec(memory_space=pltpu.VMEM),
+            pl.BlockSpec(memory_space=pltpu.HBM),
+        ],
         out_specs=pl.BlockSpec(memory_space=pltpu.HBM),
-        scratch_shapes=[pltpu.VMEM(shape, own.dtype), pltpu.SemaphoreType.DMA((parts,))],
-        compiler_params=pltpu.CompilerParams(vmem_limit_bytes=40 << 20),
+        scratch_shapes=[
+            pltpu.VMEM(shape, own.dtype),
+            pltpu.SemaphoreType.DMA((parts,)),
+            pltpu.SemaphoreType.DMA((parts,)),
+        ],
+        compiler_params=pltpu.CompilerParams(vmem_limit_bytes=24 << 20),
         name="pack1",
-    )(tab, own, mate)
+    )(tab, own, pltpu.with_memory_space_constraint(mate, pltpu.HBM))
 
 
 def pack2_kernel(c2, tab_ref, own_ref, mate_ref, got_ref, out_ref, buf, in_sem, out_sem):
@@ -375,76 +397,99 @@
 
 def place_kernel(c2, me_ref, tab_ref, loc_ref):
     me = me_ref[0]
-
-    def body(s, c):
-        count, handed = c
+    order, counts, late_of = N * GR, N * GR + N, N * GR + 2 * N
+
+    def clear(s, _):
+        loc_ref[late_of + s] = 0
         if c2 == 0:
             for g in range(GR):
                 loc_ref[s * GR + g] = s * GR + g
-        else:
-            w = tab_ref[R_F1COL, s]
-            filled = C1 - (w & 3)
-            for k in range(C1):
-                code = w >> (2 + 12 * k)
-
-                @pl.when((k < filled) & (((code >> 3) & 0xFF) == me) & (s != me))
-                def _():
-                    loc_ref[(s ^ ((code >> 11) & 1)) * GR + (code & 7)] = s * C1 + k
-
-            w = tab_ref[R_F1COLM, s]
-            for k in range(C1):
-                code = w >> (2 + 12 * k)
-                handed_here = (code >> 10) & 1
-
-                @pl.when(handed_here == 1)
-                def _():
-                    loc_ref[s * GR + (code & 7)] = (C1 + c2) * N + handed
-
-                handed = handed + handed_here
-
-            w = tab_ref[R_F2COL, s]
-            filled = c2 - (w & 3)
-            for k in range(c2):
-                code = w >> (2 + 14 * k)
-                kind = code & 3
-                origin = jnp.where(kind >= 2, (code >> 6) & (N - 1), s ^ (kind & 1))
-
-                @pl.when((k < filled) & (s != me))
-                def _():
-                    loc_ref[origin * GR + ((code >> 2) & 7)] = C1 * N + s * c2 + k
-
-        is_live = tab_ref[R_GIN, s] > 0
-
-        is_late = is_live & (tab_ref[R_GIN, s] > C1)
-        early, late = count
-
-        @pl.when(is_live)
+        return 0
+
+    lax.fori_loop(0, N, clear, 0)
+
+    def find(s, handed):
+        w = tab_ref[R_F1COL, s]
+        filled = C1 - (w & 3)
+        for k in range(C1):
+            code = w >> (2 + 12 * k)
+
+            @pl.when((k < filled) & (((code >> 3) & 0xFF) == me) & (s != me))
+            def _():
+                loc_ref[(s ^ ((code >> 11) & 1)) * GR + (code & 7)] = s * C1 + k
+
+        w = tab_ref[R_F1COLM, s]
+        for k in range(C1):
+            code = w >> (2 + 12 * k)
+            handed_here = (code >> 10) & 1
+
+            @pl.when(handed_here == 1)
+            def _():
+                loc_ref[s * GR + (code & 7)] = (C1 + c2) * N + handed
+                loc_ref[late_of + s] = 1
+
+            handed = handed + handed_here
+
+        w = tab_ref[R_F2COL, s]
+        filled = c2 - (w & 3)
+        for k in range(c2):
+            code = w >> (2 + 14 * k)
+            kind = code & 3
+            origin = jnp.where(kind >= 2, (code >> 6) & (N - 1), s ^ (kind & 1))
+
+            @pl.when((k < filled) & (s != me))
+            def _():
+                loc_ref[origin * GR + ((code >> 2) & 7)] = C1 * N + s * c2 + k
+                loc_ref[late_of + origin] = 1
+
+        return handed
+
+    if c2 > 0:
+        lax.fori_loop(0, N, find, jnp.int32(0))
+
+    def sort(s, c):
+        early, late = c
+        is_live = (tab_ref[R_GIN, s] > 0).astype(jnp.int32)
+        is_late = loc_ref[late_of + s]
+
+        @pl.when(is_live == 1)
         def _():
-            loc_ref[N * GR + jnp.where(is_late, N - 1 - late, early)] = s
-
-        late = late + is_late.astype(jnp.int32)
-        return (early + (is_live.astype(jnp.int32) - is_late.astype(jnp.int32)), late), handed
-
-    zero = jnp.int32(0)
-    (early, late), _ = lax.fori_loop(0, N, body, ((zero, zero), zero))
-    loc_ref[N * GR + N] = early
-    loc_ref[N * GR + N + 1] = late
+            loc_ref[order + jnp.where(is_late == 1, N - 1 - late, early)] = s
+
+        return early + is_live * (1 - is_late), late + is_live * is_late
+
+    early, late = lax.fori_loop(0, N, sort, (jnp.int32(0), jnp.int32(0)))
+    loc_ref[counts] = early
+    loc_ref[counts + 1] = late
 
 
 def place(c2, me, tab):
     return pl.pallas_call(
         functools.partial(place_kernel, c2),
-        out_shape=jax.ShapeDtypeStruct((N * GR + N + 128,), jnp.int32),
+        out_shape=jax.ShapeDtypeStruct((N * GR + 3 * N,), jnp.int32),
         in_specs=[pl.BlockSpec(memory_space=pltpu.SMEM)] * 2,
         out_specs=pl.BlockSpec(memory_space=pltpu.SMEM),
         name="place",
     )(me, tab)
 
 
+def best_of(row, col, len_in, len_own, incoming, own_t):
+    scale = 1.0 / jnp.sqrt(jnp.float32(own_t.shape[0]))
+    score = jnp.dot(incoming, own_t, preferred_element_type=jnp.float32) * scale
+    in_count = len_in.astype(jnp.float32)
+    real_in = row < len_in
+    real_own = col < len_own
+    over_own = jnp.sum(jnp.where(real_own, score, 0.0), 1, keepdims=True) / len_own.astype(jnp.float32)
+    over_in = jnp.sum(jnp.where(real_in, score, 0.0), 0, keepdims=True) / in_count
+    grand = jnp.sum(jnp.where(real_in[:, :1], over_own, 0.0), 0, keepdims=True) / in_count
+    own_best = jnp.max(jnp.where(real_in, score - over_own, lowest), 0, keepdims=True) - over_in + grand
+    in_best = jnp.max(jnp.where(real_own, score - over_in, lowest), 1, keepdims=True) - over_own + grand
+    return own_best, in_best
+
+
 def match_kernel(late, ends, tab_ref, loc_ref, lens_ref, own_t_ref, best0_ref, ret0_ref, *refs):
     gots, (best_ref, ret_ref, buf, sem) = refs[: len(ends)], refs[len(ends) :]
     width = own_t_ref.shape[1]
-    scale = 1.0 / jnp.sqrt(jnp.float32(width))
     best_ref[...] = best0_ref[...]
     ret_ref[...] = ret0_ref[...]
     count = loc_ref[N * GR + N + int(late)]
@@ -458,7 +503,7 @@
             s = sender(i)
             slot = i & (DEPTH - 1)
             granules = tab_ref[R_GIN, s]
-            for g in range(GR if late else min(GR, C1)):
+            for g in range(GR):
 
                 @pl.when(g < granules)
                 def _():
@@ -480,7 +525,7 @@
             s = sender(i)
             slot = i & (DEPTH - 1)
             granules = tab_ref[R_GIN, s]
-            for g in range(GR if late else min(GR, C1)):
+            for g in range(GR):
 
                 @pl.when(g < granules)
                 def _():
@@ -490,29 +535,6 @@
         fetch(i)
     row = lax.broadcasted_iota(jnp.int32, (N, N), 0)
     col = lax.broadcasted_iota(jnp.int32, (N, N), 1)
-
-    def score_of(i):
-        s = sender(i)
-        p = tab_ref[R_OWN, s]
-        incoming = buf[i & (DEPTH - 1)].reshape(N, width)
-        return s, p, jnp.dot(incoming, own_t_ref[p], preferred_element_type=jnp.float32) * scale
-
-    def best_of(s, p, score):
-        len_in = tab_ref[R_LIN, s]
-        len_own = lens_ref[p]
-        in_count = len_in.astype(jnp.float32)
-        real_in = row < len_in
-        real_own = col < len_own
-        over_own = jnp.sum(jnp.where(real_own, score, 0.0), 1, keepdims=True) / len_own.astype(jnp.float32)
-        over_in = jnp.sum(jnp.where(real_in, score, 0.0), 0, keepdims=True) / in_count
-        grand = jnp.sum(jnp.where(real_in[:, :1], over_own, 0.0), 0, keepdims=True) / in_count
-        own_best = (
-            jnp.max(jnp.where(real_in, score - over_own, lowest), 0, keepdims=True) - over_in + grand
-        )
-        in_best = (
-            jnp.max(jnp.where(real_own, score - over_in, lowest), 1, keepdims=True) - over_own + grand
-        )
-        return own_best, in_best
 
     def body(j, _):
         first = j * GROUP
@@ -520,10 +542,17 @@
             fetch(first + u + DEPTH - GROUP)
         for u in range(GROUP):
             arrive(first + u)
-        scores = [score_of(jnp.minimum(first + u, count - 1)) for u in range(GROUP)]
-        found = [best_of(*x) for x in scores]
+        found = []
+        for u in range(GROUP):
+            i = jnp.minimum(first + u, count - 1)
+            s = sender(i)
+            p = tab_ref[R_OWN, s]
+            incoming = buf[i & (DEPTH - 1)].reshape(N, width)
+            found.append((s, p) + best_of(
+                row, col, tab_ref[R_LIN, s], lens_ref[p], incoming, own_t_ref[p]
+            ))
         ret = ret_ref[...]
-        for (s, p, _), (own_best, in_best) in zip(scores, found):
+        for s, p, own_best, in_best in found:
             best_ref[pl.ds(p, 1), :] = jnp.maximum(best_ref[pl.ds(p, 1), :], own_best)
             ret = jnp.where(col == s, in_best, ret)
         ret_ref[...] = ret
@@ -554,6 +583,76 @@
     )(tab, loc, lens, own_t, best, ret, *gots)
 
 
+def near_kernel(late, ends, tab_ref, loc_ref, lens_ref, own_t_ref, best0_ref, ret0_ref, *refs):
+    gots, (best_ref, ret_ref, buf) = refs[: len(ends)], refs[len(ends) :]
+    width = own_t_ref.shape[1]
+    best_ref[...] = best0_ref[...]
+    ret_ref[...] = ret0_ref[...]
+    count = loc_ref[N * GR + N + int(late)]
+
+    def sender(i):
+        i = jnp.minimum(i, count - 1)
+        return loc_ref[N * GR + (N - 1 - i if late else i)]
+
+    def gather(i, u):
+        s = sender(i)
+        granules = tab_ref[R_GIN, s]
+        for g in range(GR):
+
+            @pl.when(g < granules)
+            def _():
+                at = loc_ref[s * GR + g]
+                start = 0
+                for got_ref, end in zip(gots, ends):
+
+                    @pl.when((at >= start) & (at < end))
+                    def _(got_ref=got_ref, start=start):
+                        buf[u, g] = got_ref[at - start]
+
+                    start = end
+
+    row = lax.broadcasted_iota(jnp.int32, (N, N), 0)
+    col = lax.broadcasted_iota(jnp.int32, (N, N), 1)
+
+    def body(j, _):
+        first = j * GROUP
+        for u in range(GROUP):
+            gather(first + u, u)
+        found = []
+        for u in range(GROUP):
+            s = sender(first + u)
+            p = tab_ref[R_OWN, s]
+            found.append((s, p) + best_of(
+                row, col, tab_ref[R_LIN, s], lens_ref[p], buf[u].reshape(N, width), own_t_ref[p]
+            ))
+        ret = ret_ref[...]
+        for s, p, own_best, in_best in found:
+            best_ref[pl.ds(p, 1), :] = jnp.maximum(best_ref[pl.ds(p, 1), :], own_best)
+            ret = jnp.where(col == s, in_best, ret)
+        ret_ref[...] = ret
+        return 0
+
+    lax.fori_loop(0, (count + GROUP - 1) // GROUP, body, 0)
+    if late:
+        ret_ref[...] = ret_ref[...].T
+
+
+def near(late, tab, loc, lens, own_t, best, ret, *gots):
+    ends = []
+    for got in gots:
+        ends.append((ends[-1] if ends else 0) + got.shape[0])
+    return pl.pallas_call(
+        functools.partial(near_kernel, late, tuple(ends)),
+        out_shape=[jax.ShapeDtypeStruct(x.shape, x.dtype) for x in (best, ret)],
+        in_specs=[pl.BlockSpec(memory_space=pltpu.SMEM)] * 3
+        + [pl.BlockSpec(memory_space=pltpu.VMEM)] * (3 + len(gots)),
+        out_specs=[pl.BlockSpec(memory_space=pltpu.VMEM)] * 2,
+        scratch_shapes=[pltpu.VMEM((GROUP, GR, 16, own_t.shape[1]), own_t.dtype)],
+        compiler_params=pltpu.CompilerParams(vmem_limit_bytes=40 << 20),
+        name="near_late" if late else "near_early",
+    )(tab, loc, lens, own_t, best, ret, *gots)
+
+
 def centred(score_matrix, row_validity_mask, col_mask):
     row_count = jnp.sum(row_validity_mask, -1)
     col_count = jnp.sum(col_mask, -1)
@@ -631,9 +730,9 @@
         send2, got1 = lax.optimization_barrier((send2, got1))
         got2 = exchange(send2)
         handed = other_core(hand(tab, got1))
-        best, ret = match(False, tab, loc, lengths, own_t, none_own, none_in, got1)
+        best, ret = near(False, tab, loc, lengths, own_t, none_own, none_in, got1)
         best, ret, got2 = lax.optimization_barrier((best, ret, got2))
-        best, ret = match(True, tab, loc, lengths, own_t, best, ret, got1, got2, handed)
+        best, ret = near(True, tab, loc, lengths, own_t, best, ret, got1, got2, handed)
         return finish(tab, best, ret, local_best)
 
     def whole(tab):
@@ -646,11 +745,11 @@
         return finish(tab, best, ret, local_best)
 
     def second(_):
-        tab = route(2, me, plan)
-        return lax.cond(tab[R_LEFT, 0] == 0, functools.partial(packed, 2), whole, tab)
-
-    tab = route(1, me, plan)
-    return lax.cond(tab[R_LEFT, 0] == 0, functools.partial(packed, 1), second, tab)
+        tab, left = route(2, me, plan)
+        return lax.cond(left[0] == 0, functools.partial(packed, 2), whole, tab)
+
+    tab, left = route(1, me, plan)
+    return lax.cond(left[0] == 0, functools.partial(packed, 1), second, tab)
 
 
 def solution(mesh):

time: 291 us -> 299 us (1.027)
  Pallas kernels: 55.7 us -> 68.1 us
  waiting for transfers between devices: 142 us -> 138 us
    pallas_call x3, Pallas kernels: 24 us -> 34.8 us  [the longest x2 23.9 us: near(): pl.pallas_call(functools.partial(near_kernel, late, tuple(ends)), out_sha...]
    all_to_all x4, waiting for transfers between devices: 142 us -> 138 us  [exchange(): return lax.all_to_all(x, 'shard', split_axis=0, concat_axis=0, tiled=True)]
  transfers between devices with their start and end apart: 6 -> 6, of which waited for: 4 -> 4; matrix products, arithmetic and copies ran while one was open for 15% -> 13% of each run, Pallas kernels for 10% -> 12%
where the time goes in v2:
time: 299 us; the launch traced here: 297 us
  waiting for transfers between devices  138 us (46%)
  Pallas kernels  68.1 us (23%)
  starting transfers between devices  39.6 us (13%)
  matrix products  19.2 us (6%)
  local copies, waits for them, and re-layouts  16.2 us (5%)
  other arithmetic  11 us (4%)
  loops' own time  4.45 us (1%)
    all_to_all x4, waiting for transfers between devices, exchange(): return lax.all_to_all(x, 'shard', split_axis=0, concat_axis=0, tiled=True)  138 us
    all_to_all x4, starting transfers between devices, exchange(): return lax.all_to_all(x, 'shard', split_axis=0, concat_axis=0, tiled=True)  37.2 us
    pallas_call x2, Pallas kernels, near(): pl.pallas_call(functools.partial(near_kernel, late, tuple(ends)), out_sha...  23.9 us
    dot_general x2, matrix products, one_block(): jnp.einsum('bie,qje->bqij', block_rows, embeddings, preferred_element_typ...  19.2 us
    pallas_call x1, Pallas kernels, route(): pl.pallas_call(functools.partial(route_kernel, c2), out_shape=[jax.ShapeD...  10.9 us
    pallas_call x1, Pallas kernels, pack1(): pl.pallas_call(pack1_kernel, out_shape=pltpu.HBM(shape, own.dtype), in_sp...  10.2 us
    pallas_call x1, Pallas kernels, pack2(): pl.pallas_call(functools.partial(pack2_kernel, c2), out_shape=pltpu.HBM(s...  7.97 us
    pallas_call x1, Pallas kernels, place(): pl.pallas_call(functools.partial(place_kernel, c2), out_shape=jax.ShapeDt...  7.93 us
  transfers between devices with their start and end apart: 6, of which 4 were waited for; matrix products, arithmetic and copies ran while one was open for 13% of the time, Pallas kernels for 12%

profile of v2, /device:TPU:1, one launch (start us, length us, event | category | flops | bytes accessed | tf_op | source)
XLA Modules:
  0.0 297.4 jit_solution(9575071445743092984)
XLA Ops:
  3.6 10.2 %all-to-all-start.8 = ((s32[128,1,384]{2,1,0:T(1,128)}), s32[128,1,384]{2,1,0:T(1,128)S(1)}, u32[]{:S(2)}, u32[]{:S(2)}) async-start(s32[128,1,384]{2,1,0:T(1,128)} %broadcast_in_dim.231), calls=%async_computation.8 | async-start | bytes 393216 | tf_op jit(solution)/shard_map/all_to_all | solution.py:694
  14.6 9.8 %all-to-all-done.8 = s32[128,1,384]{2,1,0:T(1,128)S(1)} async-done(((s32[128,1,384]{2,1,0:T(1,128)}), s32[128,1,384]{2,1,0:T(1,128)S(1)}, u32[]{:S(2)}, u32[]{:S(2)}) %all-to-all-start.8) | async-done | bytes 196640 | tf_op jit(solution)/shard_map/all_to_all | solution.py:694
  24.4 10.9 %route1.1 = (s32[16,128]{1,0:T(8,128)S(1)}, s32[1]{0:T(128)}) custom-call(s32[1]{0:T(128)} %bitcast.43.me_ref, s32[128,384]{1,0:T(8,128)S(1)} %bitcast.164), custom_call_target="tpu_custom_call" | custom-call | tf_op jit(solution)/shard_map/route1/pallas_call | solution.py:203
  35.9 260.9 %conditional.2 = ((f32[16,128]{1,0:T(8,128)}, f32[16,128]{1,0:T(8,128)S(1)})) conditional(s32[]{:T(128)} %bitcast.45, (s32[1]{0:T(128)}, s32[128,384]{1,0:T(8,128)S(1)}, f32[16,128]{1,0:T(8,128)S(1)}, bf16[16,128,1280]{2,1,0:T(8,128)(2,1)}, bf16[128,16,1280]{2,1,0:T(8,128)(2,1)}, /*index=5*/s32[16]{0:T(128)}, ...), branch_computations={%region_0.23_spmd, %region_23.34_spmd} | conditional | flops 5390275584 | bytes 172617312 | solution.py:752
  36.2 10.2 %pack1.3 = bf16[256,16,1280]{2,1,0:T(8,128)(2,1)} custom-call(s32[16,128]{1,0:T(8,128)S(1)} %get-tuple-element.249.tab_ref, bf16[128,16,1280]{2,1,0:T(8,128)(2,1)} %bitcast.162, bf16[128,16,1280]{2,1,0:T(8,128)(2,1)} %get-tuple-element.251.mate_ref), custom_call_target="tpu_custom_call" | custom-call | tf_op jit(solution)/shard_map/cond/branch_1_fun/pack1/pallas_call | solution.py:262
  46.3 8.9 %all-to-all-start = ((bf16[256,16,1280]{2,1,0:T(8,128)(2,1)}), bf16[256,16,1280]{2,1,0:T(8,128)(2,1)}, u32[]{:S(2)}, u32[]{:S(2)}) async-start(bf16[256,16,1280]{2,1,0:T(8,128)(2,1)} %pack1.3), calls=%async_computation | async-start | bytes 20971520 | tf_op jit(solution)/shard_map/cond/branch_1_fun/all_to_all | solution.py:694
  55.3 7.9 %copy.30 = bf16[16,128,1280]{1,2,0:T(8,128)(2,1)} copy(bf16[16,128,1280]{2,1,0:T(8,128)(2,1)} %get-tuple-element.602) | data formatting | bytes 10485760 | tf_op jit(solution)/shard_map
  63.3 33.6 %while.32 = (s32[]{:T(128)}, f32[2,8,128]{2,1,0:T(8,128)S(1)}, s32[2]{0:T(128)S(1)}, f32[16,128]{1,0:T(8,128)S(1)}, bf16[16,128,1280]{2,1,0:T(8,128)(2,1)}, /*in...) while((s32[]{:T(128)}, f32[2,8,128]{2,1,0:T(8,128)S(1)}, s32[2]{0:T(128)S(1)}, ...), condition=%wide.region_32.32_spmd, body=%wide.region_25.31_spmd.sunk | while | flops 5389736960 | bytes 25377404 | solution.py:690
  66.0 10.0 %multiply_reduce_fusion.15 = (f32[8,16,128]{2,1,0:T(8,128)S(1)}, f32[8,128,16]{1,2,0:T(8,128)S(1)}, f32[8,128,16,128]{1,3,2,0:T(8,128)S(1)}) fusion(f32[8,128]{1,0:T(8,128)S(1)} %broadcast_multiply_fusion.12, f32[16,128]{1,0:T(8,128)S(1)} %broadcast_multiply_fusion.13, bf16[16,128,1280]{2,1,0:T(8,128)(2,1)} %get-tuple-element.620, s32[]{:T(128)S(6)} %select_n.110), kind=kOutput, calls=%fused_computation.67.clone.1 | convolution fusion | flops 5377064960 | bytes 16396292 | tf_op jit(solution)/shard_map/cond/branch_1_fun/while/body/eval_jaxpr/bie,qje->bqij/dot_general | solution.py:677
  76.2 3.4 %fusion.41 = f32[8,16,128]{2,1,0:T(8,128)S(1)} fusion(f32[8,128,16,128]{1,3,2,0:T(8,128)S(1)} %get-tuple-element.563, f32[8,16]{1,0:T(8,128)S(1)} %broadcast_divide_fusion.9, f32[8,16,128]{2,1,0:T(8,128)S(1)} %get-tuple-element.568, f32[8,16,128]{2,1,0:T(8,128)S(1)} %get-tuple-element.569, pred[16,128]{1,0:T(8,128)(4,1)S(1)} %broadcast_compare_fusion.6), kind=kLoop, calls=%fused_computation.66.clone.1 | loop fusion | flops 12566528 | bytes 8587776 | tf_op jit(solution)/shard_map/cond/branch_1_fun/while/body/eval_jaxpr/reduce_max | solution.py:681
  83.1 9.3 %multiply_reduce_fusion.15 = (f32[8,16,128]{2,1,0:T(8,128)S(1)}, f32[8,128,16]{1,2,0:T(8,128)S(1)}, f32[8,128,16,128]{1,3,2,0:T(8,128)S(1)}) fusion(f32[8,128]{1,0:T(8,128)S(1)} %broadcast_multiply_fusion.12, f32[16,128]{1,0:T(8,128)S(1)} %broadcast_multiply_fusion.13, bf16[16,128,1280]{2,1,0:T(8,128)(2,1)} %get-tuple-element.620, s32[]{:T(128)S(6)} %select_n.110), kind=kOutput, calls=%fused_computation.67.clone.1 | convolution fusion | flops 5377064960 | bytes 16396292 | tf_op jit(solution)/shard_map/cond/branch_1_fun/while/body/eval_jaxpr/bie,qje->bqij/dot_general | solution.py:677
  92.7 3.4 %fusion.41 = f32[8,16,128]{2,1,0:T(8,128)S(1)} fusion(f32[8,128,16,128]{1,3,2,0:T(8,128)S(1)} %get-tuple-element.563, f32[8,16]{1,0:T(8,128)S(1)} %broadcast_divide_fusion.9, f32[8,16,128]{2,1,0:T(8,128)S(1)} %get-tuple-element.568, f32[8,16,128]{2,1,0:T(8,128)S(1)} %get-tuple-element.569, pred[16,128]{1,0:T(8,128)(4,1)S(1)} %broadcast_compare_fusion.6), kind=kLoop, calls=%fused_computation.66.clone.1 | loop fusion | flops 12566528 | bytes 8587776 | tf_op jit(solution)/shard_map/cond/branch_1_fun/while/body/eval_jaxpr/reduce_max | solution.py:681
  96.9 82.8 %all-to-all-done.got_ref.refs_0_ = bf16[256,16,1280]{2,1,0:T(8,128)(2,1)} async-done(((bf16[256,16,1280]{2,1,0:T(8,128)(2,1)}), bf16[256,16,1280]{2,1,0:T(8,128)(2,1)}, u32[]{:S(2)}, u32[]{:S(2)}) %all-to-all-start) | async-done | bytes 10485792 | tf_op jit(solution)/shard_map/cond/branch_1_fun/all_to_all | solution.py:694
  179.7 8.0 %pack2.3 = bf16[128,16,1280]{2,1,0:T(8,128)(2,1)} custom-call(s32[16,128]{1,0:T(8,128)S(1)} %get-tuple-element.249.tab_ref, bf16[128,16,1280]{2,1,0:T(8,128)(2,1)} %bitcast.163, bf16[128,16,1280]{2,1,0:T(8,128)(2,1)} %get-tuple-element.251.mate_ref, bf16[256,16,1280]{2,1,0:T(8,128)(2,1)} %all-to-all-done.got_ref.refs_0_), custom_call_target="tpu_custom_call" | custom-call | tf_op jit(solution)/shard_map/cond/branch_1_fun/pack2/pallas_call | solution.py:329
  187.7 9.2 %all-to-all-start.1 = ((bf16[128,16,1280]{2,1,0:T(8,128)(2,1)}), bf16[128,16,1280]{2,1,0:T(8,128)(2,1)}, u32[]{:S(2)}, u32[]{:S(2)}) async-start(bf16[128,16,1280]{2,1,0:T(8,128)(2,1)} %pack2.3), calls=%async_computation.1 | async-start | bytes 10485760 | tf_op jit(solution)/shard_map/cond/branch_1_fun/all_to_all | solution.py:694
  196.9 7.2 %hand.3 = bf16[64,16,1280]{2,1,0:T(8,128)(2,1)S(1)} custom-call(s32[16,128]{1,0:T(8,128)S(1)} %get-tuple-element.249.tab_ref, bf16[256,16,1280]{2,1,0:T(8,128)(2,1)} %all-to-all-done.got_ref.refs_0_), custom_call_target="tpu_custom_call" | custom-call | tf_op jit(solution)/shard_map/cond/branch_1_fun/hand/pallas_call | solution.py:368
  205.0 7.9 %place.5.loc_ref = s32[1408]{0:T(1024)} custom-call(s32[1]{0:T(128)} %get-tuple-element.258.me_ref, s32[16,128]{1,0:T(8,128)S(1)} %get-tuple-element.249.tab_ref), custom_call_target="tpu_custom_call" | custom-call | tf_op jit(solution)/shard_map/cond/branch_1_fun/place/pallas_call | solution.py:467
  213.0 2.5 copy-done
  216.1 9.5 %near_early.3 = (f32[16,128]{1,0:T(8,128)S(1)}, f32[128,128]{1,0:T(8,128)S(1)}) custom-call(s32[16,128]{1,0:T(8,128)S(1)} %get-tuple-element.249.tab_ref, s32[1408]{0:T(1024)S(1)} %copy-done.2, s32[16]{0:T(128)S(1)} %copy-done.10, bf16[16,1280,128]{2,1,0:T(8,128)(2,1)S(1)} %bitcast.152, f32[16,128]{1,0:T(8,128)S(1)} %broadcast_in_dim.221.best0_ref, ...), custom_call_target="tpu_custom_call" | custom-call | tf_op jit(solution)/shard_map/cond/branch_1_fun/near_early/pallas_call | solution.py:644
  225.6 35.3 %all-to-all-done.1.refs_1_ = bf16[128,16,1280]{2,1,0:T(8,128)(2,1)} async-done(((bf16[128,16,1280]{2,1,0:T(8,128)(2,1)}), bf16[128,16,1280]{2,1,0:T(8,128)(2,1)}, u32[]{:S(2)}, u32[]{:S(2)}) %all-to-all-start.1) | async-done | bytes 5242912 | tf_op jit(solution)/shard_map/cond/branch_1_fun/all_to_all | solution.py:694
  261.0 2.5 copy-done.1
  263.5 14.4 %near_late.3 = (f32[16,128]{1,0:T(8,128)S(1)}, f32[128,128]{1,0:T(8,128)}) custom-call(s32[16,128]{1,0:T(8,128)S(1)} %get-tuple-element.249.tab_ref, s32[1408]{0:T(1024)S(1)} %copy-done.3, s32[16]{0:T(128)S(1)} %copy-done.10, bf16[16,1280,128]{2,1,0:T(8,128)(2,1)S(1)} %bitcast.153, f32[16,128]{1,0:T(8,128)S(1)} %get-tuple-element.266.best0_ref, ...), custom_call_target="tpu_custom_call" | custom-call | tf_op jit(solution)/shard_map/cond/branch_1_fun/near_late/pallas_call | solution.py:644
  277.9 8.9 %all-to-all-start.2 = ((f32[128,1,128]{2,1,0:T(1,128)}), f32[128,1,128]{2,1,0:T(1,128)S(1)}, u32[]{:S(2)}, u32[]{:S(2)}) async-start(f32[128,1,128]{2,1,0:T(1,128)} %bitcast.41), calls=%async_computation.2 | async-start | bytes 131072 | tf_op jit(solution)/shard_map/cond/branch_1_fun/all_to_all | solution.py:694
  286.8 9.6 %all-to-all-done.2 = f32[128,1,128]{2,1,0:T(1,128)S(1)} async-done(((f32[128,1,128]{2,1,0:T(1,128)}), f32[128,1,128]{2,1,0:T(1,128)S(1)}, u32[]{:S(2)}, u32[]{:S(2)}) %all-to-all-start.2) | async-done | bytes 65568 | tf_op jit(solution)/shard_map/cond/branch_1_fun/all_to_all | solution.py:694
  (53 shorter events, 10.0 us)
Async XLA Ops:
  0.6 35.3 %collective-permute-start.2 = (bf16[128,16,1280]{2,1,0:T(8,128)(2,1)}, bf16[128,16,1280]{2,1,0:T(8,128)(2,1)}, u32[]{:S(2)}, u32[]{:S(2)}) collective-permute-start(bf16[128,16,1280]{2,1,0:T(8,128)(2,1)} %bitcast.158), channel_id=1, source_target_pairs={{0,1},{1,0},{2,3},{3,2},{4,5},{5,4},{6,7},{7,6},{8,9},{9,8},{10,11... | collective-permute-start | bytes 15728648 | tf_op jit(solution)/shard_map/ppermute | solution.py:698
  3.6 20.7 %all-to-all-start.8 = ((s32[128,1,384]{2,1,0:T(1,128)}), s32[128,1,384]{2,1,0:T(1,128)S(1)}, u32[]{:S(2)}, u32[]{:S(2)}) async-start(s32[128,1,384]{2,1,0:T(1,128)} %broadcast_in_dim.231), calls=%async_computation.8 | async-start | bytes 393216 | tf_op jit(solution)/shard_map/all_to_all | solution.py:694
  46.3 133.4 %all-to-all-start = ((bf16[256,16,1280]{2,1,0:T(8,128)(2,1)}), bf16[256,16,1280]{2,1,0:T(8,128)(2,1)}, u32[]{:S(2)}, u32[]{:S(2)}) async-start(bf16[256,16,1280]{2,1,0:T(8,128)(2,1)} %pack1.3), calls=%async_computation | async-start | bytes 20971520 | tf_op jit(solution)/shard_map/cond/branch_1_fun/all_to_all | solution.py:694
  96.9 128.7 %copy-start.15 = (f32[2,8,128]{2,1,0:T(8,128)}, f32[2,8,128]{2,1,0:T(8,128)S(1)}, u32[]{:S(2)}) copy-start(f32[2,8,128]{2,1,0:T(8,128)S(1)} %get-tuple-element.254) | copy-start | bytes 24580 | tf_op jit(solution)/shard_map/cond
  187.7 73.3 %all-to-all-start.1 = ((bf16[128,16,1280]{2,1,0:T(8,128)(2,1)}), bf16[128,16,1280]{2,1,0:T(8,128)(2,1)}, u32[]{:S(2)}, u32[]{:S(2)}) async-start(bf16[128,16,1280]{2,1,0:T(8,128)(2,1)} %pack2.3), calls=%async_computation.1 | async-start | bytes 10485760 | tf_op jit(solution)/shard_map/cond/branch_1_fun/all_to_all | solution.py:694
  196.9 16.1 %copy-start.10 = (s32[16]{0:T(128)S(1)}, s32[16]{0:T(128)}, u32[]{:S(2)}) copy-start(s32[16]{0:T(128)} %get-tuple-element.259.lens_ref) | copy-start | bytes 196 | tf_op jit(solution)/shard_map/cond
  204.1 56.9 %collective-permute-start = (bf16[64,16,1280]{2,1,0:T(8,128)(2,1)S(1)}, bf16[64,16,1280]{2,1,0:T(8,128)(2,1)}, u32[]{:S(2)}, u32[]{:S(2)}) collective-permute-start(bf16[64,16,1280]{2,1,0:T(8,128)(2,1)S(1)} %hand.3), channel_id=1, source_target_pairs={{0,1},{1,0},{2,3},{3,2},{4,5},{5,4},{6,7},{7,6},{8,9},{9,8},{10,11... | collective-permute-start | bytes 7864328 | tf_op jit(solution)/shard_map/cond/branch_1_fun/ppermute | solution.py:698
  212.9 48.1 %copy-start.3 = (s32[1408]{0:T(1024)S(1)}, s32[1408]{0:T(1024)}, u32[]{:S(2)}) copy-start(s32[1408]{0:T(1024)} %place.5.loc_ref) | copy-start | bytes 16900 | tf_op jit(solution)/shard_map/cond
  213.0 2.5 copy-start
  215.4 0.7 copy-start.2
  261.0 2.5 copy-start.1
  277.9 18.5 %all-to-all-start.2 = ((f32[128,1,128]{2,1,0:T(1,128)}), f32[128,1,128]{2,1,0:T(1,128)S(1)}, u32[]{:S(2)}, u32[]{:S(2)}) async-start(f32[128,1,128]{2,1,0:T(1,128)} %bitcast.41), calls=%async_computation.2 | async-start | bytes 131072 | tf_op jit(solution)/shard_map/cond/branch_1_fun/all_to_all | solution.py:694
  296.8 0.6 copy-start.11

commit v3 on v2

--- a/solution.py
+++ b/solution.py
@@ -226,9 +226,8 @@
         at = tab_ref[R_SENDM, (code >> 3) & (N - 1)] * GR + (code & 7)
         return pltpu.make_async_copy(mate_ref.at[at], buf.at[j * C1 + k], in_sem.at[part])
 
-    for part in range(parts):
-
-        def start(j, count, part=part):
+    def fill(part):
+        def start(j, count):
             for k, code in codes(j):
                 is_mate = (code >> 11) & 1
 
@@ -244,14 +243,23 @@
                 count = count + is_mate
             return count
 
-        count = lax.fori_loop(part * each, (part + 1) * each, start, jnp.int32(0), unroll=4)
-
-        def finish(i, _, part=part):
+        return lax.fori_loop(part * each, (part + 1) * each, start, jnp.int32(0), unroll=4)
+
+    def send(part, count):
+        def finish(i, _):
             pltpu.make_async_copy(mate_ref.at[0], buf.at[0], in_sem.at[part]).wait()
             return 0
 
         lax.fori_loop(0, count, finish, 0)
         pltpu.make_async_copy(piece(buf, part), piece(out_ref, part), out_sem.at[part]).start()
+
+    counts = []
+    for part in range(parts):
+        counts.append(fill(part))
+        if part >= 2:
+            send(part - 2, counts[part - 2])
+    for part in range(parts - 2, parts):
+        send(part, counts[part])
     for part in range(parts):
         pltpu.make_async_copy(piece(buf, part), piece(out_ref, part), out_sem.at[part]).wait()
 
@@ -283,9 +291,10 @@
     each = N // parts
 
     def fetch(part):
-        def body(j, _):
+        def body(j, count):
             to = part * each + j
             w = tab_ref[R_F2ROW, to]
+            filled = c2 - (w & 3)
             for k in range(c2):
                 code = w >> (2 + 14 * k)
                 kind = code & 3
@@ -293,31 +302,35 @@
                 slot = ((code >> 6) & (N - 1)) * C1 + ((code >> 5) & 1)
                 dst = buf.at[to * c2 + k]
 
-                @pl.when(kind == 0)
+                @pl.when((k < filled) & (kind == 0))
                 def _():
                     src = own_ref.at[tab_ref[R_SEND, to] * GR + g]
                     pltpu.make_async_copy(src, dst, in_sem.at[part]).start()
 
-                @pl.when(kind == 1)
+                @pl.when((k < filled) & (kind == 1))
                 def _():
                     src = mate_ref.at[tab_ref[R_SENDM, to] * GR + g]
                     pltpu.make_async_copy(src, dst, in_sem.at[part]).start()
 
-                @pl.when(kind >= 2)
+                @pl.when((k < filled) & (kind >= 2))
                 def _():
                     pltpu.make_async_copy(got_ref.at[slot], dst, in_sem.at[part]).start()
 
-            return 0
-
-        lax.fori_loop(0, each, body, 0, unroll=4)
+            return count + filled
+
+        return lax.fori_loop(0, each, body, jnp.int32(0), unroll=4)
 
     def piece(ref, part):
         return ref.at[pl.ds(part * each * c2, each * c2)]
 
+    counts = [fetch(part) for part in range(parts)]
     for part in range(parts):
-        fetch(part)
-    for part in range(parts):
-        pltpu.make_async_copy(piece(buf, part), piece(buf, part), in_sem.at[part]).wait()
+
+        def arrive(i, _, part=part):
+            pltpu.make_async_copy(own_ref.at[0], buf.at[0], in_sem.at[part]).wait()
+            return 0
+
+        lax.fori_loop(0, counts[part], arrive, 0)
         pltpu.make_async_copy(piece(buf, part), piece(out_ref, part), out_sem.at[part]).start()
     for part in range(parts):
         pltpu.make_async_copy(piece(buf, part), piece(out_ref, part), out_sem.at[part]).wait()
@@ -401,9 +414,8 @@
 
     def clear(s, _):
         loc_ref[late_of + s] = 0
-        if c2 == 0:
-            for g in range(GR):
-                loc_ref[s * GR + g] = s * GR + g
+        for g in range(GR):
+            loc_ref[s * GR + g] = s * GR + g if c2 == 0 else 0
         return 0
 
     lax.fori_loop(0, N, clear, 0)
@@ -583,8 +595,16 @@
     )(tab, loc, lens, own_t, best, ret, *gots)
 
 
-def near_kernel(late, ends, tab_ref, loc_ref, lens_ref, own_t_ref, best0_ref, ret0_ref, *refs):
-    gots, (best_ref, ret_ref, buf) = refs[: len(ends)], refs[len(ends) :]
+def near_kernel(late, tab_ref, loc_ref, lens_ref, own_t_hbm, best0_ref, ret0_ref, *refs):
+    gots, (best_ref, ret_ref, own_t_ref, all_ref, buf, sem) = refs[:-6], refs[-6:]
+    copies = [pltpu.make_async_copy(own_t_hbm, own_t_ref, sem.at[0])]
+    start = 0
+    for i, got in enumerate(gots):
+        end = start + got.shape[0]
+        copies.append(pltpu.make_async_copy(got, all_ref.at[pl.ds(start, end - start)], sem.at[i + 1]))
+        start = end
+    for copy in copies:
+        copy.start()
     width = own_t_ref.shape[1]
     best_ref[...] = best0_ref[...]
     ret_ref[...] = ret0_ref[...]
@@ -596,21 +616,11 @@
 
     def gather(i, u):
         s = sender(i)
-        granules = tab_ref[R_GIN, s]
         for g in range(GR):
-
-            @pl.when(g < granules)
-            def _():
-                at = loc_ref[s * GR + g]
-                start = 0
-                for got_ref, end in zip(gots, ends):
-
-                    @pl.when((at >= start) & (at < end))
-                    def _(got_ref=got_ref, start=start):
-                        buf[u, g] = got_ref[at - start]
-
-                    start = end
-
+            buf[u, g] = all_ref[loc_ref[s * GR + g]]
+
+    for copy in copies:
+        copy.wait()
     row = lax.broadcasted_iota(jnp.int32, (N, N), 0)
     col = lax.broadcasted_iota(jnp.int32, (N, N), 1)
 
@@ -638,19 +648,25 @@
 
 
 def near(late, tab, loc, lens, own_t, best, ret, *gots):
-    ends = []
-    for got in gots:
-        ends.append((ends[-1] if ends else 0) + got.shape[0])
+    total = sum(got.shape[0] for got in gots)
+    far = [pltpu.with_memory_space_constraint(x, pltpu.HBM) for x in (own_t,) + gots]
     return pl.pallas_call(
-        functools.partial(near_kernel, late, tuple(ends)),
+        functools.partial(near_kernel, late),
         out_shape=[jax.ShapeDtypeStruct(x.shape, x.dtype) for x in (best, ret)],
         in_specs=[pl.BlockSpec(memory_space=pltpu.SMEM)] * 3
-        + [pl.BlockSpec(memory_space=pltpu.VMEM)] * (3 + len(gots)),
+        + [pl.BlockSpec(memory_space=pltpu.HBM)]
+        + [pl.BlockSpec(memory_space=pltpu.VMEM)] * 2
+        + [pl.BlockSpec(memory_space=pltpu.HBM)] * len(gots),
         out_specs=[pl.BlockSpec(memory_space=pltpu.VMEM)] * 2,
-        scratch_shapes=[pltpu.VMEM((GROUP, GR, 16, own_t.shape[1]), own_t.dtype)],
-        compiler_params=pltpu.CompilerParams(vmem_limit_bytes=40 << 20),
+        scratch_shapes=[
+            pltpu.VMEM(own_t.shape, own_t.dtype),
+            pltpu.VMEM((total,) + gots[0].shape[1:], own_t.dtype),
+            pltpu.VMEM((GROUP, GR, 16, own_t.shape[1]), own_t.dtype),
+            pltpu.SemaphoreType.DMA((1 + len(gots),)),
+        ],
+        compiler_params=pltpu.CompilerParams(vmem_limit_bytes=44 << 20),
         name="near_late" if late else "near_early",
-    )(tab, loc, lens, own_t, best, ret, *gots)
+    )(tab, loc, lens, far[0], best, ret, *far[1:])
 
 
 def centred(score_matrix, row_validity_mask, col_mask):

time: 299 us -> 285 us (0.953)
  starting transfers between devices: 39.6 us -> 32.1 us
  local copies, waits for them, and re-layouts: 16.2 us -> 11.2 us
  Pallas kernels: 68.1 us -> 64.2 us
    all_to_all x4, starting transfers between devices: 37.2 us -> 30.5 us  [exchange(): return lax.all_to_all(x, 'shard', split_axis=0, concat_axis=0, tiled=True)]
    cond x12 -> x8, local copies, waits for them, and re-layouts: 5.68 us -> 0.71 us
  transfers between devices with their start and end apart: 6 -> 6, of which waited for: 4 -> 4; matrix products, arithmetic and copies ran while one was open for 13% -> 14% of each run, Pallas kernels for 12% -> 13%
where the time goes in v3:
time: 285 us; the launch traced here: 282 us
  waiting for transfers between devices  139 us (49%)
  Pallas kernels  64.2 us (23%)
  starting transfers between devices  32.1 us (11%)
  matrix products  19.2 us (7%)
  local copies, waits for them, and re-layouts  11.2 us (4%)
  other arithmetic  11 us (4%)
  loops' own time  4.46 us (2%)
    all_to_all x4, waiting for transfers between devices, exchange(): return lax.all_to_all(x, 'shard', split_axis=0, concat_axis=0, tiled=True)  139 us
    all_to_all x4, starting transfers between devices, exchange(): return lax.all_to_all(x, 'shard', split_axis=0, concat_axis=0, tiled=True)  30.5 us
    pallas_call x2, Pallas kernels, near(): pl.pallas_call(functools.partial(near_kernel, late), out_shape=[jax.Shape...  24.4 us
    dot_general x2, matrix products, one_block(): jnp.einsum('bie,qje->bqij', block_rows, embeddings, preferred_element_typ...  19.2 us
    pallas_call x1, Pallas kernels, route(): pl.pallas_call(functools.partial(route_kernel, c2), out_shape=[jax.ShapeD...  9.31 us
    pallas_call x1, Pallas kernels, pack1(): pl.pallas_call(pack1_kernel, out_shape=pltpu.HBM(shape, own.dtype), in_sp...  8.97 us
    pallas_call x1, Pallas kernels, place(): pl.pallas_call(functools.partial(place_kernel, c2), out_shape=jax.ShapeDt...  8.54 us
    another operation x1, local copies, waits for them, and re-layouts  7.88 us
  transfers between devices with their start and end apart: 6, of which 4 were waited for; matrix products, arithmetic and copies ran while one was open for 14% of the time, Pallas kernels for 13%

profile of v3, /device:TPU:1, one launch (start us, length us, event | category | flops | bytes accessed | tf_op | source)
XLA Modules:
  0.0 282.0 jit_solution(13606196434376962546)
XLA Ops:
  0.6 1.5 collective-permute-start.2
  2.8 0.8 broadcast_in_dim.231
  3.6 10.2 %all-to-all-start.8 = ((s32[128,1,384]{2,1,0:T(1,128)}), s32[128,1,384]{2,1,0:T(1,128)S(1)}, u32[]{:S(2)}, u32[]{:S(2)}) async-start(s32[128,1,384]{2,1,0:T(1,128)} %broadcast_in_dim.231), calls=%async_computation.8 | async-start | bytes 393216 | tf_op jit(solution)/shard_map/all_to_all | solution.py:710
  14.6 9.8 %all-to-all-done.8 = s32[128,1,384]{2,1,0:T(1,128)S(1)} async-done(((s32[128,1,384]{2,1,0:T(1,128)}), s32[128,1,384]{2,1,0:T(1,128)S(1)}, u32[]{:S(2)}, u32[]{:S(2)}) %all-to-all-start.8) | async-done | bytes 196640 | tf_op jit(solution)/shard_map/all_to_all | solution.py:710
  24.4 9.3 %route1.1 = (s32[16,128]{1,0:T(8,128)S(1)}, s32[1]{0:T(128)}) custom-call(s32[1]{0:T(128)} %bitcast.43.me_ref, s32[128,384]{1,0:T(8,128)S(1)} %bitcast.164), custom_call_target="tpu_custom_call" | custom-call | tf_op jit(solution)/shard_map/route1/pallas_call | solution.py:203
  34.4 247.1 %conditional.2 = ((f32[16,128]{1,0:T(8,128)}, f32[16,128]{1,0:T(8,128)S(1)})) conditional(s32[]{:T(128)} %bitcast.45, (s32[1]{0:T(128)}, s32[128,384]{1,0:T(8,128)S(1)}, f32[16,128]{1,0:T(8,128)S(1)}, bf16[16,128,1280]{2,1,0:T(8,128)(2,1)}, bf16[128,16,1280]{2,1,0:T(8,128)(2,1)}, /*index=5*/s32[16]{0:T(128)}, ...), branch_computations={%region_0.23_spmd, %region_23.34_spmd} | conditional | flops 5390275584 | bytes 172617312 | solution.py:768
  34.6 9.0 %pack1.3 = bf16[256,16,1280]{2,1,0:T(8,128)(2,1)} custom-call(s32[16,128]{1,0:T(8,128)S(1)} %get-tuple-element.249.tab_ref, bf16[128,16,1280]{2,1,0:T(8,128)(2,1)} %bitcast.160, bf16[128,16,1280]{2,1,0:T(8,128)(2,1)} %get-tuple-element.251.mate_ref), custom_call_target="tpu_custom_call" | custom-call | tf_op jit(solution)/shard_map/cond/branch_1_fun/pack1/pallas_call | solution.py:270
  43.6 5.3 %all-to-all-start = ((bf16[256,16,1280]{2,1,0:T(8,128)(2,1)}), bf16[256,16,1280]{2,1,0:T(8,128)(2,1)}, u32[]{:S(2)}, u32[]{:S(2)}) async-start(bf16[256,16,1280]{2,1,0:T(8,128)(2,1)} %pack1.3), calls=%async_computation | async-start | bytes 20971520 | tf_op jit(solution)/shard_map/cond/branch_1_fun/all_to_all | solution.py:710
  48.9 7.9 %copy.30 = bf16[16,128,1280]{1,2,0:T(8,128)(2,1)} copy(bf16[16,128,1280]{2,1,0:T(8,128)(2,1)} %get-tuple-element.602) | data formatting | bytes 10485760 | tf_op jit(solution)/shard_map
  56.9 33.6 %while.32 = (s32[]{:T(128)}, f32[2,8,128]{2,1,0:T(8,128)S(1)}, s32[2]{0:T(128)S(1)}, f32[16,128]{1,0:T(8,128)S(1)}, bf16[16,128,1280]{2,1,0:T(8,128)(2,1)}, /*in...) while((s32[]{:T(128)}, f32[2,8,128]{2,1,0:T(8,128)S(1)}, s32[2]{0:T(128)S(1)}, ...), condition=%wide.region_32.32_spmd, body=%wide.region_25.31_spmd.sunk | while | flops 5389736960 | bytes 25377404 | solution.py:706
  59.6 10.0 %multiply_reduce_fusion.15 = (f32[8,16,128]{2,1,0:T(8,128)S(1)}, f32[8,128,16]{1,2,0:T(8,128)S(1)}, f32[8,128,16,128]{1,3,2,0:T(8,128)S(1)}) fusion(f32[8,128]{1,0:T(8,128)S(1)} %broadcast_multiply_fusion.12, f32[16,128]{1,0:T(8,128)S(1)} %broadcast_multiply_fusion.13, bf16[16,128,1280]{2,1,0:T(8,128)(2,1)} %get-tuple-element.620, s32[]{:T(128)S(6)} %select_n.110), kind=kOutput, calls=%fused_computation.67.clone.1 | convolution fusion | flops 5377064960 | bytes 16396292 | tf_op jit(solution)/shard_map/cond/branch_1_fun/while/body/eval_jaxpr/bie,qje->bqij/dot_general | solution.py:693
  69.8 3.4 %fusion.41 = f32[8,16,128]{2,1,0:T(8,128)S(1)} fusion(f32[8,128,16,128]{1,3,2,0:T(8,128)S(1)} %get-tuple-element.563, f32[8,16]{1,0:T(8,128)S(1)} %broadcast_divide_fusion.9, f32[8,16,128]{2,1,0:T(8,128)S(1)} %get-tuple-element.568, f32[8,16,128]{2,1,0:T(8,128)S(1)} %get-tuple-element.569, pred[16,128]{1,0:T(8,128)(4,1)S(1)} %broadcast_compare_fusion.6), kind=kLoop, calls=%fused_computation.66.clone.1 | loop fusion | flops 12566528 | bytes 8587776 | tf_op jit(solution)/shard_map/cond/branch_1_fun/while/body/eval_jaxpr/reduce_max | solution.py:697
  76.7 9.3 %multiply_reduce_fusion.15 = (f32[8,16,128]{2,1,0:T(8,128)S(1)}, f32[8,128,16]{1,2,0:T(8,128)S(1)}, f32[8,128,16,128]{1,3,2,0:T(8,128)S(1)}) fusion(f32[8,128]{1,0:T(8,128)S(1)} %broadcast_multiply_fusion.12, f32[16,128]{1,0:T(8,128)S(1)} %broadcast_multiply_fusion.13, bf16[16,128,1280]{2,1,0:T(8,128)(2,1)} %get-tuple-element.620, s32[]{:T(128)S(6)} %select_n.110), kind=kOutput, calls=%fused_computation.67.clone.1 | convolution fusion | flops 5377064960 | bytes 16396292 | tf_op jit(solution)/shard_map/cond/branch_1_fun/while/body/eval_jaxpr/bie,qje->bqij/dot_general | solution.py:693
  86.3 3.4 %fusion.41 = f32[8,16,128]{2,1,0:T(8,128)S(1)} fusion(f32[8,128,16,128]{1,3,2,0:T(8,128)S(1)} %get-tuple-element.563, f32[8,16]{1,0:T(8,128)S(1)} %broadcast_divide_fusion.9, f32[8,16,128]{2,1,0:T(8,128)S(1)} %get-tuple-element.568, f32[8,16,128]{2,1,0:T(8,128)S(1)} %get-tuple-element.569, pred[16,128]{1,0:T(8,128)(4,1)S(1)} %broadcast_compare_fusion.6), kind=kLoop, calls=%fused_computation.66.clone.1 | loop fusion | flops 12566528 | bytes 8587776 | tf_op jit(solution)/shard_map/cond/branch_1_fun/while/body/eval_jaxpr/reduce_max | solution.py:697
  90.5 82.8 %all-to-all-done.got_ref.refs_0_ = bf16[256,16,1280]{2,1,0:T(8,128)(2,1)} async-done(((bf16[256,16,1280]{2,1,0:T(8,128)(2,1)}), bf16[256,16,1280]{2,1,0:T(8,128)(2,1)}, u32[]{:S(2)}, u32[]{:S(2)}) %all-to-all-start) | async-done | bytes 10485792 | tf_op jit(solution)/shard_map/cond/branch_1_fun/all_to_all | solution.py:710
  173.3 5.3 %pack2.3 = bf16[128,16,1280]{2,1,0:T(8,128)(2,1)} custom-call(s32[16,128]{1,0:T(8,128)S(1)} %get-tuple-element.249.tab_ref, bf16[128,16,1280]{2,1,0:T(8,128)(2,1)} %bitcast.161, bf16[128,16,1280]{2,1,0:T(8,128)(2,1)} %get-tuple-element.251.mate_ref, bf16[256,16,1280]{2,1,0:T(8,128)(2,1)} %all-to-all-done.got_ref.refs_0_), custom_call_target="tpu_custom_call" | custom-call | tf_op jit(solution)/shard_map/cond/branch_1_fun/pack2/pallas_call | solution.py:342
  178.6 9.1 %all-to-all-start.1 = ((bf16[128,16,1280]{2,1,0:T(8,128)(2,1)}), bf16[128,16,1280]{2,1,0:T(8,128)(2,1)}, u32[]{:S(2)}, u32[]{:S(2)}) async-start(bf16[128,16,1280]{2,1,0:T(8,128)(2,1)} %pack2.3), calls=%async_computation.1 | async-start | bytes 10485760 | tf_op jit(solution)/shard_map/cond/branch_1_fun/all_to_all | solution.py:710
  187.8 7.7 %hand.3 = bf16[64,16,1280]{2,1,0:T(8,128)(2,1)S(1)} custom-call(s32[16,128]{1,0:T(8,128)S(1)} %get-tuple-element.249.tab_ref, bf16[256,16,1280]{2,1,0:T(8,128)(2,1)} %all-to-all-done.got_ref.refs_0_), custom_call_target="tpu_custom_call" | custom-call | tf_op jit(solution)/shard_map/cond/branch_1_fun/hand/pallas_call | solution.py:381
  195.5 8.5 %place.5.loc_ref = s32[1408]{0:T(1024)} custom-call(s32[1]{0:T(128)} %get-tuple-element.258.me_ref, s32[16,128]{1,0:T(8,128)S(1)} %get-tuple-element.249.tab_ref), custom_call_target="tpu_custom_call" | custom-call | tf_op jit(solution)/shard_map/cond/branch_1_fun/place/pallas_call | solution.py:479
  204.8 10.7 %near_early.3 = (f32[16,128]{1,0:T(8,128)S(1)}, f32[128,128]{1,0:T(8,128)S(1)}) custom-call(s32[16,128]{1,0:T(8,128)S(1)} %get-tuple-element.249.tab_ref, s32[1408]{0:T(1024)S(1)} %copy-done, s32[16]{0:T(128)S(1)} %copy-done.8, bf16[16,1280,128]{2,1,0:T(8,128)(2,1)} %bitcast.162, f32[16,128]{1,0:T(8,128)S(1)} %broadcast_in_dim.221.best0_ref, ...), custom_call_target="tpu_custom_call" | custom-call | tf_op jit(solution)/shard_map/cond/branch_1_fun/near_early/pallas_call | solution.py:653
  215.6 36.3 %all-to-all-done.1.refs_1_ = bf16[128,16,1280]{2,1,0:T(8,128)(2,1)} async-done(((bf16[128,16,1280]{2,1,0:T(8,128)(2,1)}), bf16[128,16,1280]{2,1,0:T(8,128)(2,1)}, u32[]{:S(2)}, u32[]{:S(2)}) %all-to-all-start.1) | async-done | bytes 5242912 | tf_op jit(solution)/shard_map/cond/branch_1_fun/all_to_all | solution.py:710
  251.9 13.7 %near_late.3 = (f32[16,128]{1,0:T(8,128)S(1)}, f32[128,128]{1,0:T(8,128)}) custom-call(s32[16,128]{1,0:T(8,128)S(1)} %get-tuple-element.249.tab_ref, s32[1408]{0:T(1024)S(1)} %copy-done.1, s32[16]{0:T(128)S(1)} %copy-done.8, bf16[16,1280,128]{2,1,0:T(8,128)(2,1)} %bitcast.163, f32[16,128]{1,0:T(8,128)S(1)} %get-tuple-element.266.best0_ref, ...), custom_call_target="tpu_custom_call" | custom-call | tf_op jit(solution)/shard_map/cond/branch_1_fun/near_late/pallas_call | solution.py:653
  265.6 5.9 %all-to-all-start.2 = ((f32[128,1,128]{2,1,0:T(1,128)}), f32[128,1,128]{2,1,0:T(1,128)S(1)}, u32[]{:S(2)}, u32[]{:S(2)}) async-start(f32[128,1,128]{2,1,0:T(1,128)} %bitcast.41), calls=%async_computation.2 | async-start | bytes 131072 | tf_op jit(solution)/shard_map/cond/branch_1_fun/all_to_all | solution.py:710
  271.5 9.6 %all-to-all-done.2 = f32[128,1,128]{2,1,0:T(1,128)S(1)} async-done(((f32[128,1,128]{2,1,0:T(1,128)}), f32[128,1,128]{2,1,0:T(1,128)S(1)}, u32[]{:S(2)}, u32[]{:S(2)}) %all-to-all-start.2) | async-done | bytes 65568 | tf_op jit(solution)/shard_map/cond/branch_1_fun/all_to_all | solution.py:710
  (49 shorter events, 6.9 us)
Async XLA Ops:
  0.6 33.7 %collective-permute-start.2 = (bf16[128,16,1280]{2,1,0:T(8,128)(2,1)}, bf16[128,16,1280]{2,1,0:T(8,128)(2,1)}, u32[]{:S(2)}, u32[]{:S(2)}) collective-permute-start(bf16[128,16,1280]{2,1,0:T(8,128)(2,1)} %bitcast.156), channel_id=1, source_target_pairs={{0,1},{1,0},{2,3},{3,2},{4,5},{5,4},{6,7},{7,6},{8,9},{9,8},{10,11... | collective-permute-start | bytes 15728648 | tf_op jit(solution)/shard_map/ppermute | solution.py:714
  3.6 20.7 %all-to-all-start.8 = ((s32[128,1,384]{2,1,0:T(1,128)}), s32[128,1,384]{2,1,0:T(1,128)S(1)}, u32[]{:S(2)}, u32[]{:S(2)}) async-start(s32[128,1,384]{2,1,0:T(1,128)} %broadcast_in_dim.231), calls=%async_computation.8 | async-start | bytes 393216 | tf_op jit(solution)/shard_map/all_to_all | solution.py:710
  43.6 129.8 %all-to-all-start = ((bf16[256,16,1280]{2,1,0:T(8,128)(2,1)}), bf16[256,16,1280]{2,1,0:T(8,128)(2,1)}, u32[]{:S(2)}, u32[]{:S(2)}) async-start(bf16[256,16,1280]{2,1,0:T(8,128)(2,1)} %pack1.3), calls=%async_computation | async-start | bytes 20971520 | tf_op jit(solution)/shard_map/cond/branch_1_fun/all_to_all | solution.py:710
  90.5 125.1 %copy-start.13 = (f32[2,8,128]{2,1,0:T(8,128)}, f32[2,8,128]{2,1,0:T(8,128)S(1)}, u32[]{:S(2)}) copy-start(f32[2,8,128]{2,1,0:T(8,128)S(1)} %get-tuple-element.254) | copy-start | bytes 24580 | tf_op jit(solution)/shard_map/cond
  178.6 73.2 %all-to-all-start.1 = ((bf16[128,16,1280]{2,1,0:T(8,128)(2,1)}), bf16[128,16,1280]{2,1,0:T(8,128)(2,1)}, u32[]{:S(2)}, u32[]{:S(2)}) async-start(bf16[128,16,1280]{2,1,0:T(8,128)(2,1)} %pack2.3), calls=%async_computation.1 | async-start | bytes 10485760 | tf_op jit(solution)/shard_map/cond/branch_1_fun/all_to_all | solution.py:710
  187.7 16.4 %copy-start.8 = (s32[16]{0:T(128)S(1)}, s32[16]{0:T(128)}, u32[]{:S(2)}) copy-start(s32[16]{0:T(128)} %get-tuple-element.259.lens_ref) | copy-start | bytes 196 | tf_op jit(solution)/shard_map/cond
  195.4 56.4 %collective-permute-start = (bf16[64,16,1280]{2,1,0:T(8,128)(2,1)S(1)}, bf16[64,16,1280]{2,1,0:T(8,128)(2,1)}, u32[]{:S(2)}, u32[]{:S(2)}) collective-permute-start(bf16[64,16,1280]{2,1,0:T(8,128)(2,1)S(1)} %hand.3), channel_id=1, source_target_pairs={{0,1},{1,0},{2,3},{3,2},{4,5},{5,4},{6,7},{7,6},{8,9},{9,8},{10,11... | collective-permute-start | bytes 7864328 | tf_op jit(solution)/shard_map/cond/branch_1_fun/ppermute | solution.py:714
  204.1 47.8 %copy-start.1 = (s32[1408]{0:T(1024)S(1)}, s32[1408]{0:T(1024)}, u32[]{:S(2)}) copy-start(s32[1408]{0:T(1024)} %place.5.loc_ref) | copy-start | bytes 16900 | tf_op jit(solution)/shard_map/cond
  204.1 0.7 copy-start
  265.6 15.5 %all-to-all-start.2 = ((f32[128,1,128]{2,1,0:T(1,128)}), f32[128,1,128]{2,1,0:T(1,128)S(1)}, u32[]{:S(2)}, u32[]{:S(2)}) async-start(f32[128,1,128]{2,1,0:T(1,128)} %bitcast.41), calls=%async_computation.2 | async-start | bytes 131072 | tf_op jit(solution)/shard_map/cond/branch_1_fun/all_to_all | solution.py:710
  281.4 0.6 copy-start.9

commit v4 on v3

--- a/solution.py
+++ b/solution.py
@@ -14,6 +14,7 @@
 K = 64
 DEPTH = 16
 GROUP = 4
+PIECES = 4
 TRIES = 6
 
 R_F1ROW, R_F1COL, R_F1COLM, R_F2ROW, R_F2COL, R_SEND, R_SENDM, R_GIN, R_LIN, R_OWN, R_GOUT = range(11)
@@ -211,55 +212,35 @@
     )(me, plan)
 
 
-def pack1_kernel(tab_ref, own_ref, mate_ref, out_ref, buf, in_sem, out_sem):
+def pack1_kernel(tab_ref, own_ref, mate_ref, out_ref, both, buf, in_sem, out_sem):
     parts = out_sem.shape[0]
     each = N // parts
+    held = own_ref.shape[0]
 
     def piece(ref, part):
         return ref.at[pl.ds(part * each * C1, each * C1)]
 
-    def codes(j):
-        w = tab_ref[R_F1ROW, j]
-        return [(k, w >> (2 + 12 * k)) for k in range(C1)]
-
-    def from_mate(part, j, k, code):
-        at = tab_ref[R_SENDM, (code >> 3) & (N - 1)] * GR + (code & 7)
-        return pltpu.make_async_copy(mate_ref.at[at], buf.at[j * C1 + k], in_sem.at[part])
-
-    def fill(part):
-        def start(j, count):
-            for k, code in codes(j):
-                is_mate = (code >> 11) & 1
-
-                @pl.when(is_mate == 1)
-                def _():
-                    from_mate(part, j, k, code).start()
-
-                @pl.when(is_mate == 0)
-                def _():
-                    at = tab_ref[R_SEND, (code >> 3) & (N - 1)] * GR + (code & 7)
-                    buf[j * C1 + k] = own_ref[at]
-
-                count = count + is_mate
-            return count
-
-        return lax.fori_loop(part * each, (part + 1) * each, start, jnp.int32(0), unroll=4)
-
-    def send(part, count):
-        def finish(i, _):
-            pltpu.make_async_copy(mate_ref.at[0], buf.at[0], in_sem.at[part]).wait()
+    copies = [
+        pltpu.make_async_copy(ref, both.at[pl.ds(i * held, held)], in_sem.at[i])
+        for i, ref in enumerate((own_ref, mate_ref))
+    ]
+    for copy in copies:
+        copy.start()
+    for copy in copies:
+        copy.wait()
+    for part in range(parts):
+
+        def body(j, _):
+            w = tab_ref[R_F1ROW, j]
+            for k in range(C1):
+                code = w >> (2 + 12 * k)
+                core = (code >> 11) & 1
+                protein = tab_ref[R_SEND + core, (code >> 3) & (N - 1)]
+                buf[j * C1 + k] = both[core * held + protein * GR + (code & 7)]
             return 0
 
-        lax.fori_loop(0, count, finish, 0)
+        lax.fori_loop(part * each, (part + 1) * each, body, 0, unroll=8)
         pltpu.make_async_copy(piece(buf, part), piece(out_ref, part), out_sem.at[part]).start()
-
-    counts = []
-    for part in range(parts):
-        counts.append(fill(part))
-        if part >= 2:
-            send(part - 2, counts[part - 2])
-    for part in range(parts - 2, parts):
-        send(part, counts[part])
     for part in range(parts):
         pltpu.make_async_copy(piece(buf, part), piece(out_ref, part), out_sem.at[part]).wait()
 
@@ -270,20 +251,17 @@
     return pl.pallas_call(
         pack1_kernel,
         out_shape=pltpu.HBM(shape, own.dtype),
-        in_specs=[
-            pl.BlockSpec(memory_space=pltpu.SMEM),
-            pl.BlockSpec(memory_space=pltpu.VMEM),
-            pl.BlockSpec(memory_space=pltpu.HBM),
-        ],
+        in_specs=[pl.BlockSpec(memory_space=pltpu.SMEM)] + [pl.BlockSpec(memory_space=pltpu.HBM)] * 2,
         out_specs=pl.BlockSpec(memory_space=pltpu.HBM),
         scratch_shapes=[
+            pltpu.VMEM((2 * own.shape[0],) + own.shape[1:], own.dtype),
             pltpu.VMEM(shape, own.dtype),
-            pltpu.SemaphoreType.DMA((parts,)),
+            pltpu.SemaphoreType.DMA((2,)),
             pltpu.SemaphoreType.DMA((parts,)),
         ],
-        compiler_params=pltpu.CompilerParams(vmem_limit_bytes=24 << 20),
+        compiler_params=pltpu.CompilerParams(vmem_limit_bytes=40 << 20),
         name="pack1",
-    )(tab, own, pltpu.with_memory_space_constraint(mate, pltpu.HBM))
+    )(tab, *(pltpu.with_memory_space_constraint(x, pltpu.HBM) for x in (own, mate)))
 
 
 def pack2_kernel(c2, tab_ref, own_ref, mate_ref, got_ref, out_ref, buf, in_sem, out_sem):
@@ -596,14 +574,22 @@
 
 
 def near_kernel(late, tab_ref, loc_ref, lens_ref, own_t_hbm, best0_ref, ret0_ref, *refs):
-    gots, (best_ref, ret_ref, own_t_ref, all_ref, buf, sem) = refs[:-6], refs[-6:]
+    gots, (best_ref, ret_ref, own_t_ref, all_ref, buf, sem, piece_sem) = refs[:-7], refs[-7:]
     copies = [pltpu.make_async_copy(own_t_hbm, own_t_ref, sem.at[0])]
-    start = 0
-    for i, got in enumerate(gots):
+    start = gots[0].shape[0]
+    for i, got in enumerate(gots[1:]):
         end = start + got.shape[0]
         copies.append(pltpu.make_async_copy(got, all_ref.at[pl.ds(start, end - start)], sem.at[i + 1]))
         start = end
-    for copy in copies:
+    senders = N // PIECES
+    rows = senders * C1
+    pieces = [
+        pltpu.make_async_copy(
+            gots[0].at[pl.ds(c * rows, rows)], all_ref.at[pl.ds(c * rows, rows)], piece_sem.at[c]
+        )
+        for c in range(PIECES)
+    ]
+    for copy in copies + pieces:
         copy.start()
     width = own_t_ref.shape[1]
     best_ref[...] = best0_ref[...]
@@ -624,8 +610,15 @@
     row = lax.broadcasted_iota(jnp.int32, (N, N), 0)
     col = lax.broadcasted_iota(jnp.int32, (N, N), 1)
 
-    def body(j, _):
+    def body(j, here):
         first = j * GROUP
+        need = sender(first + GROUP - 1) // senders + 1
+        for c in range(PIECES):
+
+            @pl.when((c >= here) & (c < need))
+            def _(c=c):
+                pieces[c].wait()
+
         for u in range(GROUP):
             gather(first + u, u)
         found = []
@@ -640,9 +633,15 @@
             best_ref[pl.ds(p, 1), :] = jnp.maximum(best_ref[pl.ds(p, 1), :], own_best)
             ret = jnp.where(col == s, in_best, ret)
         ret_ref[...] = ret
-        return 0
-
-    lax.fori_loop(0, (count + GROUP - 1) // GROUP, body, 0)
+        return jnp.maximum(here, need)
+
+    here = lax.fori_loop(0, (count + GROUP - 1) // GROUP, body, jnp.int32(0))
+    for c in range(PIECES):
+
+        @pl.when(c >= here)
+        def _(c=c):
+            pieces[c].wait()
+
     if late:
         ret_ref[...] = ret_ref[...].T
 
@@ -662,7 +661,8 @@
             pltpu.VMEM(own_t.shape, own_t.dtype),
             pltpu.VMEM((total,) + gots[0].shape[1:], own_t.dtype),
             pltpu.VMEM((GROUP, GR, 16, own_t.shape[1]), own_t.dtype),
-            pltpu.SemaphoreType.DMA((1 + len(gots),)),
+            pltpu.SemaphoreType.DMA((len(gots),)),
+            pltpu.SemaphoreType.DMA((PIECES,)),
         ],
         compiler_params=pltpu.CompilerParams(vmem_limit_bytes=44 << 20),
         name="near_late" if late else "near_early",

time: 285 us -> 279 us (0.979)
  Pallas kernels: 64.2 us -> 59.9 us
    pallas_call x2, Pallas kernels: 24.4 us -> 21.1 us  [near(): pl.pallas_call(functools.partial(near_kernel, late), out_shape=[jax.Shape...]
  transfers between devices with their start and end apart: 6 -> 6, of which waited for: 4 -> 4; matrix products, arithmetic and copies ran while one was open for 14% -> 14% of each run, Pallas kernels for 13% -> 12%
where the time goes in v4:
time: 279 us; the launch traced here: 278 us
  waiting for transfers between devices  140 us (50%)
  Pallas kernels  59.9 us (21%)
  starting transfers between devices  31.4 us (11%)
  matrix products  19.2 us (7%)
  local copies, waits for them, and re-layouts  11.2 us (4%)
  other arithmetic  11 us (4%)
  loops' own time  4.45 us (2%)
    all_to_all x4, waiting for transfers between devices, exchange(): return lax.all_to_all(x, 'shard', split_axis=0, concat_axis=0, tiled=True)  140 us
    all_to_all x4, starting transfers between devices, exchange(): return lax.all_to_all(x, 'shard', split_axis=0, concat_axis=0, tiled=True)  29.6 us
    pallas_call x2, Pallas kernels, near(): pl.pallas_call(functools.partial(near_kernel, late), out_shape=[jax.Shape...  21.1 us
    dot_general x2, matrix products, one_block(): jnp.einsum('bie,qje->bqij', block_rows, embeddings, preferred_element_typ...  19.2 us
    pallas_call x1, Pallas kernels, pack1(): pl.pallas_call(pack1_kernel, out_shape=pltpu.HBM(shape, own.dtype), in_sp...  8.8 us
    pallas_call x1, Pallas kernels, place(): pl.pallas_call(functools.partial(place_kernel, c2), out_shape=jax.ShapeDt...  8.54 us
    pallas_call x1, Pallas kernels, route(): pl.pallas_call(functools.partial(route_kernel, c2), out_shape=[jax.ShapeD...  8.53 us
    another operation x1, local copies, waits for them, and re-layouts  7.88 us
  transfers between devices with their start and end apart: 6, of which 4 were waited for; matrix products, arithmetic and copies ran while one was open for 14% of the time, Pallas kernels for 12%

profile of v4, /device:TPU:1, one launch (start us, length us, event | category | flops | bytes accessed | tf_op | source)
XLA Modules:
  0.0 278.2 jit_solution(1314846570444966202)
XLA Ops:
  0.6 1.5 collective-permute-start.2
  2.8 0.8 broadcast_in_dim.231
  3.6 10.2 %all-to-all-start.8 = ((s32[128,1,384]{2,1,0:T(1,128)}), s32[128,1,384]{2,1,0:T(1,128)S(1)}, u32[]{:S(2)}, u32[]{:S(2)}) async-start(s32[128,1,384]{2,1,0:T(1,128)} %broadcast_in_dim.231), calls=%async_computation.8 | async-start | bytes 393216 | tf_op jit(solution)/shard_map/all_to_all | solution.py:710
  14.6 9.8 %all-to-all-done.8 = s32[128,1,384]{2,1,0:T(1,128)S(1)} async-done(((s32[128,1,384]{2,1,0:T(1,128)}), s32[128,1,384]{2,1,0:T(1,128)S(1)}, u32[]{:S(2)}, u32[]{:S(2)}) %all-to-all-start.8) | async-done | bytes 196640 | tf_op jit(solution)/shard_map/all_to_all | solution.py:710
  24.4 8.5 %route1.1 = (s32[16,128]{1,0:T(8,128)S(1)}, s32[1]{0:T(128)}) custom-call(s32[1]{0:T(128)} %bitcast.43.me_ref, s32[128,384]{1,0:T(8,128)S(1)} %bitcast.164), custom_call_target="tpu_custom_call" | custom-call | tf_op jit(solution)/shard_map/route1/pallas_call | solution.py:204
  33.6 244.0 %conditional.2 = ((f32[16,128]{1,0:T(8,128)}, f32[16,128]{1,0:T(8,128)S(1)})) conditional(s32[]{:T(128)} %bitcast.45, (s32[1]{0:T(128)}, s32[128,384]{1,0:T(8,128)S(1)}, f32[16,128]{1,0:T(8,128)S(1)}, bf16[16,128,1280]{2,1,0:T(8,128)(2,1)}, bf16[128,16,1280]{2,1,0:T(8,128)(2,1)}, /*index=5*/s32[16]{0:T(128)}, ...), branch_computations={%region_0.23_spmd, %region_23.34_spmd} | conditional | flops 5390275584 | bytes 172617312 | solution.py:768
  33.8 8.8 %pack1.3 = bf16[256,16,1280]{2,1,0:T(8,128)(2,1)} custom-call(s32[16,128]{1,0:T(8,128)S(1)} %get-tuple-element.249.tab_ref, bf16[128,16,1280]{2,1,0:T(8,128)(2,1)} %bitcast.160, bf16[128,16,1280]{2,1,0:T(8,128)(2,1)} %get-tuple-element.251.mate_ref), custom_call_target="tpu_custom_call" | custom-call | tf_op jit(solution)/shard_map/cond/branch_1_fun/pack1/pallas_call | solution.py:251
  42.6 5.2 %all-to-all-start = ((bf16[256,16,1280]{2,1,0:T(8,128)(2,1)}), bf16[256,16,1280]{2,1,0:T(8,128)(2,1)}, u32[]{:S(2)}, u32[]{:S(2)}) async-start(bf16[256,16,1280]{2,1,0:T(8,128)(2,1)} %pack1.3), calls=%async_computation | async-start | bytes 20971520 | tf_op jit(solution)/shard_map/cond/branch_1_fun/all_to_all | solution.py:710
  47.9 7.9 %copy.30 = bf16[16,128,1280]{1,2,0:T(8,128)(2,1)} copy(bf16[16,128,1280]{2,1,0:T(8,128)(2,1)} %get-tuple-element.602) | data formatting | bytes 10485760 | tf_op jit(solution)/shard_map
  55.9 33.6 %while.32 = (s32[]{:T(128)}, f32[2,8,128]{2,1,0:T(8,128)S(1)}, s32[2]{0:T(128)S(1)}, f32[16,128]{1,0:T(8,128)S(1)}, bf16[16,128,1280]{2,1,0:T(8,128)(2,1)}, /*in...) while((s32[]{:T(128)}, f32[2,8,128]{2,1,0:T(8,128)S(1)}, s32[2]{0:T(128)S(1)}, ...), condition=%wide.region_32.32_spmd, body=%wide.region_25.31_spmd.sunk | while | flops 5389736960 | bytes 25377404 | solution.py:706
  58.5 10.0 %multiply_reduce_fusion.15 = (f32[8,16,128]{2,1,0:T(8,128)S(1)}, f32[8,128,16]{1,2,0:T(8,128)S(1)}, f32[8,128,16,128]{1,3,2,0:T(8,128)S(1)}) fusion(f32[8,128]{1,0:T(8,128)S(1)} %broadcast_multiply_fusion.12, f32[16,128]{1,0:T(8,128)S(1)} %broadcast_multiply_fusion.13, bf16[16,128,1280]{2,1,0:T(8,128)(2,1)} %get-tuple-element.620, s32[]{:T(128)S(6)} %select_n.110), kind=kOutput, calls=%fused_computation.67.clone.1 | convolution fusion | flops 5377064960 | bytes 16396292 | tf_op jit(solution)/shard_map/cond/branch_1_fun/while/body/eval_jaxpr/bie,qje->bqij/dot_general | solution.py:693
  68.7 3.4 %fusion.41 = f32[8,16,128]{2,1,0:T(8,128)S(1)} fusion(f32[8,128,16,128]{1,3,2,0:T(8,128)S(1)} %get-tuple-element.563, f32[8,16]{1,0:T(8,128)S(1)} %broadcast_divide_fusion.9, f32[8,16,128]{2,1,0:T(8,128)S(1)} %get-tuple-element.568, f32[8,16,128]{2,1,0:T(8,128)S(1)} %get-tuple-element.569, pred[16,128]{1,0:T(8,128)(4,1)S(1)} %broadcast_compare_fusion.6), kind=kLoop, calls=%fused_computation.66.clone.1 | loop fusion | flops 12566528 | bytes 8587776 | tf_op jit(solution)/shard_map/cond/branch_1_fun/while/body/eval_jaxpr/reduce_max | solution.py:697
  75.7 9.3 %multiply_reduce_fusion.15 = (f32[8,16,128]{2,1,0:T(8,128)S(1)}, f32[8,128,16]{1,2,0:T(8,128)S(1)}, f32[8,128,16,128]{1,3,2,0:T(8,128)S(1)}) fusion(f32[8,128]{1,0:T(8,128)S(1)} %broadcast_multiply_fusion.12, f32[16,128]{1,0:T(8,128)S(1)} %broadcast_multiply_fusion.13, bf16[16,128,1280]{2,1,0:T(8,128)(2,1)} %get-tuple-element.620, s32[]{:T(128)S(6)} %select_n.110), kind=kOutput, calls=%fused_computation.67.clone.1 | convolution fusion | flops 5377064960 | bytes 16396292 | tf_op jit(solution)/shard_map/cond/branch_1_fun/while/body/eval_jaxpr/bie,qje->bqij/dot_general | solution.py:693
  85.2 3.4 %fusion.41 = f32[8,16,128]{2,1,0:T(8,128)S(1)} fusion(f32[8,128,16,128]{1,3,2,0:T(8,128)S(1)} %get-tuple-element.563, f32[8,16]{1,0:T(8,128)S(1)} %broadcast_divide_fusion.9, f32[8,16,128]{2,1,0:T(8,128)S(1)} %get-tuple-element.568, f32[8,16,128]{2,1,0:T(8,128)S(1)} %get-tuple-element.569, pred[16,128]{1,0:T(8,128)(4,1)S(1)} %broadcast_compare_fusion.6), kind=kLoop, calls=%fused_computation.66.clone.1 | loop fusion | flops 12566528 | bytes 8587776 | tf_op jit(solution)/shard_map/cond/branch_1_fun/while/body/eval_jaxpr/reduce_max | solution.py:697
  89.4 82.8 %all-to-all-done.got_ref.refs_0_ = bf16[256,16,1280]{2,1,0:T(8,128)(2,1)} async-done(((bf16[256,16,1280]{2,1,0:T(8,128)(2,1)}), bf16[256,16,1280]{2,1,0:T(8,128)(2,1)}, u32[]{:S(2)}, u32[]{:S(2)}) %all-to-all-start) | async-done | bytes 10485792 | tf_op jit(solution)/shard_map/cond/branch_1_fun/all_to_all | solution.py:710
  172.3 5.3 %pack2.3 = bf16[128,16,1280]{2,1,0:T(8,128)(2,1)} custom-call(s32[16,128]{1,0:T(8,128)S(1)} %get-tuple-element.249.tab_ref, bf16[128,16,1280]{2,1,0:T(8,128)(2,1)} %bitcast.161, bf16[128,16,1280]{2,1,0:T(8,128)(2,1)} %get-tuple-element.251.mate_ref, bf16[256,16,1280]{2,1,0:T(8,128)(2,1)} %all-to-all-done.got_ref.refs_0_), custom_call_target="tpu_custom_call" | custom-call | tf_op jit(solution)/shard_map/cond/branch_1_fun/pack2/pallas_call | solution.py:320
  177.6 9.1 %all-to-all-start.1 = ((bf16[128,16,1280]{2,1,0:T(8,128)(2,1)}), bf16[128,16,1280]{2,1,0:T(8,128)(2,1)}, u32[]{:S(2)}, u32[]{:S(2)}) async-start(bf16[128,16,1280]{2,1,0:T(8,128)(2,1)} %pack2.3), calls=%async_computation.1 | async-start | bytes 10485760 | tf_op jit(solution)/shard_map/cond/branch_1_fun/all_to_all | solution.py:710
  186.7 7.6 %hand.3 = bf16[64,16,1280]{2,1,0:T(8,128)(2,1)S(1)} custom-call(s32[16,128]{1,0:T(8,128)S(1)} %get-tuple-element.249.tab_ref, bf16[256,16,1280]{2,1,0:T(8,128)(2,1)} %all-to-all-done.got_ref.refs_0_), custom_call_target="tpu_custom_call" | custom-call | tf_op jit(solution)/shard_map/cond/branch_1_fun/hand/pallas_call | solution.py:359
  194.6 8.5 %place.5.loc_ref = s32[1408]{0:T(1024)} custom-call(s32[1]{0:T(128)} %get-tuple-element.258.me_ref, s32[16,128]{1,0:T(8,128)S(1)} %get-tuple-element.249.tab_ref), custom_call_target="tpu_custom_call" | custom-call | tf_op jit(solution)/shard_map/cond/branch_1_fun/place/pallas_call | solution.py:457
  203.9 9.4 %near_early.3 = (f32[16,128]{1,0:T(8,128)S(1)}, f32[128,128]{1,0:T(8,128)S(1)}) custom-call(s32[16,128]{1,0:T(8,128)S(1)} %get-tuple-element.249.tab_ref, s32[1408]{0:T(1024)S(1)} %copy-done, s32[16]{0:T(128)S(1)} %copy-done.8, bf16[16,1280,128]{2,1,0:T(8,128)(2,1)} %bitcast.162, f32[16,128]{1,0:T(8,128)S(1)} %broadcast_in_dim.221.best0_ref, ...), custom_call_target="tpu_custom_call" | custom-call | tf_op jit(solution)/shard_map/cond/branch_1_fun/near_early/pallas_call | solution.py:652
  213.4 37.5 %all-to-all-done.1.refs_1_ = bf16[128,16,1280]{2,1,0:T(8,128)(2,1)} async-done(((bf16[128,16,1280]{2,1,0:T(8,128)(2,1)}), bf16[128,16,1280]{2,1,0:T(8,128)(2,1)}, u32[]{:S(2)}, u32[]{:S(2)}) %all-to-all-start.1) | async-done | bytes 5242912 | tf_op jit(solution)/shard_map/cond/branch_1_fun/all_to_all | solution.py:710
  250.8 11.7 %near_late.3 = (f32[16,128]{1,0:T(8,128)S(1)}, f32[128,128]{1,0:T(8,128)}) custom-call(s32[16,128]{1,0:T(8,128)S(1)} %get-tuple-element.249.tab_ref, s32[1408]{0:T(1024)S(1)} %copy-done.1, s32[16]{0:T(128)S(1)} %copy-done.8, bf16[16,1280,128]{2,1,0:T(8,128)(2,1)} %bitcast.163, f32[16,128]{1,0:T(8,128)S(1)} %get-tuple-element.266.best0_ref, ...), custom_call_target="tpu_custom_call" | custom-call | tf_op jit(solution)/shard_map/cond/branch_1_fun/near_late/pallas_call | solution.py:652
  262.5 5.1 %all-to-all-start.2 = ((f32[128,1,128]{2,1,0:T(1,128)}), f32[128,1,128]{2,1,0:T(1,128)S(1)}, u32[]{:S(2)}, u32[]{:S(2)}) async-start(f32[128,1,128]{2,1,0:T(1,128)} %bitcast.41), calls=%async_computation.2 | async-start | bytes 131072 | tf_op jit(solution)/shard_map/cond/branch_1_fun/all_to_all | solution.py:710
  267.6 9.6 %all-to-all-done.2 = f32[128,1,128]{2,1,0:T(1,128)S(1)} async-done(((f32[128,1,128]{2,1,0:T(1,128)}), f32[128,1,128]{2,1,0:T(1,128)S(1)}, u32[]{:S(2)}, u32[]{:S(2)}) %all-to-all-start.2) | async-done | bytes 65568 | tf_op jit(solution)/shard_map/cond/branch_1_fun/all_to_all | solution.py:710
  (49 shorter events, 7.1 us)
Async XLA Ops:
  0.6 32.9 %collective-permute-start.2 = (bf16[128,16,1280]{2,1,0:T(8,128)(2,1)}, bf16[128,16,1280]{2,1,0:T(8,128)(2,1)}, u32[]{:S(2)}, u32[]{:S(2)}) collective-permute-start(bf16[128,16,1280]{2,1,0:T(8,128)(2,1)} %bitcast.156), channel_id=1, source_target_pairs={{0,1},{1,0},{2,3},{3,2},{4,5},{5,4},{6,7},{7,6},{8,9},{9,8},{10,11... | collective-permute-start | bytes 15728648 | tf_op jit(solution)/shard_map/ppermute | solution.py:714
  3.6 20.7 %all-to-all-start.8 = ((s32[128,1,384]{2,1,0:T(1,128)}), s32[128,1,384]{2,1,0:T(1,128)S(1)}, u32[]{:S(2)}, u32[]{:S(2)}) async-start(s32[128,1,384]{2,1,0:T(1,128)} %broadcast_in_dim.231), calls=%async_computation.8 | async-start | bytes 393216 | tf_op jit(solution)/shard_map/all_to_all | solution.py:710
  42.6 129.6 %all-to-all-start = ((bf16[256,16,1280]{2,1,0:T(8,128)(2,1)}), bf16[256,16,1280]{2,1,0:T(8,128)(2,1)}, u32[]{:S(2)}, u32[]{:S(2)}) async-start(bf16[256,16,1280]{2,1,0:T(8,128)(2,1)} %pack1.3), calls=%async_computation | async-start | bytes 20971520 | tf_op jit(solution)/shard_map/cond/branch_1_fun/all_to_all | solution.py:710
  89.4 123.9 %copy-start.13 = (f32[2,8,128]{2,1,0:T(8,128)}, f32[2,8,128]{2,1,0:T(8,128)S(1)}, u32[]{:S(2)}) copy-start(f32[2,8,128]{2,1,0:T(8,128)S(1)} %get-tuple-element.254) | copy-start | bytes 24580 | tf_op jit(solution)/shard_map/cond
  177.6 73.2 %all-to-all-start.1 = ((bf16[128,16,1280]{2,1,0:T(8,128)(2,1)}), bf16[128,16,1280]{2,1,0:T(8,128)(2,1)}, u32[]{:S(2)}, u32[]{:S(2)}) async-start(bf16[128,16,1280]{2,1,0:T(8,128)(2,1)} %pack2.3), calls=%async_computation.1 | async-start | bytes 10485760 | tf_op jit(solution)/shard_map/cond/branch_1_fun/all_to_all | solution.py:710
  186.7 16.5 %copy-start.8 = (s32[16]{0:T(128)S(1)}, s32[16]{0:T(128)}, u32[]{:S(2)}) copy-start(s32[16]{0:T(128)} %get-tuple-element.259.lens_ref) | copy-start | bytes 196 | tf_op jit(solution)/shard_map/cond
  194.3 56.5 %collective-permute-start = (bf16[64,16,1280]{2,1,0:T(8,128)(2,1)S(1)}, bf16[64,16,1280]{2,1,0:T(8,128)(2,1)}, u32[]{:S(2)}, u32[]{:S(2)}) collective-permute-start(bf16[64,16,1280]{2,1,0:T(8,128)(2,1)S(1)} %hand.3), channel_id=1, source_target_pairs={{0,1},{1,0},{2,3},{3,2},{4,5},{5,4},{6,7},{7,6},{8,9},{9,8},{10,11... | collective-permute-start | bytes 7864328 | tf_op jit(solution)/shard_map/cond/branch_1_fun/ppermute | solution.py:714
  203.1 47.7 %copy-start.1 = (s32[1408]{0:T(1024)S(1)}, s32[1408]{0:T(1024)}, u32[]{:S(2)}) copy-start(s32[1408]{0:T(1024)} %place.5.loc_ref) | copy-start | bytes 16900 | tf_op jit(solution)/shard_map/cond
  203.2 0.7 copy-start
  262.5 14.7 %all-to-all-start.2 = ((f32[128,1,128]{2,1,0:T(1,128)}), f32[128,1,128]{2,1,0:T(1,128)S(1)}, u32[]{:S(2)}, u32[]{:S(2)}) async-start(f32[128,1,128]{2,1,0:T(1,128)} %bitcast.41), calls=%async_computation.2 | async-start | bytes 131072 | tf_op jit(solution)/shard_map/cond/branch_1_fun/all_to_all | solution.py:710
  277.6 0.6 copy-start.9

commit v5 on v4

--- a/solution.py
+++ b/solution.py
@@ -16,6 +16,7 @@
 GROUP = 4
 PIECES = 4
 TRIES = 6
+FEW = 32
 
 R_F1ROW, R_F1COL, R_F1COLM, R_F2ROW, R_F2COL, R_SEND, R_SENDM, R_GIN, R_LIN, R_OWN, R_GOUT = range(11)
 
@@ -58,12 +59,14 @@
         lb = jnp.where(req == p, lens_t[p : p + 1, :], lb)
     la = la * live
     lb = lb * live
+    la_t = la.T
     lb_t = lb.T
+    req_t = req.T
     ga = (la + 15) >> 4
     gb = (lb + 15) >> 4
-    ga_t = ga.T
-    gb_t = gb.T
-    anti = live - live.T
+    ga_t = (la_t + 15) >> 4
+    gb_t = (lb_t + 15) >> 4
+    anti = live - (lb_t > 0).astype(jnp.int32)
     base = 1000 * (gb + gb_t - ga - ga_t) + jnp.where(((s + r) & 1) == 0, 250, -250)
     score = base
     bias_col = jnp.zeros((N, 1), jnp.int32)
@@ -76,8 +79,9 @@
         score = base + anti * (bias_col - bias_row)
     lister_gets = score < 0
     lin = jnp.where(lister_gets, lb_t, la)
-    psend = jnp.where(lister_gets, req.T, q)
-    pown = jnp.where(lister_gets, q.T, req)
+    lin_t = jnp.where(lister_gets, lb, la_t)
+    psend = jnp.where(lister_gets, req_t, q)
+    pown_t = jnp.where(lister_gets, q, req_t)
     m_tot = (lin + 15) >> 4
 
     diag = s == r
@@ -167,11 +171,12 @@
         tries, _, _, _, _, urgent = c
         limit = jnp.where(urgent > 0, last, -1)
         _, turns, w1, w2, g = sweep(limit, 0, first_ref[0], first_ref[1], first_ref[2])
-        most, turns, w1, w2, g = sweep(last, turns, w1, w2, g)
-        return tries + 1, most + 1, turns, w1, w2, jnp.where(g <= last, 1, urgent)
+        _, turns, w1, w2, g = sweep(last, turns, w1, w2, g)
+        late = (g <= last).astype(jnp.int32)
+        return tries + 1, jnp.sum(late), turns, w1, w2, jnp.maximum(late, urgent)
 
     _, left, turns, w1, w2, _ = lax.while_loop(
-        lambda c: (c[0] < TRIES) & (c[1] > 0),
+        lambda c: (c[0] < TRIES) & (c[1] > 0) & (c[1] <= FEW),
         attempt,
         (jnp.int32(0), jnp.int32(1), jnp.int32(0), w1, w2, jnp.zeros((N, N), jnp.int32)),
     )
@@ -192,9 +197,9 @@
     put(w2, (R_F2ROW, me))
     put(w2.T, (R_F2COL, me))
     put(psend, (R_SEND, me), (R_SENDM, mate))
-    put(m_tot.T, (R_GIN, me))
-    put(lin.T, (R_LIN, me))
-    put(pown.T, (R_OWN, me))
+    put((lin_t + 15) >> 4, (R_GIN, me))
+    put(lin_t, (R_LIN, me))
+    put(pown_t, (R_OWN, me))
     left_ref[0] = left
     put(m_tot, (R_GOUT, me))
     tab_ref[R_GOUT + 1 :, :] = jnp.zeros((16 - R_GOUT - 1, N), jnp.int32)

time: 279 us -> 285 us (1.022); the launches traced: 278 us -> 281 us
  no operation moved by 1% of the time
where the time goes in v5:
time: 285 us; the launch traced here: 281 us
  waiting for transfers between devices  140 us (49%)
  Pallas kernels  60.3 us (21%)
  starting transfers between devices  33.4 us (12%)
  matrix products  19.2 us (7%)
  local copies, waits for them, and re-layouts  11.2 us (4%)
  other arithmetic  11 us (4%)
  loops' own time  4.45 us (2%)
    all_to_all x4, waiting for transfers between devices, exchange(): return lax.all_to_all(x, 'shard', split_axis=0, concat_axis=0, tiled=True)  140 us
    all_to_all x4, starting transfers between devices, exchange(): return lax.all_to_all(x, 'shard', split_axis=0, concat_axis=0, tiled=True)  31 us
    pallas_call x2, Pallas kernels, near(): pl.pallas_call(functools.partial(near_kernel, late), out_shape=[jax.Shape...  20.5 us
    dot_general x2, matrix products, one_block(): jnp.einsum('bie,qje->bqij', block_rows, embeddings, preferred_element_typ...  19.2 us
    pallas_call x1, Pallas kernels, route(): pl.pallas_call(functools.partial(route_kernel, c2), out_shape=[jax.ShapeD...  10.1 us
    pallas_call x1, Pallas kernels, pack1(): pl.pallas_call(pack1_kernel, out_shape=pltpu.HBM(shape, own.dtype), in_sp...  8.8 us
    pallas_call x1, Pallas kernels, place(): pl.pallas_call(functools.partial(place_kernel, c2), out_shape=jax.ShapeDt...  8.54 us
    another operation x1, local copies, waits for them, and re-layouts  7.88 us
  transfers between devices with their start and end apart: 6, of which 4 were waited for; matrix products, arithmetic and copies ran while one was open for 14% of the time, Pallas kernels for 12%

profile of v5, /device:TPU:1, one launch (start us, length us, event | category | flops | bytes accessed | tf_op | source)
XLA Modules:
  0.0 281.1 jit_solution(4329185654358770474)
XLA Ops:
  0.6 1.5 collective-permute-start.2
  3.6 10.2 %all-to-all-start.8 = ((s32[128,1,384]{2,1,0:T(1,128)}), s32[128,1,384]{2,1,0:T(1,128)S(1)}, u32[]{:S(2)}, u32[]{:S(2)}) async-start(s32[128,1,384]{2,1,0:T(1,128)} %broadcast_in_dim.231), calls=%async_computation.8 | async-start | bytes 393216 | tf_op jit(solution)/shard_map/all_to_all | solution.py:715
  14.6 9.8 %all-to-all-done.8 = s32[128,1,384]{2,1,0:T(1,128)S(1)} async-done(((s32[128,1,384]{2,1,0:T(1,128)}), s32[128,1,384]{2,1,0:T(1,128)S(1)}, u32[]{:S(2)}, u32[]{:S(2)}) %all-to-all-start.8) | async-done | bytes 196640 | tf_op jit(solution)/shard_map/all_to_all | solution.py:715
  24.4 10.1 %route1.1 = (s32[16,128]{1,0:T(8,128)S(1)}, s32[1]{0:T(128)}) custom-call(s32[1]{0:T(128)} %bitcast.43.me_ref, s32[128,384]{1,0:T(8,128)S(1)} %bitcast.164), custom_call_target="tpu_custom_call" | custom-call | tf_op jit(solution)/shard_map/route1/pallas_call | solution.py:209
  35.1 245.4 %conditional.2 = ((f32[16,128]{1,0:T(8,128)}, f32[16,128]{1,0:T(8,128)S(1)})) conditional(s32[]{:T(128)} %bitcast.45, (s32[1]{0:T(128)}, s32[128,384]{1,0:T(8,128)S(1)}, f32[16,128]{1,0:T(8,128)S(1)}, bf16[16,128,1280]{2,1,0:T(8,128)(2,1)}, bf16[128,16,1280]{2,1,0:T(8,128)(2,1)}, /*index=5*/s32[16]{0:T(128)}, ...), branch_computations={%region_0.23_spmd, %region_23.34_spmd} | conditional | flops 5390275584 | bytes 172617312 | solution.py:773
  35.4 8.8 %pack1.3 = bf16[256,16,1280]{2,1,0:T(8,128)(2,1)} custom-call(s32[16,128]{1,0:T(8,128)S(1)} %get-tuple-element.249.tab_ref, bf16[128,16,1280]{2,1,0:T(8,128)(2,1)} %bitcast.160, bf16[128,16,1280]{2,1,0:T(8,128)(2,1)} %get-tuple-element.251.mate_ref), custom_call_target="tpu_custom_call" | custom-call | tf_op jit(solution)/shard_map/cond/branch_1_fun/pack1/pallas_call | solution.py:256
  44.2 5.2 %all-to-all-start = ((bf16[256,16,1280]{2,1,0:T(8,128)(2,1)}), bf16[256,16,1280]{2,1,0:T(8,128)(2,1)}, u32[]{:S(2)}, u32[]{:S(2)}) async-start(bf16[256,16,1280]{2,1,0:T(8,128)(2,1)} %pack1.3), calls=%async_computation | async-start | bytes 20971520 | tf_op jit(solution)/shard_map/cond/branch_1_fun/all_to_all | solution.py:715
  49.4 7.9 %copy.30 = bf16[16,128,1280]{1,2,0:T(8,128)(2,1)} copy(bf16[16,128,1280]{2,1,0:T(8,128)(2,1)} %get-tuple-element.602) | data formatting | bytes 10485760 | tf_op jit(solution)/shard_map
  57.4 33.6 %while.32 = (s32[]{:T(128)}, f32[2,8,128]{2,1,0:T(8,128)S(1)}, s32[2]{0:T(128)S(1)}, f32[16,128]{1,0:T(8,128)S(1)}, bf16[16,128,1280]{2,1,0:T(8,128)(2,1)}, /*in...) while((s32[]{:T(128)}, f32[2,8,128]{2,1,0:T(8,128)S(1)}, s32[2]{0:T(128)S(1)}, ...), condition=%wide.region_32.32_spmd, body=%wide.region_25.31_spmd.sunk | while | flops 5389736960 | bytes 25377404 | solution.py:711
  60.1 10.0 %multiply_reduce_fusion.15 = (f32[8,16,128]{2,1,0:T(8,128)S(1)}, f32[8,128,16]{1,2,0:T(8,128)S(1)}, f32[8,128,16,128]{1,3,2,0:T(8,128)S(1)}) fusion(f32[8,128]{1,0:T(8,128)S(1)} %broadcast_multiply_fusion.12, f32[16,128]{1,0:T(8,128)S(1)} %broadcast_multiply_fusion.13, bf16[16,128,1280]{2,1,0:T(8,128)(2,1)} %get-tuple-element.620, s32[]{:T(128)S(6)} %select_n.110), kind=kOutput, calls=%fused_computation.67.clone.1 | convolution fusion | flops 5377064960 | bytes 16396292 | tf_op jit(solution)/shard_map/cond/branch_1_fun/while/body/eval_jaxpr/bie,qje->bqij/dot_general | solution.py:698
  70.3 3.4 %fusion.41 = f32[8,16,128]{2,1,0:T(8,128)S(1)} fusion(f32[8,128,16,128]{1,3,2,0:T(8,128)S(1)} %get-tuple-element.563, f32[8,16]{1,0:T(8,128)S(1)} %broadcast_divide_fusion.9, f32[8,16,128]{2,1,0:T(8,128)S(1)} %get-tuple-element.568, f32[8,16,128]{2,1,0:T(8,128)S(1)} %get-tuple-element.569, pred[16,128]{1,0:T(8,128)(4,1)S(1)} %broadcast_compare_fusion.6), kind=kLoop, calls=%fused_computation.66.clone.1 | loop fusion | flops 12566528 | bytes 8587776 | tf_op jit(solution)/shard_map/cond/branch_1_fun/while/body/eval_jaxpr/reduce_max | solution.py:702
  77.2 9.3 %multiply_reduce_fusion.15 = (f32[8,16,128]{2,1,0:T(8,128)S(1)}, f32[8,128,16]{1,2,0:T(8,128)S(1)}, f32[8,128,16,128]{1,3,2,0:T(8,128)S(1)}) fusion(f32[8,128]{1,0:T(8,128)S(1)} %broadcast_multiply_fusion.12, f32[16,128]{1,0:T(8,128)S(1)} %broadcast_multiply_fusion.13, bf16[16,128,1280]{2,1,0:T(8,128)(2,1)} %get-tuple-element.620, s32[]{:T(128)S(6)} %select_n.110), kind=kOutput, calls=%fused_computation.67.clone.1 | convolution fusion | flops 5377064960 | bytes 16396292 | tf_op jit(solution)/shard_map/cond/branch_1_fun/while/body/eval_jaxpr/bie,qje->bqij/dot_general | solution.py:698
  86.8 3.4 %fusion.41 = f32[8,16,128]{2,1,0:T(8,128)S(1)} fusion(f32[8,128,16,128]{1,3,2,0:T(8,128)S(1)} %get-tuple-element.563, f32[8,16]{1,0:T(8,128)S(1)} %broadcast_divide_fusion.9, f32[8,16,128]{2,1,0:T(8,128)S(1)} %get-tuple-element.568, f32[8,16,128]{2,1,0:T(8,128)S(1)} %get-tuple-element.569, pred[16,128]{1,0:T(8,128)(4,1)S(1)} %broadcast_compare_fusion.6), kind=kLoop, calls=%fused_computation.66.clone.1 | loop fusion | flops 12566528 | bytes 8587776 | tf_op jit(solution)/shard_map/cond/branch_1_fun/while/body/eval_jaxpr/reduce_max | solution.py:702
  91.0 82.8 %all-to-all-done.got_ref.refs_0_ = bf16[256,16,1280]{2,1,0:T(8,128)(2,1)} async-done(((bf16[256,16,1280]{2,1,0:T(8,128)(2,1)}), bf16[256,16,1280]{2,1,0:T(8,128)(2,1)}, u32[]{:S(2)}, u32[]{:S(2)}) %all-to-all-start) | async-done | bytes 10485792 | tf_op jit(solution)/shard_map/cond/branch_1_fun/all_to_all | solution.py:715
  173.8 5.3 %pack2.3 = bf16[128,16,1280]{2,1,0:T(8,128)(2,1)} custom-call(s32[16,128]{1,0:T(8,128)S(1)} %get-tuple-element.249.tab_ref, bf16[128,16,1280]{2,1,0:T(8,128)(2,1)} %bitcast.161, bf16[128,16,1280]{2,1,0:T(8,128)(2,1)} %get-tuple-element.251.mate_ref, bf16[256,16,1280]{2,1,0:T(8,128)(2,1)} %all-to-all-done.got_ref.refs_0_), custom_call_target="tpu_custom_call" | custom-call | tf_op jit(solution)/shard_map/cond/branch_1_fun/pack2/pallas_call | solution.py:325
  179.1 9.1 %all-to-all-start.1 = ((bf16[128,16,1280]{2,1,0:T(8,128)(2,1)}), bf16[128,16,1280]{2,1,0:T(8,128)(2,1)}, u32[]{:S(2)}, u32[]{:S(2)}) async-start(bf16[128,16,1280]{2,1,0:T(8,128)(2,1)} %pack2.3), calls=%async_computation.1 | async-start | bytes 10485760 | tf_op jit(solution)/shard_map/cond/branch_1_fun/all_to_all | solution.py:715
  188.3 7.1 %hand.3 = bf16[64,16,1280]{2,1,0:T(8,128)(2,1)S(1)} custom-call(s32[16,128]{1,0:T(8,128)S(1)} %get-tuple-element.249.tab_ref, bf16[256,16,1280]{2,1,0:T(8,128)(2,1)} %all-to-all-done.got_ref.refs_0_), custom_call_target="tpu_custom_call" | custom-call | tf_op jit(solution)/shard_map/cond/branch_1_fun/hand/pallas_call | solution.py:364
  195.3 0.9 collective-permute-start
  196.3 8.5 %place.5.loc_ref = s32[1408]{0:T(1024)} custom-call(s32[1]{0:T(128)} %get-tuple-element.258.me_ref, s32[16,128]{1,0:T(8,128)S(1)} %get-tuple-element.249.tab_ref), custom_call_target="tpu_custom_call" | custom-call | tf_op jit(solution)/shard_map/cond/branch_1_fun/place/pallas_call | solution.py:462
  205.6 8.8 %near_early.3 = (f32[16,128]{1,0:T(8,128)S(1)}, f32[128,128]{1,0:T(8,128)S(1)}) custom-call(s32[16,128]{1,0:T(8,128)S(1)} %get-tuple-element.249.tab_ref, s32[1408]{0:T(1024)S(1)} %copy-done, s32[16]{0:T(128)S(1)} %copy-done.8, bf16[16,1280,128]{2,1,0:T(8,128)(2,1)} %bitcast.162, f32[16,128]{1,0:T(8,128)S(1)} %broadcast_in_dim.221.best0_ref, ...), custom_call_target="tpu_custom_call" | custom-call | tf_op jit(solution)/shard_map/cond/branch_1_fun/near_early/pallas_call | solution.py:657
  214.4 37.9 %all-to-all-done.1.refs_1_ = bf16[128,16,1280]{2,1,0:T(8,128)(2,1)} async-done(((bf16[128,16,1280]{2,1,0:T(8,128)(2,1)}), bf16[128,16,1280]{2,1,0:T(8,128)(2,1)}, u32[]{:S(2)}, u32[]{:S(2)}) %all-to-all-start.1) | async-done | bytes 5242912 | tf_op jit(solution)/shard_map/cond/branch_1_fun/all_to_all | solution.py:715
  252.4 11.7 %near_late.3 = (f32[16,128]{1,0:T(8,128)S(1)}, f32[128,128]{1,0:T(8,128)}) custom-call(s32[16,128]{1,0:T(8,128)S(1)} %get-tuple-element.249.tab_ref, s32[1408]{0:T(1024)S(1)} %copy-done.1, s32[16]{0:T(128)S(1)} %copy-done.8, bf16[16,1280,128]{2,1,0:T(8,128)(2,1)} %bitcast.163, f32[16,128]{1,0:T(8,128)S(1)} %get-tuple-element.266.best0_ref, ...), custom_call_target="tpu_custom_call" | custom-call | tf_op jit(solution)/shard_map/cond/branch_1_fun/near_late/pallas_call | solution.py:657
  264.1 6.4 %all-to-all-start.2 = ((f32[128,1,128]{2,1,0:T(1,128)}), f32[128,1,128]{2,1,0:T(1,128)S(1)}, u32[]{:S(2)}, u32[]{:S(2)}) async-start(f32[128,1,128]{2,1,0:T(1,128)} %bitcast.41), calls=%async_computation.2 | async-start | bytes 131072 | tf_op jit(solution)/shard_map/cond/branch_1_fun/all_to_all | solution.py:715
  270.5 9.6 %all-to-all-done.2 = f32[128,1,128]{2,1,0:T(1,128)S(1)} async-done(((f32[128,1,128]{2,1,0:T(1,128)}), f32[128,1,128]{2,1,0:T(1,128)S(1)}, u32[]{:S(2)}, u32[]{:S(2)}) %all-to-all-start.2) | async-done | bytes 65568 | tf_op jit(solution)/shard_map/cond/branch_1_fun/all_to_all | solution.py:715
  (49 shorter events, 7.6 us)
Async XLA Ops:
  0.6 34.5 %collective-permute-start.2 = (bf16[128,16,1280]{2,1,0:T(8,128)(2,1)}, bf16[128,16,1280]{2,1,0:T(8,128)(2,1)}, u32[]{:S(2)}, u32[]{:S(2)}) collective-permute-start(bf16[128,16,1280]{2,1,0:T(8,128)(2,1)} %bitcast.156), channel_id=1, source_target_pairs={{0,1},{1,0},{2,3},{3,2},{4,5},{5,4},{6,7},{7,6},{8,9},{9,8},{10,11... | collective-permute-start | bytes 15728648 | tf_op jit(solution)/shard_map/ppermute | solution.py:719
  3.6 20.7 %all-to-all-start.8 = ((s32[128,1,384]{2,1,0:T(1,128)}), s32[128,1,384]{2,1,0:T(1,128)S(1)}, u32[]{:S(2)}, u32[]{:S(2)}) async-start(s32[128,1,384]{2,1,0:T(1,128)} %broadcast_in_dim.231), calls=%async_computation.8 | async-start | bytes 393216 | tf_op jit(solution)/shard_map/all_to_all | solution.py:715
  44.2 129.6 %all-to-all-start = ((bf16[256,16,1280]{2,1,0:T(8,128)(2,1)}), bf16[256,16,1280]{2,1,0:T(8,128)(2,1)}, u32[]{:S(2)}, u32[]{:S(2)}) async-start(bf16[256,16,1280]{2,1,0:T(8,128)(2,1)} %pack1.3), calls=%async_computation | async-start | bytes 20971520 | tf_op jit(solution)/shard_map/cond/branch_1_fun/all_to_all | solution.py:715
  91.0 123.4 %copy-start.13 = (f32[2,8,128]{2,1,0:T(8,128)}, f32[2,8,128]{2,1,0:T(8,128)S(1)}, u32[]{:S(2)}) copy-start(f32[2,8,128]{2,1,0:T(8,128)S(1)} %get-tuple-element.254) | copy-start | bytes 24580 | tf_op jit(solution)/shard_map/cond
  179.1 73.2 %all-to-all-start.1 = ((bf16[128,16,1280]{2,1,0:T(8,128)(2,1)}), bf16[128,16,1280]{2,1,0:T(8,128)(2,1)}, u32[]{:S(2)}, u32[]{:S(2)}) async-start(bf16[128,16,1280]{2,1,0:T(8,128)(2,1)} %pack2.3), calls=%async_computation.1 | async-start | bytes 10485760 | tf_op jit(solution)/shard_map/cond/branch_1_fun/all_to_all | solution.py:715
  188.2 16.6 %copy-start.8 = (s32[16]{0:T(128)S(1)}, s32[16]{0:T(128)}, u32[]{:S(2)}) copy-start(s32[16]{0:T(128)} %get-tuple-element.259.lens_ref) | copy-start | bytes 196 | tf_op jit(solution)/shard_map/cond
  195.3 57.0 %collective-permute-start = (bf16[64,16,1280]{2,1,0:T(8,128)(2,1)S(1)}, bf16[64,16,1280]{2,1,0:T(8,128)(2,1)}, u32[]{:S(2)}, u32[]{:S(2)}) collective-permute-start(bf16[64,16,1280]{2,1,0:T(8,128)(2,1)S(1)} %hand.3), channel_id=1, source_target_pairs={{0,1},{1,0},{2,3},{3,2},{4,5},{5,4},{6,7},{7,6},{8,9},{9,8},{10,11... | collective-permute-start | bytes 7864328 | tf_op jit(solution)/shard_map/cond/branch_1_fun/ppermute | solution.py:719
  204.8 47.5 %copy-start.1 = (s32[1408]{0:T(1024)S(1)}, s32[1408]{0:T(1024)}, u32[]{:S(2)}) copy-start(s32[1408]{0:T(1024)} %place.5.loc_ref) | copy-start | bytes 16900 | tf_op jit(solution)/shard_map/cond
  204.9 0.7 copy-start
  264.1 16.0 %all-to-all-start.2 = ((f32[128,1,128]{2,1,0:T(1,128)}), f32[128,1,128]{2,1,0:T(1,128)S(1)}, u32[]{:S(2)}, u32[]{:S(2)}) async-start(f32[128,1,128]{2,1,0:T(1,128)} %bitcast.41), calls=%async_computation.2 | async-start | bytes 131072 | tf_op jit(solution)/shard_map/cond/branch_1_fun/all_to_all | solution.py:715
  280.5 0.6 copy-start.9
